TPU v7x, 128 devices: a whole 4x4x4 slice. The times are simulated.
128 devices in a mesh: gy: 4 (over z), gz: 32 (over x, y, core).
Axes of the slice: x: 4, y: 4, z: 4, core: 2. Of those that a mesh axis runs over, the one named last changes fastest.
Arguments:
- fields: float32 [2, 2, 1024, 2048], P(None, None, 'gz', 'gy'), may hold values from -8 to 8
- cond_x: float32 [2, 2], replicated, may hold values from 0.05 to 0.4
- cond_y: float32 [2, 2, 1024, 2048], P(None, None, 'gz', 'gy'), may hold values from 4096 to 32768
- cond_z: float32 [2, 2, 1024, 2048], P(None, None, 'gz', 'gy'), may hold values from 256 to 2048
- coupling: float32 [2], replicated, may hold values from 0.2 to 1.5
Outputs:
- stepped: float32 [2, 2, 1024, 2048], P(None, None, 'gz', 'gy')
All inputs are finite; a program needn't handle non-finite values.
Results may differ from a plain program's by a relative error of at most 0.0018.
Values sent between devices are 32-bit elements; how exact they have to be, the bound alone decides.
No kernel may reach another device: no remote copies, remote signals or barrier semaphores. Data moves between devices by JAX's collectives and lax.ppermute only.
A program may use at most 128 MiB of HBM per device.

v0:
```python
import jax
import jax.numpy as jnp
from jax import lax
from jax.experimental import pallas as pl
from jax.experimental.pallas import tpu as pltpu
from jax.sharding import PartitionSpec as P

SUB = 8
F32 = jnp.float32
VMEM = pl.BlockSpec(memory_space=pltpu.VMEM)
SMEM = pl.BlockSpec(memory_space=pltpu.SMEM)


def strided(ref, start, count, stride):
    return ref[pl.ds(start, count, stride=stride), :]


def factor_kernel(
    cx, cp, u, ky, kz, gpy, gsy, ymat, gpz, gsz, zmat, r0, kt, zr, wa, wb, wc, wd, zz
):
    lines, length = ky.shape
    steps = length // SUB
    planes, depth = zmat.shape[1], lines // zmat.shape[1]
    kt[...] = ky[...].T
    first = strided(kt, 0, SUB, steps)
    here = first
    for t in range(steps):
        after = strided(kt, t + 1, SUB, steps) if t + 1 < steps else pltpu.roll(first, SUB - 1, 0)
        zr[t] = 4.0 / (here + after)
        here = after
    last = strided(kt, steps - 1, SUB, steps)
    row = lax.broadcasted_iota(jnp.int32, (SUB, lines), 0)
    one, zero = jnp.ones((SUB, lines), F32), jnp.zeros((SUB, lines), F32)
    aw, aj, bw, bj = one, zero, zero, one
    for t in range(steps):
        wa[t], wb[t] = aw, bw
        aj, bj = aj + aw, bj + bw
        aw, bw = aw + zr[t] * aj, bw + zr[t] * bj
    cw, cj, dw, dj = one, zero, zero, one
    for t in reversed(range(steps)):
        wc[t], wd[t] = cw, dw
        cj, dj = cj + cw, dj + dw
        z = zr[t - 1] if t else pltpu.roll(zr[steps - 1], 1, 0)
        cw, dw = cw + z * cj, dw + z * dj
    al, be, ga, de = one, zero, one, zero
    for j in range(SUB - 1):
        nal, nbe = pltpu.roll(aw * al + bw * be, 1, 0), pltpu.roll(aj * al + bj * be, 1, 0)
        al, be = jnp.where(row == j + 1, nal, al), jnp.where(row == j + 1, nbe, be)
        nga = pltpu.roll(cw * ga + dw * de, SUB - 1, 0)
        nde = pltpu.roll(cj * ga + dj * de, SUB - 1, 0)
        at = SUB - 2 - j
        ga, de = jnp.where(row == at, nga, ga), jnp.where(row == at, nde, de)
    iw = 1.0 / (aj * al + bj * be)[SUB - 1 :, :]
    iv = 1.0 / (cj * ga + dj * de)[:1, :]
    al, be, ga, de = al * iw, be * iw, ga * iv, de * iv
    for t in range(steps):
        gpy[t] = al * wa[t] + be * wb[t]
        gsy[t] = ga * wc[t] + de * wd[t]
    ymat[...] = jnp.zeros_like(ymat)
    ymat[2:3, :] = gsy[0][:1, :]
    ymat[3:4, :] = iw
    ymat[4:5, :] = gpy[steps - 1][SUB - 1 :, :]
    ymat[5:6, :] = first[:1, :]
    ymat[6:7, :] = last[SUB - 1 :, :]
    here = [kz[pl.ds(p * depth, 1), :] for p in range(planes)]
    here = jnp.concatenate(here, 0)
    for t in range(depth - 1):
        after = jnp.concatenate([kz[pl.ds(p * depth + t + 1, 1), :] for p in range(planes)], 0)
        zz[t] = 4.0 / (here + after)
        here = after
    w, j = jnp.ones_like(here), jnp.zeros_like(here)
    ws = []
    for t in range(depth):
        ws.append(w)
        j = j + w
        if t + 1 < depth:
            w = w + zz[t] * j
    ij = 1.0 / j
    for t in range(depth):
        g = ws[t] * ij
        for p in range(planes):
            gpz[pl.ds(p * depth + t, 1), :] = g[p : p + 1, :]
    zmat[1] = ij
    zmat[2] = ws[depth - 1] * ij
    w, j = jnp.ones_like(here), jnp.zeros_like(here)
    ws = []
    for t in reversed(range(depth)):
        ws.append(w)
        j = j + w
        if t:
            w = w + zz[t - 1] * j
    ij = 1.0 / j
    for t in range(depth):
        g = ws[depth - 1 - t] * ij
        for p in range(planes):
            gsz[pl.ds(p * depth + t, 1), :] = g[p : p + 1, :]
    zmat[0] = ws[depth - 1] * ij
    for f in range(2):
        for x in range(2):
            at = (f * 2 + x) * depth
            me = u[at : at + depth, :]
            beside = u[(f * 2 + 1 - x) * depth : (f * 2 + 2 - x) * depth, :]
            other = u[((1 - f) * 2 + x) * depth : ((1 - f) * 2 + x + 1) * depth, :]
            face = 0.5 * (cx[f, 0] + cx[f, 1])
            k = kz[at : at + depth, :]
            flux = 0.5 * (k[1:] + k[:-1]) * (me[1:] - me[:-1])
            none = jnp.zeros((1, length), F32)
            flow = jnp.concatenate([flux, none], 0) - jnp.concatenate([none, flux], 0)
            r0[at : at + depth, :] = (
                (2.0 - 0.5 * cx[f, x]) * me
                + face * (beside - me)
                + cp[x] * (other - me)
                + flow
            )


def y_local_kernel(r0, lo, hi, gpy, gsy, ymat, msg, vloc, rt, ss):
    steps, _, lines = gpy.shape
    length = steps * SUB
    planes = lo.shape[0]
    depth = lines // planes
    row = lax.broadcasted_iota(jnp.int32, (SUB, length), 0)
    parts = []
    for p in range(planes):
        at = p * depth
        top, mid, end = r0[at : at + SUB], r0[at + SUB : at + depth - SUB], r0[at + depth - SUB : at + depth]
        parts += [
            jnp.where(row == 0, top + lo[p : p + 1, :], top),
            mid,
            jnp.where(row == SUB - 1, end + hi[p : p + 1, :], end),
        ]
    rt[...] = jnp.concatenate(parts, 0).T
    s = jnp.zeros((SUB, lines), F32)
    for t in range(steps):
        s = s + gpy[t] * strided(rt, t, SUB, steps)
        ss[t] = s
    q = jnp.zeros((SUB, lines), F32)
    for t in reversed(range(steps)):
        vloc[t] = q
        q = q + gsy[t] * strided(rt, t, SUB, steps)
    srow = lax.broadcasted_iota(jnp.int32, (SUB, lines), 0)
    so, qo = jnp.zeros_like(s), jnp.zeros_like(q)
    for j in range(1, SUB):
        so = so + jnp.where(srow >= j, pltpu.roll(s, j, 0), 0.0)
        qo = qo + jnp.where(srow < SUB - j, pltpu.roll(q, SUB - j, 0), 0.0)
    msg[...] = ymat[...]
    msg[0:1, :] = (q + qo)[:1, :]
    msg[1:2, :] = (s + so)[SUB - 1 :, :]
    w = 1.0 / ymat[3:4, :]
    for t in range(steps):
        vloc[t] = gsy[t] * w * (ss[t] + so) + gpy[t] * w * (vloc[t] + qo)


def y_finish_kernel(me, m0, m1, m2, m3, vloc, gpy, gsy, u, gpz, gsz, rz, az, dz, buf, vt):
    steps, _, lines = gpy.shape
    planes = az.shape[0]
    depth = lines // planes
    got = (m0, m1, m2, m3)
    mine = me[0]
    for k in range(4):
        buf[lax.rem(mine + 4 - k, 4)] = got[k][...]
    seg = []
    for j in range(4):
        s = buf[j]
        seg.append([s[i : i + 1, :] for i in range(7)])
    zero = jnp.zeros((1, lines), F32)
    gap = [4.0 / (seg[j][6] + seg[j + 1][5]) for j in range(3)]
    e, r = zero, 4.0 / seg[0][5]
    el, rl = e, r
    for j in range(3):
        a, d, b, c, f = seg[j][:5]
        inv = 1.0 / (r + b)
        e, r = d + c * (e - a) * inv, f - c * c * inv + gap[j]
        el, rl = jnp.where(mine == j + 1, e, el), jnp.where(mine == j + 1, r, rl)
    e, r = zero, 4.0 / seg[3][6]
    er, rr = e, r
    for j in (3, 2, 1):
        a, d, b, c, f = seg[j][:5]
        inv = 1.0 / (r + f)
        e, r = a + c * (e - d) * inv, b - c * c * inv + gap[j - 1]
        er, rr = jnp.where(mine == j - 1, e, er), jnp.where(mine == j - 1, r, rr)
    a, d, b, c, f = [m0[i : i + 1, :] for i in range(5)]
    left, right = b + rl, f + rr
    inv = 1.0 / (left * right - c * c)
    ql = ((el - a) * right - c * (er - d)) * inv
    qr = ((er - d) * left - c * (el - a)) * inv
    for t in range(steps):
        vt[pl.ds(t, SUB, stride=steps), :] = vloc[t] + gsy[t] * ql + gpy[t] * qr
    v = vt[...].T
    for p in range(planes):
        at = p * depth
        r = v[at : at + depth, :] - 2.0 * u[at : at + depth, :]
        rz[at : at + depth, :] = r
        az[p : p + 1, :] = jnp.sum(gsz[at : at + depth, :] * r, axis=0, keepdims=True)
        dz[p : p + 1, :] = jnp.sum(gpz[at : at + depth, :] * r, axis=0, keepdims=True)


def z_local_kernel(u, rz, gpz, gsz, cross, out):
    planes, length = cross.shape
    depth = rz.shape[0] // planes
    for p in range(planes):
        w = 1.0 / cross[p : p + 1, :]
        s = jnp.zeros((1, length), F32)
        ss = []
        for t in range(depth):
            at = pl.ds(p * depth + t, 1)
            s = s + gpz[at, :] * rz[at, :]
            ss.append(s)
        q = jnp.zeros((1, length), F32)
        for t in reversed(range(depth)):
            at = pl.ds(p * depth + t, 1)
            out[at, :] = u[at, :] + w * (gsz[at, :] * ss[t] + gpz[at, :] * q)
            q = q + gsz[at, :] * rz[at, :]


def call(kernel, outs, scratch, cost, in_specs, *args):
    return pl.pallas_call(
        kernel,
        out_shape=[jax.ShapeDtypeStruct(s, F32) for s in outs],
        in_specs=in_specs,
        out_specs=[VMEM] * len(outs),
        scratch_shapes=[pltpu.VMEM(s, F32) for s in scratch],
        compiler_params=pltpu.CompilerParams(vmem_limit_bytes=40 * 1024 * 1024),
        cost_estimate=pl.CostEstimate(flops=cost, bytes_accessed=cost // 4, transcendentals=0),
    )(*args)


def join(s, t):
    a1, d1, b1, e1, f1 = s
    a2, d2, b2, e2, f2 = t
    inv = 1.0 / (f1 + b2)
    jump = (a2 - d1) * inv
    cross = e1 * inv
    return (
        a1 + e1 * jump,
        d2 - e2 * jump,
        b1 - e1 * cross,
        e2 * cross,
        f2 - e2 * e2 * inv,
    )


def middle(s, t, ql, qr):
    return (t[0] - s[1] + t[3] * qr - s[3] * ql) / (s[4] + t[2])


def ring(value, shift_of, position):
    got = [value] + [lax.ppermute(value, "gz", shift_of(k)) for k in (1, 2, 3)]
    ordered = []
    for j in range(4):
        pick = got[0]
        for k in (1, 2, 3):
            pick = jnp.where(position == (j + k) % 4, got[k], pick)
        ordered.append(tuple(pick[i] for i in range(5)))
    return ordered


def around_y(k):
    return [(i, (i // 8) * 8 + ((i // 2 % 4 + k) % 4) * 2 + i % 2) for i in range(32)]


def around_x(k):
    return [(i, ((i // 8 + k) % 4) * 8 + i % 8) for i in range(32)]


def shards(fields, cond_x, cond_y, cond_z, coupling):
    nf, nx, nz, ny = fields.shape
    planes, lines = nf * nx, nf * nx * nz
    u, ky, kz = (a.reshape(lines, ny) for a in (fields, cond_y, cond_z))
    u3, kz3 = u.reshape(planes, nz, ny), kz.reshape(planes, nz, ny)
    iy, iz = lax.axis_index("gy"), lax.axis_index("gz")
    peers = lax.axis_size("gz")
    low = jnp.stack([u3[:, 0], kz3[:, 0]])
    high = jnp.stack([u3[:, -1], kz3[:, -1]])
    below = lax.ppermute(high, "gz", [(i, (i + 1) % peers) for i in range(peers)])
    above = lax.ppermute(low, "gz", [(i, (i - 1) % peers) for i in range(peers)])
    steps = ny // SUB
    tall = (steps, SUB, lines)
    gpy, gsy, ymat, gpz, gsz, zmat, r0 = call(
        factor_kernel,
        [tall, tall, (8, lines), (lines, ny), (lines, ny), (3, planes, ny), (lines, ny)],
        [(ny, lines)] + [tall] * 5 + [(nz, planes, ny)],
        4_000_000,
        [SMEM, SMEM, VMEM, VMEM, VMEM],
        cond_x, coupling, u, ky, kz,
    )
    below = jnp.where(iz == 0, 0.0, below)
    above = jnp.where(iz == peers - 1, 0.0, above)
    lo = 0.5 * (below[1] + low[1]) * (below[0] - low[0])
    hi = 0.5 * (above[1] + high[1]) * (above[0] - high[0])
    msg, vloc = call(
        y_local_kernel, [(8, lines), tall], [(ny, lines), tall], 2_000_000, [VMEM] * 6,
        r0, lo, hi, gpy, gsy, ymat,
    )
    others = [lax.ppermute(msg, "gy", [(i, (i + k) % 4) for i in range(4)]) for k in (1, 2, 3)]
    rz, az, dz = call(
        y_finish_kernel,
        [(lines, ny), (planes, ny), (planes, ny)],
        [(4, 8, lines), (ny, lines)],
        1_000_000,
        [SMEM] + [VMEM] * 10,
        iy.reshape(1).astype(jnp.int32), msg, *others, vloc, gpy, gsy, u, gpz, gsz,
    )
    b = zmat[0] + jnp.where(iz == 0, 4.0 / low[1], 0.0)
    f = zmat[2] + 4.0 / (above[1] + high[1])
    own = jnp.stack([az, dz, b, zmat[1], f])
    peer = lax.ppermute(own, "gz", [(i, i ^ 1) for i in range(peers)])
    [local] = call(
        z_local_kernel, [(lines, ny)], [], 1_000_000, [VMEM] * 5, u, rz, gpz, gsz, zmat[1]
    )
    core, at_y, at_x = iz % 2, iz // 2 % 4, iz // 8
    first, second = jnp.where(core == 0, own, peer), jnp.where(core == 0, peer, own)
    chip = jnp.stack(join(first, second))
    column = ring(chip, around_y, at_y)
    lower, upper = join(column[0], column[1]), join(column[2], column[3])
    plane = jnp.stack(join(lower, upper))
    whole = ring(plane, around_x, at_x)
    halves = join(whole[0], whole[1]), join(whole[2], whole[3])

    (a1, d1, b1, e1, f1), (a2, d2, b2, e2, f2) = halves
    a, d, b, e, f = join(*halves)
    inv = 1.0 / (b * f - e * e)
    ql, qr = (e * d - f * a) * inv, (e * a - b * d) * inv

    def descend(level, position, ql, qr):
        for bit in range(len(level).bit_length() - 2, -1, -1):
            groups = list(level)
            for _ in range(bit):
                groups = [join(groups[i], groups[i + 1]) for i in range(0, len(groups), 2)]
            n = len(groups)
            span = position // (2**bit)
            pair = [
                tuple(sum_pick(groups, span // 2 * 2 + side, n, i) for i in range(5))
                for side in (0, 1)
            ]
            q = middle(pair[0], pair[1], ql, qr)
            up = span % 2 == 1
            ql, qr = jnp.where(up, -q, ql), jnp.where(up, qr, q)
        return ql, qr

    def sum_pick(groups, index, n, i):
        pick = groups[0][i]
        for j in range(1, n):
            pick = jnp.where(index == j, groups[j][i], pick)
        return pick

    ql, qr = descend(whole, at_x, ql, qr)
    ql, qr = descend(column, at_y, ql, qr)
    ql, qr = descend([tuple(first), tuple(second)], core, ql, qr)
    shape = (planes, nz, ny)
    out = (
        local.reshape(shape)
        + gsz.reshape(shape) * ql[:, None, :]
        + gpz.reshape(shape) * qr[:, None, :]
    )
    return out.reshape(fields.shape)


def solution(mesh):
    block = P(None, None, "gz", "gy")
    return jax.shard_map(
        shards,
        mesh=mesh,
        in_specs=(block, P(), block, block, P()),
        out_specs=block,
        check_vma=False,
    )
```

profile of v0, /device:TPU:0, one launch (start us, length us, event | category | flops | bytes accessed | tf_op | source)
XLA Modules:
  0.0 40.2 jit_solution(7522982660093707888)
XLA Ops:
  0.0 0.9 %fusion.7 = (f32[4,1,512]{2,1,0:T(1,128)S(1)}, f32[4,1,512]{2,1,0:T(1,128)S(1)}) fusion(f32[4,32,512]{2,1,0:T(8,128)} %bitcast.68), kind=kLoop, calls=%fused_computation.100 | loop fusion | bytes 32768 | tf_op jit(solution)/shard_map/slice | solution.py:273
  0.9 0.9 %fusion.8 = (f32[4,1,512]{2,1,0:T(1,128)S(1)}, f32[4,1,512]{2,1,0:T(1,128)S(1)}) fusion(f32[4,32,512]{2,1,0:T(8,128)} %bitcast.61), kind=kLoop, calls=%fused_computation.101 | loop fusion | bytes 32768 | tf_op jit(solution)/shard_map/slice | solution.py:273
  1.8 0.1 collective-permute-start
  1.9 5.1 %collective-permute-start.1 = (f32[2,4,512]{2,1,0:T(4,128)S(1)}, f32[2,4,512]{2,1,0:T(4,128)S(1)}, u32[]{:S(2)}, u32[]{:S(2)}) collective-permute-start(f32[2,4,512]{2,1,0:T(4,128)S(1)} %pad_maximum_fusion.1), channel_id=1, source_target_pairs={{0,31},{1,0},{2,1},{3,2},{4,3},{5,4},{6,5},{7,6},{8,7},{9,8},{10,9... | collective-permute-start | bytes 49160 | tf_op jit(solution)/shard_map/ppermute | solution.py:276
  7.0 0.0 copy-start.4
  7.0 0.0 copy-start.5
  7.0 0.7 %copy-done.4 = f32[2,2]{1,0:T(2,128)S(1)} copy-done((f32[2,2]{1,0:T(2,128)S(1)}, f32[2,2]{1,0:T(2,128)}, u32[]{:S(2)}) %copy-start.4) | copy-done | bytes 40
  7.7 0.0 copy-done.5
  7.7 0.0 copy-start
  7.7 0.9 %copy-done = f32[2,2,32,512]{3,2,1,0:T(8,128)S(1)} copy-done((f32[2,2,32,512]{3,2,1,0:T(8,128)S(1)}, f32[2,2,32,512]{3,2,1,0:T(8,128)}, u32[]{:S(2)}) %copy-start) | copy-done | bytes 262168
  8.7 0.0 copy-start.2
  8.7 0.9 %copy-done.2 = f32[2,2,32,512]{3,2,1,0:T(8,128)S(1)} copy-done((f32[2,2,32,512]{3,2,1,0:T(8,128)S(1)}, f32[2,2,32,512]{3,2,1,0:T(8,128)}, u32[]{:S(2)}) %copy-start.2) | copy-done | bytes 262168
  9.6 0.0 copy-start.3
  9.6 0.9 %copy-done.3 = f32[2,2,32,512]{3,2,1,0:T(8,128)S(1)} copy-done((f32[2,2,32,512]{3,2,1,0:T(8,128)S(1)}, f32[2,2,32,512]{3,2,1,0:T(8,128)}, u32[]{:S(2)}) %copy-start.3) | copy-done | bytes 262168
  10.6 1.5 %shard_map.55 = (f32[64,8,128]{2,1,0:T(8,128)S(1)}, f32[64,8,128]{2,1,0:T(8,128)S(1)}, f32[8,128]{1,0:T(8,128)S(1)}, f32[128,512]{1,0:T(8,128)S(1)}, f32[128,512...) custom-call(f32[2,2]{1,0:T(2,128)S(1)} %copy-done.4, f32[2]{0:T(128)S(1)} %copy-done.5, ...), custom_call_target="tpu_custom_call" | custom-call | flops 4000000 | bytes 1000000 | tf_op jit(solution)/shard_map/pallas_call | solution.py:217
  12.0 0.0 collective-permute-done
  12.1 0.0 collective-permute-done.1
  12.1 0.0 copy-start.1
  12.1 0.4 shard_map.56
  12.6 2.1 %collective-permute-start.2 = (f32[8,128]{1,0:T(8,128)S(1)}, f32[8,128]{1,0:T(8,128)S(1)}, u32[]{:S(2)}, u32[]{:S(2)}) collective-permute-start(f32[8,128]{1,0:T(8,128)S(1)} %get-tuple-element.21.m0), channel_id=1, source_target_pairs={{0,32},{32,64},{64,96},{96,0},{1,33},{33,65},{65,97},{97,1},{2,34}... | collective-permute-start | bytes 12296 | tf_op jit(solution)/shard_map/ppermute | solution.py:295
  14.6 3.6 %collective-permute-start.3 = (f32[8,128]{1,0:T(8,128)S(1)}, f32[8,128]{1,0:T(8,128)S(1)}, u32[]{:S(2)}, u32[]{:S(2)}) collective-permute-start(f32[8,128]{1,0:T(8,128)S(1)} %get-tuple-element.21.m0), channel_id=1, source_target_pairs={{0,64},{32,96},{64,0},{96,32},{1,65},{33,97},{65,1},{97,33},{2,66}... | collective-permute-start | bytes 12296 | tf_op jit(solution)/shard_map/ppermute | solution.py:295
  18.2 1.0 %collective-permute-start.4 = (f32[8,128]{1,0:T(8,128)S(1)}, f32[8,128]{1,0:T(8,128)S(1)}, u32[]{:S(2)}, u32[]{:S(2)}) collective-permute-start(f32[8,128]{1,0:T(8,128)S(1)} %get-tuple-element.21.m0), channel_id=1, source_target_pairs={{0,96},{32,0},{64,32},{96,64},{1,97},{33,1},{65,33},{97,65},{2,98}... | collective-permute-start | bytes 12296 | tf_op jit(solution)/shard_map/ppermute | solution.py:295
  19.2 0.0 collective-permute-done.2.m1
  19.2 0.6 %collective-permute-done.3.m2 = f32[8,128]{1,0:T(8,128)S(1)} collective-permute-done((f32[8,128]{1,0:T(8,128)S(1)}, f32[8,128]{1,0:T(8,128)S(1)}, u32[]{:S(2)}, u32[]{:S(2)}) %collective-permute-start.3) | collective-permute-done | bytes 4128 | tf_op jit(solution)/shard_map/ppermute | solution.py:295
  19.8 2.0 %collective-permute-done.4.m3 = f32[8,128]{1,0:T(8,128)S(1)} collective-permute-done((f32[8,128]{1,0:T(8,128)S(1)}, f32[8,128]{1,0:T(8,128)S(1)}, u32[]{:S(2)}, u32[]{:S(2)}) %collective-permute-start.4) | collective-permute-done | bytes 4128 | tf_op jit(solution)/shard_map/ppermute | solution.py:295
  21.8 0.0 copy-done.1
  21.8 0.4 shard_map.57
  22.3 0.1 collective-permute-start.5
  22.4 1.2 %collective-permute-done.5 = f32[5,4,512]{2,1,0:T(4,128)S(1)} collective-permute-done((f32[5,4,512]{2,1,0:T(4,128)S(1)}, f32[5,4,512]{2,1,0:T(4,128)S(1)}, u32[]{:S(2)}, u32[]{:S(2)}) %collective-permute-start.5) | collective-permute-done | bytes 40992 | tf_op jit(solution)/shard_map/ppermute | solution.py:307
  23.7 0.1 collective-permute-start.6
  23.8 0.3 collective-permute-start.7
  24.1 1.7 %collective-permute-start.8 = (f32[5,4,512]{2,1,0:T(4,128)S(1)}, f32[5,4,512]{2,1,0:T(4,128)S(1)}, u32[]{:S(2)}, u32[]{:S(2)}) collective-permute-start(f32[5,4,512]{2,1,0:T(4,128)S(1)} %constant_dynamic-update-slice_fusion.5), channel_id=1, source_target_pairs={{0,2},{1,3},{2,4},{3,5},{4,6},{5,7},{6,0},{7,1},{8,10},{9,11},{10,... | collective-permute-start | bytes 122888 | tf_op jit(solution)/shard_map/ppermute | solution.py:248
  25.8 2.0 %collective-permute-done.6 = f32[5,4,512]{2,1,0:T(4,128)S(1)} collective-permute-done((f32[5,4,512]{2,1,0:T(4,128)S(1)}, f32[5,4,512]{2,1,0:T(4,128)S(1)}, u32[]{:S(2)}, u32[]{:S(2)}) %collective-permute-start.6) | collective-permute-done | bytes 40992 | tf_op jit(solution)/shard_map/ppermute | solution.py:248
  27.8 1.6 %collective-permute-done.7 = f32[5,4,512]{2,1,0:T(4,128)S(1)} collective-permute-done((f32[5,4,512]{2,1,0:T(4,128)S(1)}, f32[5,4,512]{2,1,0:T(4,128)S(1)}, u32[]{:S(2)}, u32[]{:S(2)}) %collective-permute-start.7) | collective-permute-done | bytes 40992 | tf_op jit(solution)/shard_map/ppermute | solution.py:248
  29.5 1.0 %collective-permute-done.8 = f32[5,4,512]{2,1,0:T(4,128)S(1)} collective-permute-done((f32[5,4,512]{2,1,0:T(4,128)S(1)}, f32[5,4,512]{2,1,0:T(4,128)S(1)}, u32[]{:S(2)}, u32[]{:S(2)}) %collective-permute-start.8) | collective-permute-done | bytes 40992 | tf_op jit(solution)/shard_map/ppermute | solution.py:248
  30.6 1.8 %collective-permute-start.9 = (f32[5,4,512]{2,1,0:T(4,128)S(1)}, f32[5,4,512]{2,1,0:T(4,128)S(1)}, u32[]{:S(2)}, u32[]{:S(2)}) collective-permute-start(f32[5,4,512]{2,1,0:T(4,128)S(1)} %get-tuple-element.99), channel_id=1, source_target_pairs={{0,24},{1,25},{2,26},{3,27},{4,28},{5,29},{6,30},{7,31},{8,0},{9,1... | collective-permute-start | bytes 122888 | tf_op jit(solution)/shard_map/ppermute | solution.py:248
  32.4 0.8 %collective-permute-start.10 = (f32[5,4,512]{2,1,0:T(4,128)S(1)}, f32[5,4,512]{2,1,0:T(4,128)S(1)}, u32[]{:S(2)}, u32[]{:S(2)}) collective-permute-start(f32[5,4,512]{2,1,0:T(4,128)S(1)} %get-tuple-element.99), channel_id=1, source_target_pairs={{0,16},{1,17},{2,18},{3,19},{4,20},{5,21},{6,22},{7,23},{8,24},{9,... | collective-permute-start | bytes 122888 | tf_op jit(solution)/shard_map/ppermute | solution.py:248
  33.2 0.9 %collective-permute-start.11 = (f32[5,4,512]{2,1,0:T(4,128)S(1)}, f32[5,4,512]{2,1,0:T(4,128)S(1)}, u32[]{:S(2)}, u32[]{:S(2)}) collective-permute-start(f32[5,4,512]{2,1,0:T(4,128)S(1)} %get-tuple-element.99), channel_id=1, source_target_pairs={{0,8},{1,9},{2,10},{3,11},{4,12},{5,13},{6,14},{7,15},{8,16},{9,17... | collective-permute-start | bytes 122888 | tf_op jit(solution)/shard_map/ppermute | solution.py:248
  34.1 0.2 shard_map.58
  34.8 0.0 collective-permute-done.9
  34.8 3.1 %collective-permute-done.10 = f32[5,4,512]{2,1,0:T(4,128)S(1)} collective-permute-done((f32[5,4,512]{2,1,0:T(4,128)S(1)}, f32[5,4,512]{2,1,0:T(4,128)S(1)}, u32[]{:S(2)}, u32[]{:S(2)}) %collective-permute-start.10) | collective-permute-done | bytes 40992 | tf_op jit(solution)/shard_map/ppermute | solution.py:248
  37.9 0.5 %collective-permute-done.11 = f32[5,4,512]{2,1,0:T(4,128)S(1)} collective-permute-done((f32[5,4,512]{2,1,0:T(4,128)S(1)}, f32[5,4,512]{2,1,0:T(4,128)S(1)}, u32[]{:S(2)}, u32[]{:S(2)}) %collective-permute-start.11) | collective-permute-done | bytes 40992 | tf_op jit(solution)/shard_map/ppermute | solution.py:248
  39.0 0.1 add_divide_fusion.3
  39.1 0.2 add_divide_fusion.1
  39.3 0.1 negate_select_fusion
  39.4 0.8 %multiply_add_fusion = f32[2,2,32,512]{3,2,1,0:T(8,128)} fusion(f32[2,2,32,512]{3,2,1,0:T(8,128)S(1)} %bitcast.65, f32[2,2,32,512]{3,2,1,0:T(8,128)S(1)} %bitcast.67, f32[2,2,32,512]{3,2,1,0:T(8,128)S(1)} %bitcast.66, f32[2,2,512]{2,1,0:T(2,128)S(1)} %broadcast_select_fusion.8, f32[2,2,512]{2,1,0:T(2,128)S(1)} %get-tuple-element.29), kind=kLoop, calls=%fused_computation | loop fusion | flops 262144 | bytes 1064960 | tf_op jit(solution)/shard_map/add | solution.py:352
  (78 shorter events, 1.3 us)
Async XLA Ops:
  1.8 10.2 %collective-permute-start = (f32[2,4,512]{2,1,0:T(4,128)S(1)}, f32[2,4,512]{2,1,0:T(4,128)S(1)}, u32[]{:S(2)}, u32[]{:S(2)}) collective-permute-start(f32[2,4,512]{2,1,0:T(4,128)S(1)} %pad_maximum_fusion), channel_id=1, source_target_pairs={{0,1},{1,2},{2,3},{3,4},{4,5},{5,6},{6,7},{7,8},{8,9},{9,10},{10,1... | collective-permute-start | bytes 49160 | tf_op jit(solution)/shard_map/ppermute | solution.py:275
  1.9 10.2 %collective-permute-start.1 = (f32[2,4,512]{2,1,0:T(4,128)S(1)}, f32[2,4,512]{2,1,0:T(4,128)S(1)}, u32[]{:S(2)}, u32[]{:S(2)}) collective-permute-start(f32[2,4,512]{2,1,0:T(4,128)S(1)} %pad_maximum_fusion.1), channel_id=1, source_target_pairs={{0,31},{1,0},{2,1},{3,2},{4,3},{5,4},{6,5},{7,6},{8,7},{9,8},{10,9... | collective-permute-start | bytes 49160 | tf_op jit(solution)/shard_map/ppermute | solution.py:276
  7.0 0.7 %copy-start.4 = (f32[2,2]{1,0:T(2,128)S(1)}, f32[2,2]{1,0:T(2,128)}, u32[]{:S(2)}) copy-start(f32[2,2]{1,0:T(2,128)} %cx.1) | copy-start | bytes 52
  7.0 0.7 %copy-start.5 = (f32[2]{0:T(128)S(1)}, f32[2]{0:T(128)}, u32[]{:S(2)}) copy-start(f32[2]{0:T(128)} %cp.1) | copy-start | bytes 28
  7.7 1.0 %copy-start = (f32[2,2,32,512]{3,2,1,0:T(8,128)S(1)}, f32[2,2,32,512]{3,2,1,0:T(8,128)}, u32[]{:S(2)}) copy-start(f32[2,2,32,512]{3,2,1,0:T(8,128)} %param.5) | copy-start | bytes 786436
  8.7 0.9 %copy-start.2 = (f32[2,2,32,512]{3,2,1,0:T(8,128)S(1)}, f32[2,2,32,512]{3,2,1,0:T(8,128)}, u32[]{:S(2)}) copy-start(f32[2,2,32,512]{3,2,1,0:T(8,128)} %param.8) | copy-start | bytes 786436
  9.6 0.9 %copy-start.3 = (f32[2,2,32,512]{3,2,1,0:T(8,128)S(1)}, f32[2,2,32,512]{3,2,1,0:T(8,128)}, u32[]{:S(2)}) copy-start(f32[2,2,32,512]{3,2,1,0:T(8,128)} %param.7) | copy-start | bytes 786436
  12.1 9.7 %copy-start.1 = (f32[2,2,32,512]{3,2,1,0:T(8,128)S(1)}, f32[2,2,32,512]{3,2,1,0:T(8,128)}, u32[]{:S(2)}) copy-start(f32[2,2,32,512]{3,2,1,0:T(8,128)} %param.5) | copy-start | bytes 786436
  12.6 6.7 %collective-permute-start.2 = (f32[8,128]{1,0:T(8,128)S(1)}, f32[8,128]{1,0:T(8,128)S(1)}, u32[]{:S(2)}, u32[]{:S(2)}) collective-permute-start(f32[8,128]{1,0:T(8,128)S(1)} %get-tuple-element.21.m0), channel_id=1, source_target_pairs={{0,32},{32,64},{64,96},{96,0},{1,33},{33,65},{65,97},{97,1},{2,34}... | collective-permute-start | bytes 12296 | tf_op jit(solution)/shard_map/ppermute | solution.py:295
  14.6 5.2 %collective-permute-start.3 = (f32[8,128]{1,0:T(8,128)S(1)}, f32[8,128]{1,0:T(8,128)S(1)}, u32[]{:S(2)}, u32[]{:S(2)}) collective-permute-start(f32[8,128]{1,0:T(8,128)S(1)} %get-tuple-element.21.m0), channel_id=1, source_target_pairs={{0,64},{32,96},{64,0},{96,32},{1,65},{33,97},{65,1},{97,33},{2,66}... | collective-permute-start | bytes 12296 | tf_op jit(solution)/shard_map/ppermute | solution.py:295
  18.2 3.6 %collective-permute-start.4 = (f32[8,128]{1,0:T(8,128)S(1)}, f32[8,128]{1,0:T(8,128)S(1)}, u32[]{:S(2)}, u32[]{:S(2)}) collective-permute-start(f32[8,128]{1,0:T(8,128)S(1)} %get-tuple-element.21.m0), channel_id=1, source_target_pairs={{0,96},{32,0},{64,32},{96,64},{1,97},{33,1},{65,33},{97,65},{2,98}... | collective-permute-start | bytes 12296 | tf_op jit(solution)/shard_map/ppermute | solution.py:295
  22.3 1.3 %collective-permute-start.5 = (f32[5,4,512]{2,1,0:T(4,128)S(1)}, f32[5,4,512]{2,1,0:T(4,128)S(1)}, u32[]{:S(2)}, u32[]{:S(2)}) collective-permute-start(f32[5,4,512]{2,1,0:T(4,128)S(1)} %get-tuple-element.121), channel_id=1, source_target_pairs={{0,1},{1,0},{2,3},{3,2},{4,5},{5,4},{6,7},{7,6},{8,9},{9,8},{10,11... | collective-permute-start | bytes 122888 | tf_op jit(solution)/shard_map/ppermute | solution.py:307
  23.7 4.1 %collective-permute-start.6 = (f32[5,4,512]{2,1,0:T(4,128)S(1)}, f32[5,4,512]{2,1,0:T(4,128)S(1)}, u32[]{:S(2)}, u32[]{:S(2)}) collective-permute-start(f32[5,4,512]{2,1,0:T(4,128)S(1)} %constant_dynamic-update-slice_fusion.5), channel_id=1, source_target_pairs={{0,6},{1,7},{2,0},{3,1},{4,2},{5,3},{6,4},{7,5},{8,14},{9,15},{10,... | collective-permute-start | bytes 122888 | tf_op jit(solution)/shard_map/ppermute | solution.py:248
  23.8 5.7 %collective-permute-start.7 = (f32[5,4,512]{2,1,0:T(4,128)S(1)}, f32[5,4,512]{2,1,0:T(4,128)S(1)}, u32[]{:S(2)}, u32[]{:S(2)}) collective-permute-start(f32[5,4,512]{2,1,0:T(4,128)S(1)} %constant_dynamic-update-slice_fusion.5), channel_id=1, source_target_pairs={{0,4},{1,5},{2,6},{3,7},{4,0},{5,1},{6,2},{7,3},{8,12},{9,13},{10,... | collective-permute-start | bytes 122888 | tf_op jit(solution)/shard_map/ppermute | solution.py:248
  24.1 6.4 %collective-permute-start.8 = (f32[5,4,512]{2,1,0:T(4,128)S(1)}, f32[5,4,512]{2,1,0:T(4,128)S(1)}, u32[]{:S(2)}, u32[]{:S(2)}) collective-permute-start(f32[5,4,512]{2,1,0:T(4,128)S(1)} %constant_dynamic-update-slice_fusion.5), channel_id=1, source_target_pairs={{0,2},{1,3},{2,4},{3,5},{4,6},{5,7},{6,0},{7,1},{8,10},{9,11},{10,... | collective-permute-start | bytes 122888 | tf_op jit(solution)/shard_map/ppermute | solution.py:248
  30.6 4.2 %collective-permute-start.9 = (f32[5,4,512]{2,1,0:T(4,128)S(1)}, f32[5,4,512]{2,1,0:T(4,128)S(1)}, u32[]{:S(2)}, u32[]{:S(2)}) collective-permute-start(f32[5,4,512]{2,1,0:T(4,128)S(1)} %get-tuple-element.99), channel_id=1, source_target_pairs={{0,24},{1,25},{2,26},{3,27},{4,28},{5,29},{6,30},{7,31},{8,0},{9,1... | collective-permute-start | bytes 122888 | tf_op jit(solution)/shard_map/ppermute | solution.py:248
  32.4 5.5 %collective-permute-start.10 = (f32[5,4,512]{2,1,0:T(4,128)S(1)}, f32[5,4,512]{2,1,0:T(4,128)S(1)}, u32[]{:S(2)}, u32[]{:S(2)}) collective-permute-start(f32[5,4,512]{2,1,0:T(4,128)S(1)} %get-tuple-element.99), channel_id=1, source_target_pairs={{0,16},{1,17},{2,18},{3,19},{4,20},{5,21},{6,22},{7,23},{8,24},{9,... | collective-permute-start | bytes 122888 | tf_op jit(solution)/shard_map/ppermute | solution.py:248
  33.2 5.2 %collective-permute-start.11 = (f32[5,4,512]{2,1,0:T(4,128)S(1)}, f32[5,4,512]{2,1,0:T(4,128)S(1)}, u32[]{:S(2)}, u32[]{:S(2)}) collective-permute-start(f32[5,4,512]{2,1,0:T(4,128)S(1)} %get-tuple-element.99), channel_id=1, source_target_pairs={{0,8},{1,9},{2,10},{3,11},{4,12},{5,13},{6,14},{7,15},{8,16},{9,17... | collective-permute-start | bytes 122888 | tf_op jit(solution)/shard_map/ppermute | solution.py:248
where the time goes:
time: 40.5 us; the launch traced here: 40.2 us
  starting transfers between devices  17.5 us (43%)
  waiting for transfers between devices  12.1 us (30%)
  local copies, waits for them, and re-layouts  6.11 us (15%)
  Pallas kernels  2.51 us (6%)
  other arithmetic  1.68 us (4%)
    ppermute x6, waiting for transfers between devices, ring(): got = [value] + [lax.ppermute(value, 'gz', shift_of(k)) for k in (1, 2, 3)]  8.28 us
    ppermute x3, starting transfers between devices, shards(): lax.ppermute(msg, 'gy', [(i, (i + k) % 4) for i in range(4)])  6.66 us
    ppermute x6, starting transfers between devices, ring(): got = [value] + [lax.ppermute(value, 'gz', shift_of(k)) for k in (1, 2, 3)]  5.56 us
    ppermute x1, starting transfers between devices, shards(): lax.ppermute(low, 'gz', [(i, (i - 1) % peers) for i in range(peers)])  5.11 us
    unnamed x15, local copies, waits for them, and re-layouts  3.56 us
    ppermute x3, waiting for transfers between devices, shards(): lax.ppermute(msg, 'gy', [(i, (i + k) % 4) for i in range(4)])  2.6 us
    pallas_call x4, Pallas kernels, call(): pl.pallas_call(kernel, out_shape=[jax.ShapeDtypeStruct(s, F32) for s in o...  2.51 us
    slice x2, local copies, waits for them, and re-layouts, shards(): low = jnp.stack([u3[:, 0], kz3[:, 0]])  1.77 us
  transfers between devices with their start and end apart: 12, of which 8 were waited for; matrix products, arithmetic and copies ran while one was open for 1% of the time, Pallas kernels for 4%

commit v1 on v0

v1 whole, which is shorter than its diff:
```python
import functools

import jax
import jax.numpy as jnp
from jax import lax
from jax.experimental import pallas as pl
from jax.experimental.pallas import tpu as pltpu
from jax.sharding import PartitionSpec as P

SUB = 8
F32 = jnp.float32
VMEM = pl.BlockSpec(memory_space=pltpu.VMEM)
SMEM = pl.BlockSpec(memory_space=pltpu.SMEM)


def strided(ref, start, count, stride):
    return ref[pl.ds(start, count, stride=stride), :]


def load_kernel(uh, kyh, kzh, u, ky, kz, low, high, inner, outer, sem):
    copies = [
        pltpu.make_async_copy(src, dst, sem.at[i])
        for i, (src, dst) in enumerate(((uh, u), (kzh, kz), (kyh, ky)))
    ]
    for copy in copies:
        copy.start()
    planes = low.shape[1]
    depth = u.shape[0] // planes
    even = lax.axis_index("gz") % 2 == 0
    for i, array in enumerate((u, kz)):
        copies[i].wait()
        for p in range(planes):
            at = p * depth
            bottom, top = array[at : at + 1, :], array[at + depth - 1 : at + depth, :]
            low[i, p : p + 1, :] = bottom
            high[i, p : p + 1, :] = top
            inner[i, p : p + 1, :] = jnp.where(even, top, bottom)
            outer[i, p : p + 1, :] = jnp.where(even, bottom, top)
    copies[2].wait()


def factor_kernel(
    cxh, cph, u, ky, kz, gpy, gsy, ymat, gpz, gsz, zmat, r0, kt, zr, wa, wb, wc, wd, zz, cx, cp, sem
):
    small = [pltpu.make_async_copy(cxh, cx, sem.at[0]), pltpu.make_async_copy(cph, cp, sem.at[1])]
    for copy in small:
        copy.start()
    lines, length = ky.shape
    steps = length // SUB
    planes, depth = zmat.shape[1], lines // zmat.shape[1]
    kt[...] = ky[...].T
    first = strided(kt, 0, SUB, steps)
    here = first
    for t in range(steps):
        after = strided(kt, t + 1, SUB, steps) if t + 1 < steps else pltpu.roll(first, SUB - 1, 0)
        zr[t] = 4.0 / (here + after)
        here = after
    last = strided(kt, steps - 1, SUB, steps)
    row = lax.broadcasted_iota(jnp.int32, (SUB, lines), 0)
    one, zero = jnp.ones((SUB, lines), F32), jnp.zeros((SUB, lines), F32)
    aw, aj, bw, bj = one, zero, zero, one
    for t in range(steps):
        wa[t], wb[t] = aw, bw
        aj, bj = aj + aw, bj + bw
        aw, bw = aw + zr[t] * aj, bw + zr[t] * bj
    cw, cj, dw, dj = one, zero, zero, one
    for t in reversed(range(steps)):
        wc[t], wd[t] = cw, dw
        cj, dj = cj + cw, dj + dw
        z = zr[t - 1] if t else pltpu.roll(zr[steps - 1], 1, 0)
        cw, dw = cw + z * cj, dw + z * dj
    al, be, ga, de = one, zero, one, zero
    for j in range(SUB - 1):
        nal, nbe = pltpu.roll(aw * al + bw * be, 1, 0), pltpu.roll(aj * al + bj * be, 1, 0)
        al, be = jnp.where(row == j + 1, nal, al), jnp.where(row == j + 1, nbe, be)
        nga = pltpu.roll(cw * ga + dw * de, SUB - 1, 0)
        nde = pltpu.roll(cj * ga + dj * de, SUB - 1, 0)
        at = SUB - 2 - j
        ga, de = jnp.where(row == at, nga, ga), jnp.where(row == at, nde, de)
    iw = 1.0 / (aj * al + bj * be)[SUB - 1 :, :]
    iv = 1.0 / (cj * ga + dj * de)[:1, :]
    al, be, ga, de = al * iw, be * iw, ga * iv, de * iv
    for t in range(steps):
        gpy[t] = al * wa[t] + be * wb[t]
        gsy[t] = ga * wc[t] + de * wd[t]
    ymat[...] = jnp.zeros_like(ymat)
    ymat[2:3, :] = gsy[0][:1, :]
    ymat[3:4, :] = iw
    ymat[4:5, :] = gpy[steps - 1][SUB - 1 :, :]
    ymat[5:6, :] = first[:1, :]
    ymat[6:7, :] = last[SUB - 1 :, :]
    here = [kz[pl.ds(p * depth, 1), :] for p in range(planes)]
    here = jnp.concatenate(here, 0)
    for t in range(depth - 1):
        after = jnp.concatenate([kz[pl.ds(p * depth + t + 1, 1), :] for p in range(planes)], 0)
        zz[t] = 4.0 / (here + after)
        here = after
    w, j = jnp.ones_like(here), jnp.zeros_like(here)
    ws = []
    for t in range(depth):
        ws.append(w)
        j = j + w
        if t + 1 < depth:
            w = w + zz[t] * j
    ij = 1.0 / j
    for t in range(depth):
        g = ws[t] * ij
        for p in range(planes):
            gpz[pl.ds(p * depth + t, 1), :] = g[p : p + 1, :]
    zmat[1] = ij
    zmat[2] = ws[depth - 1] * ij
    w, j = jnp.ones_like(here), jnp.zeros_like(here)
    ws = []
    for t in reversed(range(depth)):
        ws.append(w)
        j = j + w
        if t:
            w = w + zz[t - 1] * j
    ij = 1.0 / j
    for t in range(depth):
        g = ws[depth - 1 - t] * ij
        for p in range(planes):
            gsz[pl.ds(p * depth + t, 1), :] = g[p : p + 1, :]
    zmat[0] = ws[depth - 1] * ij
    for copy in small:
        copy.wait()
    for f in range(2):
        for x in range(2):
            at = (f * 2 + x) * depth
            me = u[at : at + depth, :]
            beside = u[(f * 2 + 1 - x) * depth : (f * 2 + 2 - x) * depth, :]
            other = u[((1 - f) * 2 + x) * depth : ((1 - f) * 2 + x + 1) * depth, :]
            face = 0.5 * (cx[f, 0] + cx[f, 1])
            k = kz[at : at + depth, :]
            flux = 0.5 * (k[1:] + k[:-1]) * (me[1:] - me[:-1])
            none = jnp.zeros((1, length), F32)
            flow = jnp.concatenate([flux, none], 0) - jnp.concatenate([none, flux], 0)
            r0[at : at + depth, :] = (
                (2.0 - 0.5 * cx[f, x]) * me
                + face * (beside - me)
                + cp[x] * (other - me)
                + flow
            )


def y_ends_kernel(peers, r0, low, high, inner, outer, gpy, gsy, ymat, msg, rt, ss, qq):
    steps, _, lines = gpy.shape
    length = steps * SUB
    planes = low.shape[1]
    depth = lines // planes
    under = jnp.where(lax.axis_index("gz") > 0, 1.0, 0.0)
    over = jnp.where(lax.axis_index("gz") < peers - 1, 1.0, 0.0)
    even = lax.axis_index("gz") % 2 == 0
    below = [jnp.where(even, outer[i], inner[i]) * under for i in range(2)]
    above = [jnp.where(even, inner[i], outer[i]) * over for i in range(2)]
    lo = 0.5 * (below[1] + low[1]) * (below[0] - low[0])
    hi = 0.5 * (above[1] + high[1]) * (above[0] - high[0])
    row = lax.broadcasted_iota(jnp.int32, (SUB, length), 0)
    parts = []
    for p in range(planes):
        i = p * depth
        top, mid, end = r0[i : i + SUB], r0[i + SUB : i + depth - SUB], r0[i + depth - SUB : i + depth]
        parts += [
            jnp.where(row == 0, top + lo[p : p + 1, :], top),
            mid,
            jnp.where(row == SUB - 1, end + hi[p : p + 1, :], end),
        ]
    rt[...] = jnp.concatenate(parts, 0).T
    s = jnp.zeros((SUB, lines), F32)
    q = jnp.zeros((SUB, lines), F32)
    for t in range(steps):
        back = steps - 1 - t
        s = s + gpy[t] * strided(rt, t, SUB, steps)
        ss[t] = s
        qq[back] = q
        q = q + gsy[back] * strided(rt, back, SUB, steps)
    msg[...] = ymat[...]
    msg[0:1, :] = jnp.sum(q, axis=0, keepdims=True)
    msg[1:2, :] = jnp.sum(s, axis=0, keepdims=True)


def y_local_kernel(peers, low, high, inner, outer, zmat, rt, ss, qq, gpy, gsy, ymat, vloc, zends):
    steps, _, lines = gpy.shape
    s = ss[steps - 1]
    q = qq[0] + gsy[0] * strided(rt, 0, SUB, steps)
    row = lax.broadcasted_iota(jnp.int32, (SUB, lines), 0)
    so, qo = jnp.zeros_like(s), jnp.zeros_like(q)
    for j in range(1, SUB):
        so = so + jnp.where(row >= j, pltpu.roll(s, j, 0), 0.0)
        qo = qo + jnp.where(row < SUB - j, pltpu.roll(q, SUB - j, 0), 0.0)
    w = 1.0 / ymat[3:4, :]
    for t in range(steps):
        vloc[t] = gsy[t] * w * (ss[t] + so) + gpy[t] * w * (qq[t] + qo)
    under = jnp.where(lax.axis_index("gz") > 0, 0.0, 1.0)
    over = jnp.where(lax.axis_index("gz") < peers - 1, 1.0, 0.0)
    zends[0] = zmat[0] + under * 4.0 / low[1]
    zends[1] = zmat[1]
    above = jnp.where(lax.axis_index("gz") % 2 == 0, inner[1], outer[1])
    zends[2] = zmat[2] + 4.0 / (above * over + high[1])


def y_finish_kernel(m0, m1, m2, m3, vloc, gpy, gsy, u, gpz, gsz, zends, rz, own, buf, vt):
    steps, _, lines = gpy.shape
    planes = own.shape[1]
    depth = lines // planes
    got = (m0, m1, m2, m3)
    mine = lax.axis_index("gy")
    for k in range(4):
        buf[mine ^ k] = got[k][...]
    seg = []
    for j in range(4):
        s = buf[j]
        seg.append([s[i : i + 1, :] for i in range(7)])
    zero = jnp.zeros((1, lines), F32)
    gap = [4.0 / (seg[j][6] + seg[j + 1][5]) for j in range(3)]
    e, r = zero, 4.0 / seg[0][5]
    el, rl = e, r
    for j in range(3):
        a, d, b, c, f = seg[j][:5]
        inv = 1.0 / (r + b)
        e, r = d + c * (e - a) * inv, f - c * c * inv + gap[j]
        el, rl = jnp.where(mine == j + 1, e, el), jnp.where(mine == j + 1, r, rl)
    e, r = zero, 4.0 / seg[3][6]
    er, rr = e, r
    for j in (3, 2, 1):
        a, d, b, c, f = seg[j][:5]
        inv = 1.0 / (r + f)
        e, r = a + c * (e - d) * inv, b - c * c * inv + gap[j - 1]
        er, rr = jnp.where(mine == j - 1, e, er), jnp.where(mine == j - 1, r, rr)
    a, d, b, c, f = [m0[i : i + 1, :] for i in range(5)]
    left, right = b + rl, f + rr
    inv = 1.0 / (left * right - c * c)
    ql = ((el - a) * right - c * (er - d)) * inv
    qr = ((er - d) * left - c * (el - a)) * inv
    for t in range(steps):
        vt[pl.ds(t, SUB, stride=steps), :] = vloc[t] + gsy[t] * ql + gpy[t] * qr
    v = vt[...].T
    for p in range(planes):
        i = p * depth
        r = v[i : i + depth, :] - 2.0 * u[i : i + depth, :]
        rz[i : i + depth, :] = r
        own[0, p : p + 1, :] = jnp.sum(gsz[i : i + depth, :] * r, axis=0, keepdims=True)
        own[1, p : p + 1, :] = jnp.sum(gpz[i : i + depth, :] * r, axis=0, keepdims=True)
    for i in range(3):
        own[i + 2] = zends[i]


def z_local_kernel(u, rz, gpz, gsz, zmat, out):
    _, planes, length = zmat.shape
    depth = rz.shape[0] // planes
    for p in range(planes):
        w = 1.0 / zmat[1, p : p + 1, :]
        s = jnp.zeros((1, length), F32)
        ss = []
        for t in range(depth):
            at = pl.ds(p * depth + t, 1)
            s = s + gpz[at, :] * rz[at, :]
            ss.append(s)
        q = jnp.zeros((1, length), F32)
        for t in reversed(range(depth)):
            at = pl.ds(p * depth + t, 1)
            out[at, :] = u[at, :] + w * (gsz[at, :] * ss[t] + gpz[at, :] * q)
            q = q + gsz[at, :] * rz[at, :]


def call(kernel, outs, scratch, cost, in_specs, *args, vmem=32):
    return pl.pallas_call(
        kernel,
        out_shape=[jax.ShapeDtypeStruct(s, F32) for s in outs],
        in_specs=in_specs,
        out_specs=[VMEM] * len(outs),
        scratch_shapes=[pltpu.VMEM(s, F32) if isinstance(s, tuple) else s for s in scratch],
        compiler_params=pltpu.CompilerParams(vmem_limit_bytes=int(vmem * 2**20)),
        cost_estimate=pl.CostEstimate(flops=cost, bytes_accessed=cost // 4, transcendentals=0),
    )(*args)


def join(s, t):
    a1, d1, b1, e1, f1 = s
    a2, d2, b2, e2, f2 = t
    inv = 1.0 / (f1 + b2)
    jump = (a2 - d1) * inv
    cross = e1 * inv
    return (
        a1 + e1 * jump,
        d2 - e2 * jump,
        b1 - e1 * cross,
        e2 * cross,
        f2 - e2 * e2 * inv,
    )


def middle(s, t, ql, qr):
    return (t[0] - s[1] + t[3] * qr - s[3] * ql) / (s[4] + t[2])


def parts_of(ref):
    return tuple(ref[i] for i in range(5))


def choose(flag, s, t):
    return tuple(jnp.where(flag, a, b) for a, b in zip(s, t))


def put(ref, value):
    for i in range(5):
        ref[i] = value[i]


def core_kernel(own, peer, chip):
    lower = lax.axis_index("gz") % 2 == 0
    mine, theirs = parts_of(own), parts_of(peer)
    put(chip, join(choose(lower, mine, theirs), choose(lower, theirs, mine)))


def ring_kernel(position, m0, m1, m2, m3, plane, buf):
    mine = position(lax.axis_index("gz"))
    for k, got in enumerate((m0, m1, m2, m3)):
        buf[mine ^ k] = got[...]
    s = [parts_of(buf.at[j]) for j in range(4)]
    put(plane, join(join(s[0], s[1]), join(s[2], s[3])))


def descend(mine, s, ql, qr):
    lower, upper = join(s[0], s[1]), join(s[2], s[3])
    q = middle(lower, upper, ql, qr)
    up = mine // 2 == 1
    ql, qr = jnp.where(up, -q, ql), jnp.where(up, qr, q)
    q = middle(choose(up, s[2], s[0]), choose(up, s[3], s[1]), ql, qr)
    up = mine % 2 == 1
    return jnp.where(up, -q, ql), jnp.where(up, qr, q)


def finish_kernel(
    own, peer, c0, c1, c2, c3, p0, p1, p2, p3, local, gpz, gsz, out, cbuf, pbuf
):
    iy, ix = position_y(lax.axis_index("gz")), position_x(lax.axis_index("gz"))
    for k, (c, p) in enumerate(((c0, p0), (c1, p1), (c2, p2), (c3, p3))):
        cbuf[iy ^ k] = c[...]
        pbuf[ix ^ k] = p[...]
    column = [parts_of(cbuf.at[j]) for j in range(4)]
    whole = [parts_of(pbuf.at[j]) for j in range(4)]
    a, d, b, e, f = join(join(whole[0], whole[1]), join(whole[2], whole[3]))
    inv = 1.0 / (b * f - e * e)
    ql, qr = (e * d - f * a) * inv, (e * a - b * d) * inv
    ql, qr = descend(ix, whole, ql, qr)
    ql, qr = descend(iy, column, ql, qr)
    lower = lax.axis_index("gz") % 2 == 0
    mine, theirs = parts_of(own), parts_of(peer)
    q = middle(choose(lower, mine, theirs), choose(lower, theirs, mine), ql, qr)
    ql, qr = jnp.where(lower, ql, -q), jnp.where(lower, q, qr)
    planes = ql.shape[0]
    depth = out.shape[0] // planes
    for p in range(planes):
        i = p * depth
        out[i : i + depth, :] = (
            local[i : i + depth, :]
            + gsz[i : i + depth, :] * ql[p : p + 1, :]
            + gpz[i : i + depth, :] * qr[p : p + 1, :]
        )


def position_y(z):
    return z // 2 % 4


def position_x(z):
    return z // 8


def partners(value, axis, count, unit):
    return [
        lax.ppermute(value, axis, [(i, i ^ (k * unit)) for i in range(count)]) for k in (1, 2, 3)
    ]


def shards(fields, cond_x, cond_y, cond_z, coupling):
    nf, nx, nz, ny = fields.shape
    planes, lines = nf * nx, nf * nx * nz
    peers = lax.axis_size("gz")
    steps = ny // SUB
    tall, flat, face, ends = (steps, SUB, lines), (lines, ny), (planes, ny), (5, planes, ny)
    hbm = pl.BlockSpec(memory_space=pltpu.HBM)
    dma = pltpu.SemaphoreType.DMA
    u, ky, kz, low, high, inner, outer = call(
        load_kernel, [flat] * 3 + [(2, *face)] * 4, [dma((3,))], 100_000, [hbm] * 3,
        fields.reshape(flat), cond_y.reshape(flat), cond_z.reshape(flat), vmem=53,
    )
    across = [pair for i in range(1, peers - 1, 2) for pair in ((i, i + 1), (i + 1, i))]
    outer = lax.ppermute(outer, "gz", across)
    inner = lax.ppermute(inner, "gz", [(i, i ^ 1) for i in range(peers)])
    gpy, gsy, ymat, gpz, gsz, zmat, r0 = call(
        factor_kernel,
        [tall, tall, (8, lines), flat, flat, (3, *face), flat],
        [(ny, lines)] + [tall] * 5 + [(nz, *face), pltpu.SMEM(cond_x.shape, F32), pltpu.SMEM(coupling.shape, F32), dma((2,))],
        4_000_000,
        [hbm, hbm, VMEM, VMEM, VMEM],
        cond_x, coupling, u, ky, kz,
    )
    msg, rt, ss, qq = call(
        functools.partial(y_ends_kernel, peers), [(8, lines), (ny, lines), tall, tall], [], 1_000_000, [VMEM] * 8,
        r0, low, high, inner, outer, gpy, gsy, ymat,
    )
    others = partners(msg, "gy", 4, 1)
    vloc, zends = call(
        functools.partial(y_local_kernel, peers), [tall, (3, *face)], [], 1_000_000, [VMEM] * 11,
        low, high, inner, outer, zmat, rt, ss, qq, gpy, gsy, ymat,
    )
    rz, own = call(
        y_finish_kernel, [flat, ends], [(4, 8, lines), (ny, lines)], 1_000_000, [VMEM] * 11,
        msg, *others, vloc, gpy, gsy, u, gpz, gsz, zends,
    )
    peer = lax.ppermute(own, "gz", [(i, i ^ 1) for i in range(peers)])
    [local] = call(z_local_kernel, [flat], [], 1_000_000, [VMEM] * 5, u, rz, gpz, gsz, zmat)
    [chip] = call(core_kernel, [ends], [], 50_000, [VMEM] * 2, own, peer)
    column = [chip] + partners(chip, "gz", peers, 2)
    [plane] = call(
        functools.partial(ring_kernel, position_y), [ends], [(4, *ends)], 50_000,
        [VMEM] * 4, *column,
    )
    whole = [plane] + partners(plane, "gz", peers, 8)
    [out] = call(
        finish_kernel, [flat], [(4, *ends), (4, *ends)], 1_000_000, [VMEM] * 13,
        own, peer, *column, *whole, local, gpz, gsz,
    )
    return out.reshape(fields.shape)


def solution(mesh):
    block = P(None, None, "gz", "gy")
    return jax.shard_map(
        shards,
        mesh=mesh,
        in_specs=(block, P(), block, block, P()),
        out_specs=block,
        check_vma=False,
    )
```

time: 40.5 us -> 35.8 us (0.88)
  local copies, waits for them, and re-layouts: 6.11 us -> 0.67 us
  other arithmetic: 1.68 us -> 0 us
  Pallas kernels: 2.51 us -> 4.18 us
  waiting for transfers between devices: 12.1 us -> 12.7 us
  starting transfers between devices: 17.5 us -> 18 us
    unnamed x15 -> x4, local copies, waits for them, and re-layouts: 3.56 us -> 0.67 us
    slice x6 -> x0, local copies, waits for them, and re-layouts: 1.8 us -> none  [the longest x2 1.77 us: shards(): low = jnp.stack([u3[:, 0], kz3[:, 0]])]
    ppermute x1, starting transfers between devices: 0.09 us -> 1.8 us  [shards(): peer = lax.ppermute(own, 'gz', [(i, i ^ 1) for i in range(peers)])]
    pallas_call x4 -> x9, Pallas kernels: 2.51 us -> 4.18 us  [call(): pl.pallas_call(kernel, out_shape=[jax.ShapeDtypeStruct(s, F32) for s in o...]
    ppermute x11, starting transfers between devices: 17.4 us -> 16.2 us  [the longest x9 15.5 us: partners(): lax.ppermute(value, axis, [(i, i ^ k * unit) for i in range(count)])]
    ppermute x11, waiting for transfers between devices: 10.9 us -> 11.8 us  [the longest x9 11.8 us: partners(): lax.ppermute(value, axis, [(i, i ^ k * unit) for i in range(count)])]
    add x2 -> x0, other arithmetic: 0.82 us -> none  [the longest x1 0.78 us: shards(): local.reshape(shape) + gsz.reshape(shape) * ql[:, None, :]]
    squeeze x40 -> x0, local copies, waits for them, and re-layouts: 0.67 us -> none  [ring(): ordered.append(tuple((pick[i] for i in range(5))))]
  transfers between devices with their start and end apart: 12 -> 12, of which waited for: 8 -> 7; matrix products, arithmetic and copies ran while one was open for 1% -> 0% of each run, Pallas kernels for 4% -> 4%
where the time goes in v1:
time: 35.8 us; the launch traced here: 35.7 us
  starting transfers between devices  18 us (50%)
  waiting for transfers between devices  12.7 us (35%)
  Pallas kernels  4.18 us (12%)
  local copies, waits for them, and re-layouts  0.67 us (2%)
    ppermute x9, starting transfers between devices, partners(): lax.ppermute(value, axis, [(i, i ^ k * unit) for i in range(count)])  15.5 us
    ppermute x9, waiting for transfers between devices, partners(): lax.ppermute(value, axis, [(i, i ^ k * unit) for i in range(count)])  11.8 us
    pallas_call x9, Pallas kernels, call(): pl.pallas_call(kernel, out_shape=[jax.ShapeDtypeStruct(s, F32) for s in o...  4.18 us
    ppermute x1, starting transfers between devices, shards(): peer = lax.ppermute(own, 'gz', [(i, i ^ 1) for i in range(peers)])  1.8 us
    ppermute x1, waiting for transfers between devices, shards(): peer = lax.ppermute(own, 'gz', [(i, i ^ 1) for i in range(peers)])  0.87 us
  transfers between devices with their start and end apart: 12, of which 7 were waited for; matrix products, arithmetic and copies ran while one was open for 0% of the time, Pallas kernels for 4%

profile of v1, /device:TPU:0, one launch (start us, length us, event | category | flops | bytes accessed | tf_op | source)
XLA Modules:
  0.0 35.7 jit_solution(9103385770759120830)
XLA Ops:
  0.0 1.1 %shard_map.55 = (f32[128,512]{1,0:T(8,128)S(1)}, f32[128,512]{1,0:T(8,128)S(1)}, f32[128,512]{1,0:T(8,128)S(1)}, f32[2,4,512]{2,1,0:T(4,128)S(1)}, f32[2,4,512]{...) custom-call(f32[128,512]{1,0:T(8,128)} %bitcast.4, f32[128,512]{1,0:T(8,128)} %bitcast.5, ...), custom_call_target="tpu_custom_call" | custom-call | flops 100000 | bytes 25000 | tf_op jit(solution)/shard_map/pallas_call | solution.py:267
  1.1 0.1 collective-permute-start
  1.2 0.7 %collective-permute-start.1 = (f32[2,4,512]{2,1,0:T(4,128)S(1)}, f32[2,4,512]{2,1,0:T(4,128)S(1)}, u32[]{:S(2)}, u32[]{:S(2)}) collective-permute-start(f32[2,4,512]{2,1,0:T(4,128)S(1)} %get-tuple-element.34), channel_id=1, source_target_pairs={{1,2},{2,1},{3,4},{4,3},{5,6},{6,5},{7,8},{8,7},{9,10},{10,9},{11,... | collective-permute-start | bytes 49160 | tf_op jit(solution)/shard_map/ppermute | solution.py:390
  1.9 0.0 copy-start
  1.9 0.0 copy-start.1
  1.9 0.7 %copy-done = f32[2,2]{1,0:T(2,128)S(1)} copy-done((f32[2,2]{1,0:T(2,128)S(1)}, f32[2,2]{1,0:T(2,128)}, u32[]{:S(2)}) %copy-start) | copy-done | bytes 40
  2.6 0.0 copy-done.1
  2.6 1.0 %shard_map.56 = (f32[64,8,128]{2,1,0:T(8,128)S(1)}, f32[64,8,128]{2,1,0:T(8,128)S(1)}, f32[8,128]{1,0:T(8,128)S(1)}, f32[128,512]{1,0:T(8,128)S(1)}, f32[128,512...) custom-call(f32[2,2]{1,0:T(2,128)S(1)} %copy-done, f32[2]{0:T(128)S(1)} %copy-done.1, ...), custom_call_target="tpu_custom_call" | custom-call | flops 4000000 | bytes 1000000 | tf_op jit(solution)/shard_map/pallas_call | solution.py:267
  3.6 0.0 collective-permute-done.inner
  3.6 0.0 collective-permute-done.1.outer
  3.6 0.4 %shard_map.57 = (f32[8,128]{1,0:T(8,128)S(1)}, f32[512,128]{1,0:T(8,128)S(1)}, f32[64,8,128]{2,1,0:T(8,128)S(1)}, f32[64,8,128]{2,1,0:T(8,128)S(1)}) custom-call(f32[128,512]{1,0:T(8,128)S(1)} %get-tuple-element.30.r0, f32[2,4,512]{2,1,0:T(4,128)S(1)} %get-tuple-element.31.low, f32[2,4,512]{2,1,0:T(4,128)S(1)} %get-tuple-element.32.high, ...), custom_call_target="tpu_custom_call" | custom-call | flops 1000000 | bytes 250000 | tf_op jit(solution)/shard_map/pallas_call | solution.py:267
  4.0 4.2 %collective-permute-start.4 = (f32[8,128]{1,0:T(8,128)S(1)}, f32[8,128]{1,0:T(8,128)S(1)}, u32[]{:S(2)}, u32[]{:S(2)}) collective-permute-start(f32[8,128]{1,0:T(8,128)S(1)} %get-tuple-element.38.m0), channel_id=1, source_target_pairs={{0,96},{32,64},{64,32},{96,0},{1,97},{33,65},{65,33},{97,1},{2,98}... | collective-permute-start | bytes 12296 | tf_op jit(solution)/shard_map/ppermute | solution.py:373
  8.2 0.0 collective-permute-start.3
  8.2 0.9 %collective-permute-start.2 = (f32[8,128]{1,0:T(8,128)S(1)}, f32[8,128]{1,0:T(8,128)S(1)}, u32[]{:S(2)}, u32[]{:S(2)}) collective-permute-start(f32[8,128]{1,0:T(8,128)S(1)} %get-tuple-element.38.m0), channel_id=1, source_target_pairs={{0,32},{32,0},{64,96},{96,64},{1,33},{33,1},{65,97},{97,65},{2,34}... | collective-permute-start | bytes 12296 | tf_op jit(solution)/shard_map/ppermute | solution.py:373
  9.2 0.1 shard_map.58
  9.3 0.5 %collective-permute-done.4.m3 = f32[8,128]{1,0:T(8,128)S(1)} collective-permute-done((f32[8,128]{1,0:T(8,128)S(1)}, f32[8,128]{1,0:T(8,128)S(1)}, u32[]{:S(2)}, u32[]{:S(2)}) %collective-permute-start.4) | collective-permute-done | bytes 4128 | tf_op jit(solution)/shard_map/ppermute | solution.py:373
  9.8 3.5 %collective-permute-done.3.m2 = f32[8,128]{1,0:T(8,128)S(1)} collective-permute-done((f32[8,128]{1,0:T(8,128)S(1)}, f32[8,128]{1,0:T(8,128)S(1)}, u32[]{:S(2)}, u32[]{:S(2)}) %collective-permute-start.3) | collective-permute-done | bytes 4128 | tf_op jit(solution)/shard_map/ppermute | solution.py:373
  13.3 0.0 collective-permute-done.2.m1
  13.3 0.4 %shard_map.59 = (f32[128,512]{1,0:T(8,128)S(1)}, f32[5,4,512]{2,1,0:T(4,128)S(1)}) custom-call(f32[8,128]{1,0:T(8,128)S(1)} %get-tuple-element.38.m0, f32[8,128]{1,0:T(8,128)S(1)} %collective-permute-done.2.m1, f32[8,128]{1,0:T(8,128)S(1)} %collective-permute-done.3.m2, f32[8,128]{1,0:T(8,128)S(1)} %collective-permute-done.4.m3, ...), custom_call_target="tpu_custom_call" | custom-call | flops 1000000 | bytes 250000 | tf_op jit(solution)/shard_map/pallas_call | solution.py:267
  13.7 1.8 %collective-permute-start.5 = (f32[5,4,512]{2,1,0:T(4,128)S(1)}, f32[5,4,512]{2,1,0:T(4,128)S(1)}, u32[]{:S(2)}, u32[]{:S(2)}) collective-permute-start(f32[5,4,512]{2,1,0:T(4,128)S(1)} %get-tuple-element.47.own), channel_id=1, source_target_pairs={{0,1},{1,0},{2,3},{3,2},{4,5},{5,4},{6,7},{7,6},{8,9},{9,8},{10,11... | collective-permute-start | bytes 122888 | tf_op jit(solution)/shard_map/ppermute | solution.py:413
  15.5 0.9 %collective-permute-done.5.peer = f32[5,4,512]{2,1,0:T(4,128)S(1)} collective-permute-done((f32[5,4,512]{2,1,0:T(4,128)S(1)}, f32[5,4,512]{2,1,0:T(4,128)S(1)}, u32[]{:S(2)}, u32[]{:S(2)}) %collective-permute-start.5) | collective-permute-done | bytes 40992 | tf_op jit(solution)/shard_map/ppermute | solution.py:413
  16.4 5.2 %collective-permute-start.8 = (f32[5,4,512]{2,1,0:T(4,128)S(1)}, f32[5,4,512]{2,1,0:T(4,128)S(1)}, u32[]{:S(2)}, u32[]{:S(2)}) collective-permute-start(f32[5,4,512]{2,1,0:T(4,128)S(1)} %shard_map.60.m0.c0), channel_id=1, source_target_pairs={{0,6},{1,7},{2,4},{3,5},{4,2},{5,3},{6,0},{7,1},{8,14},{9,15},{10,... | collective-permute-start | bytes 122888 | tf_op jit(solution)/shard_map/ppermute | solution.py:373
  21.6 0.0 collective-permute-start.7
  21.6 0.9 %collective-permute-start.6 = (f32[5,4,512]{2,1,0:T(4,128)S(1)}, f32[5,4,512]{2,1,0:T(4,128)S(1)}, u32[]{:S(2)}, u32[]{:S(2)}) collective-permute-start(f32[5,4,512]{2,1,0:T(4,128)S(1)} %shard_map.60.m0.c0), channel_id=1, source_target_pairs={{0,2},{1,3},{2,0},{3,1},{4,6},{5,7},{6,4},{7,5},{8,10},{9,11},{10,... | collective-permute-start | bytes 122888 | tf_op jit(solution)/shard_map/ppermute | solution.py:373
  22.6 1.2 %collective-permute-done.8.m3.c3 = f32[5,4,512]{2,1,0:T(4,128)S(1)} collective-permute-done((f32[5,4,512]{2,1,0:T(4,128)S(1)}, f32[5,4,512]{2,1,0:T(4,128)S(1)}, u32[]{:S(2)}, u32[]{:S(2)}) %collective-permute-start.8) | collective-permute-done | bytes 40992 | tf_op jit(solution)/shard_map/ppermute | solution.py:373
  23.7 3.4 %collective-permute-done.7.m2.c2 = f32[5,4,512]{2,1,0:T(4,128)S(1)} collective-permute-done((f32[5,4,512]{2,1,0:T(4,128)S(1)}, f32[5,4,512]{2,1,0:T(4,128)S(1)}, u32[]{:S(2)}, u32[]{:S(2)}) %collective-permute-start.7) | collective-permute-done | bytes 40992 | tf_op jit(solution)/shard_map/ppermute | solution.py:373
  27.1 0.0 collective-permute-done.6.m1.c1
  27.2 2.1 %collective-permute-start.11 = (f32[5,4,512]{2,1,0:T(4,128)S(1)}, f32[5,4,512]{2,1,0:T(4,128)S(1)}, u32[]{:S(2)}, u32[]{:S(2)}) collective-permute-start(f32[5,4,512]{2,1,0:T(4,128)S(1)} %shard_map.61.p0), channel_id=1, source_target_pairs={{0,24},{1,25},{2,26},{3,27},{4,28},{5,29},{6,30},{7,31},{8,16},{9,... | collective-permute-start | bytes 122888 | tf_op jit(solution)/shard_map/ppermute | solution.py:373
  29.3 1.5 %collective-permute-start.10 = (f32[5,4,512]{2,1,0:T(4,128)S(1)}, f32[5,4,512]{2,1,0:T(4,128)S(1)}, u32[]{:S(2)}, u32[]{:S(2)}) collective-permute-start(f32[5,4,512]{2,1,0:T(4,128)S(1)} %shard_map.61.p0), channel_id=1, source_target_pairs={{0,16},{1,17},{2,18},{3,19},{4,20},{5,21},{6,22},{7,23},{8,24},{9,... | collective-permute-start | bytes 122888 | tf_op jit(solution)/shard_map/ppermute | solution.py:373
  30.8 0.5 %collective-permute-start.9 = (f32[5,4,512]{2,1,0:T(4,128)S(1)}, f32[5,4,512]{2,1,0:T(4,128)S(1)}, u32[]{:S(2)}, u32[]{:S(2)}) collective-permute-start(f32[5,4,512]{2,1,0:T(4,128)S(1)} %shard_map.61.p0), channel_id=1, source_target_pairs={{0,8},{1,9},{2,10},{3,11},{4,12},{5,13},{6,14},{7,15},{8,0},{9,1},... | collective-permute-start | bytes 122888 | tf_op jit(solution)/shard_map/ppermute | solution.py:373
  31.4 0.2 shard_map.62.local
  31.6 1.3 %collective-permute-done.11.p3 = f32[5,4,512]{2,1,0:T(4,128)S(1)} collective-permute-done((f32[5,4,512]{2,1,0:T(4,128)S(1)}, f32[5,4,512]{2,1,0:T(4,128)S(1)}, u32[]{:S(2)}, u32[]{:S(2)}) %collective-permute-start.11) | collective-permute-done | bytes 40992 | tf_op jit(solution)/shard_map/ppermute | solution.py:373
  32.9 1.9 %collective-permute-done.10.p2 = f32[5,4,512]{2,1,0:T(4,128)S(1)} collective-permute-done((f32[5,4,512]{2,1,0:T(4,128)S(1)}, f32[5,4,512]{2,1,0:T(4,128)S(1)}, u32[]{:S(2)}, u32[]{:S(2)}) %collective-permute-start.10) | collective-permute-done | bytes 40992 | tf_op jit(solution)/shard_map/ppermute | solution.py:373
  34.8 0.0 collective-permute-done.9.p1
  34.8 0.8 %shard_map.63 = f32[128,512]{1,0:T(8,128)} custom-call(f32[5,4,512]{2,1,0:T(4,128)S(1)} %get-tuple-element.47.own, f32[5,4,512]{2,1,0:T(4,128)S(1)} %collective-permute-done.5.peer, f32[5,4,512]{2,1,0:T(4,128)S(1)} %shard_map.60.m0.c0, f32[5,4,512]{2,1,0:T(4,128)S(1)} %collective-permute-done.6.m1.c1, f32[5,4,512]{2,1,0:T(4,128)S(1)} %collective-permute-done.7.m2.c2, ...), custom_call_target="tpu_custom_call" | custom-call | flops 1000000 | bytes 250000 | tf_op jit(solution)/shard_map/pallas_call | solution.py:267
  (2 shorter events, 0.1 us)
Async XLA Ops:
  1.1 2.5 %collective-permute-start = (f32[2,4,512]{2,1,0:T(4,128)S(1)}, f32[2,4,512]{2,1,0:T(4,128)S(1)}, u32[]{:S(2)}, u32[]{:S(2)}) collective-permute-start(f32[2,4,512]{2,1,0:T(4,128)S(1)} %get-tuple-element.33), channel_id=1, source_target_pairs={{0,1},{1,0},{2,3},{3,2},{4,5},{5,4},{6,7},{7,6},{8,9},{9,8},{10,11... | collective-permute-start | bytes 49160 | tf_op jit(solution)/shard_map/ppermute | solution.py:391
  1.2 2.4 %collective-permute-start.1 = (f32[2,4,512]{2,1,0:T(4,128)S(1)}, f32[2,4,512]{2,1,0:T(4,128)S(1)}, u32[]{:S(2)}, u32[]{:S(2)}) collective-permute-start(f32[2,4,512]{2,1,0:T(4,128)S(1)} %get-tuple-element.34), channel_id=1, source_target_pairs={{1,2},{2,1},{3,4},{4,3},{5,6},{6,5},{7,8},{8,7},{9,10},{10,9},{11,... | collective-permute-start | bytes 49160 | tf_op jit(solution)/shard_map/ppermute | solution.py:390
  1.9 0.7 %copy-start = (f32[2,2]{1,0:T(2,128)S(1)}, f32[2,2]{1,0:T(2,128)}, u32[]{:S(2)}) copy-start(f32[2,2]{1,0:T(2,128)} %cxh.1) | copy-start | bytes 52
  1.9 0.7 %copy-start.1 = (f32[2]{0:T(128)S(1)}, f32[2]{0:T(128)}, u32[]{:S(2)}) copy-start(f32[2]{0:T(128)} %cph.1) | copy-start | bytes 28
  4.0 5.8 %collective-permute-start.4 = (f32[8,128]{1,0:T(8,128)S(1)}, f32[8,128]{1,0:T(8,128)S(1)}, u32[]{:S(2)}, u32[]{:S(2)}) collective-permute-start(f32[8,128]{1,0:T(8,128)S(1)} %get-tuple-element.38.m0), channel_id=1, source_target_pairs={{0,96},{32,64},{64,32},{96,0},{1,97},{33,65},{65,33},{97,1},{2,98}... | collective-permute-start | bytes 12296 | tf_op jit(solution)/shard_map/ppermute | solution.py:373
  8.2 5.1 %collective-permute-start.3 = (f32[8,128]{1,0:T(8,128)S(1)}, f32[8,128]{1,0:T(8,128)S(1)}, u32[]{:S(2)}, u32[]{:S(2)}) collective-permute-start(f32[8,128]{1,0:T(8,128)S(1)} %get-tuple-element.38.m0), channel_id=1, source_target_pairs={{0,64},{32,96},{64,0},{96,32},{1,65},{33,97},{65,1},{97,33},{2,66}... | collective-permute-start | bytes 12296 | tf_op jit(solution)/shard_map/ppermute | solution.py:373
  8.2 5.1 %collective-permute-start.2 = (f32[8,128]{1,0:T(8,128)S(1)}, f32[8,128]{1,0:T(8,128)S(1)}, u32[]{:S(2)}, u32[]{:S(2)}) collective-permute-start(f32[8,128]{1,0:T(8,128)S(1)} %get-tuple-element.38.m0), channel_id=1, source_target_pairs={{0,32},{32,0},{64,96},{96,64},{1,33},{33,1},{65,97},{97,65},{2,34}... | collective-permute-start | bytes 12296 | tf_op jit(solution)/shard_map/ppermute | solution.py:373
  13.7 2.7 %collective-permute-start.5 = (f32[5,4,512]{2,1,0:T(4,128)S(1)}, f32[5,4,512]{2,1,0:T(4,128)S(1)}, u32[]{:S(2)}, u32[]{:S(2)}) collective-permute-start(f32[5,4,512]{2,1,0:T(4,128)S(1)} %get-tuple-element.47.own), channel_id=1, source_target_pairs={{0,1},{1,0},{2,3},{3,2},{4,5},{5,4},{6,7},{7,6},{8,9},{9,8},{10,11... | collective-permute-start | bytes 122888 | tf_op jit(solution)/shard_map/ppermute | solution.py:413
  16.4 7.3 %collective-permute-start.8 = (f32[5,4,512]{2,1,0:T(4,128)S(1)}, f32[5,4,512]{2,1,0:T(4,128)S(1)}, u32[]{:S(2)}, u32[]{:S(2)}) collective-permute-start(f32[5,4,512]{2,1,0:T(4,128)S(1)} %shard_map.60.m0.c0), channel_id=1, source_target_pairs={{0,6},{1,7},{2,4},{3,5},{4,2},{5,3},{6,0},{7,1},{8,14},{9,15},{10,... | collective-permute-start | bytes 122888 | tf_op jit(solution)/shard_map/ppermute | solution.py:373
  21.6 5.5 %collective-permute-start.7 = (f32[5,4,512]{2,1,0:T(4,128)S(1)}, f32[5,4,512]{2,1,0:T(4,128)S(1)}, u32[]{:S(2)}, u32[]{:S(2)}) collective-permute-start(f32[5,4,512]{2,1,0:T(4,128)S(1)} %shard_map.60.m0.c0), channel_id=1, source_target_pairs={{0,4},{1,5},{2,6},{3,7},{4,0},{5,1},{6,2},{7,3},{8,12},{9,13},{10,... | collective-permute-start | bytes 122888 | tf_op jit(solution)/shard_map/ppermute | solution.py:373
  21.6 5.5 %collective-permute-start.6 = (f32[5,4,512]{2,1,0:T(4,128)S(1)}, f32[5,4,512]{2,1,0:T(4,128)S(1)}, u32[]{:S(2)}, u32[]{:S(2)}) collective-permute-start(f32[5,4,512]{2,1,0:T(4,128)S(1)} %shard_map.60.m0.c0), channel_id=1, source_target_pairs={{0,2},{1,3},{2,0},{3,1},{4,6},{5,7},{6,4},{7,5},{8,10},{9,11},{10,... | collective-permute-start | bytes 122888 | tf_op jit(solution)/shard_map/ppermute | solution.py:373
  27.2 5.7 %collective-permute-start.11 = (f32[5,4,512]{2,1,0:T(4,128)S(1)}, f32[5,4,512]{2,1,0:T(4,128)S(1)}, u32[]{:S(2)}, u32[]{:S(2)}) collective-permute-start(f32[5,4,512]{2,1,0:T(4,128)S(1)} %shard_map.61.p0), channel_id=1, source_target_pairs={{0,24},{1,25},{2,26},{3,27},{4,28},{5,29},{6,30},{7,31},{8,16},{9,... | collective-permute-start | bytes 122888 | tf_op jit(solution)/shard_map/ppermute | solution.py:373
  29.3 5.5 %collective-permute-start.10 = (f32[5,4,512]{2,1,0:T(4,128)S(1)}, f32[5,4,512]{2,1,0:T(4,128)S(1)}, u32[]{:S(2)}, u32[]{:S(2)}) collective-permute-start(f32[5,4,512]{2,1,0:T(4,128)S(1)} %shard_map.61.p0), channel_id=1, source_target_pairs={{0,16},{1,17},{2,18},{3,19},{4,20},{5,21},{6,22},{7,23},{8,24},{9,... | collective-permute-start | bytes 122888 | tf_op jit(solution)/shard_map/ppermute | solution.py:373
  30.8 4.0 %collective-permute-start.9 = (f32[5,4,512]{2,1,0:T(4,128)S(1)}, f32[5,4,512]{2,1,0:T(4,128)S(1)}, u32[]{:S(2)}, u32[]{:S(2)}) collective-permute-start(f32[5,4,512]{2,1,0:T(4,128)S(1)} %shard_map.61.p0), channel_id=1, source_target_pairs={{0,8},{1,9},{2,10},{3,11},{4,12},{5,13},{6,14},{7,15},{8,0},{9,1},... | collective-permute-start | bytes 122888 | tf_op jit(solution)/shard_map/ppermute | solution.py:373

commit v2 on v1

--- a/solution.py
+++ b/solution.py
@@ -40,11 +40,8 @@
 
 
 def factor_kernel(
-    cxh, cph, u, ky, kz, gpy, gsy, ymat, gpz, gsz, zmat, r0, kt, zr, wa, wb, wc, wd, zz, cx, cp, sem
+    cx, cp, u, ky, kz, gpy, gsy, ymat, gpz, gsz, zmat, r0, kt, zr, wa, wb, wc, wd, zz
 ):
-    small = [pltpu.make_async_copy(cxh, cx, sem.at[0]), pltpu.make_async_copy(cph, cp, sem.at[1])]
-    for copy in small:
-        copy.start()
     lines, length = ky.shape
     steps = length // SUB
     planes, depth = zmat.shape[1], lines // zmat.shape[1]
@@ -122,23 +119,21 @@
         for p in range(planes):
             gsz[pl.ds(p * depth + t, 1), :] = g[p : p + 1, :]
     zmat[0] = ws[depth - 1] * ij
-    for copy in small:
-        copy.wait()
     for f in range(2):
         for x in range(2):
             at = (f * 2 + x) * depth
             me = u[at : at + depth, :]
             beside = u[(f * 2 + 1 - x) * depth : (f * 2 + 2 - x) * depth, :]
             other = u[((1 - f) * 2 + x) * depth : ((1 - f) * 2 + x + 1) * depth, :]
-            face = 0.5 * (cx[f, 0] + cx[f, 1])
+            face = 0.5 * (cx[f : f + 1, 0:1] + cx[f : f + 1, 1:2])
             k = kz[at : at + depth, :]
             flux = 0.5 * (k[1:] + k[:-1]) * (me[1:] - me[:-1])
             none = jnp.zeros((1, length), F32)
             flow = jnp.concatenate([flux, none], 0) - jnp.concatenate([none, flux], 0)
             r0[at : at + depth, :] = (
-                (2.0 - 0.5 * cx[f, x]) * me
+                (2.0 - 0.5 * cx[f : f + 1, x : x + 1]) * me
                 + face * (beside - me)
-                + cp[x] * (other - me)
+                + cp[:, x : x + 1] * (other - me)
                 + flow
             )
 
@@ -370,8 +365,18 @@
 
 def partners(value, axis, count, unit):
     return [
-        lax.ppermute(value, axis, [(i, i ^ (k * unit)) for i in range(count)]) for k in (1, 2, 3)
+        lax.ppermute(value, axis, [(i, i ^ (k * unit) ^ (unit > 1)) for i in range(count)]) for k in (1, 2, 3)
     ]
+
+
+def chip_neighbours(rows, peers):
+    pairs = []
+    for y in range(rows):
+        for z in range(peers):
+            end = z in (0, peers - 1)
+            to = ((y ^ 1) * peers + z) if end else (y * peers + (z + 1 if z % 2 else z - 1))
+            pairs.append((y * peers + z, to))
+    return pairs
 
 
 def shards(fields, cond_x, cond_y, cond_z, coupling):
@@ -386,16 +391,15 @@
         load_kernel, [flat] * 3 + [(2, *face)] * 4, [dma((3,))], 100_000, [hbm] * 3,
         fields.reshape(flat), cond_y.reshape(flat), cond_z.reshape(flat), vmem=53,
     )
-    across = [pair for i in range(1, peers - 1, 2) for pair in ((i, i + 1), (i + 1, i))]
-    outer = lax.ppermute(outer, "gz", across)
     inner = lax.ppermute(inner, "gz", [(i, i ^ 1) for i in range(peers)])
+    outer = lax.ppermute(outer, ("gy", "gz"), chip_neighbours(lax.axis_size("gy"), peers))
     gpy, gsy, ymat, gpz, gsz, zmat, r0 = call(
         factor_kernel,
         [tall, tall, (8, lines), flat, flat, (3, *face), flat],
-        [(ny, lines)] + [tall] * 5 + [(nz, *face), pltpu.SMEM(cond_x.shape, F32), pltpu.SMEM(coupling.shape, F32), dma((2,))],
+        [(ny, lines)] + [tall] * 5 + [(nz, *face)],
         4_000_000,
-        [hbm, hbm, VMEM, VMEM, VMEM],
-        cond_x, coupling, u, ky, kz,
+        [VMEM] * 5,
+        cond_x, coupling[None], u, ky, kz,
     )
     msg, rt, ss, qq = call(
         functools.partial(y_ends_kernel, peers), [(8, lines), (ny, lines), tall, tall], [], 1_000_000, [VMEM] * 8,

time: 35.8 us -> 34.1 us (0.953)
  the two profiles are of different devices: /device:TPU:0 before, /device:TPU:1 now
where the time goes in v2:
time: 34.1 us; the launch traced here: 33.9 us
  starting transfers between devices  17 us (50%)
  waiting for transfers between devices  12.1 us (35%)
  Pallas kernels  4.13 us (12%)
  local copies, waits for them, and re-layouts  0.68 us (2%)
    ppermute x9, starting transfers between devices, partners(): lax.ppermute(value, axis, [(i, i ^ k * unit ^ (unit > 1)) for i in range(...  12.2 us
    ppermute x9, waiting for transfers between devices, partners(): lax.ppermute(value, axis, [(i, i ^ k * unit ^ (unit > 1)) for i in range(...  10.8 us
    pallas_call x9, Pallas kernels, call(): pl.pallas_call(kernel, out_shape=[jax.ShapeDtypeStruct(s, F32) for s in o...  4.13 us
    ppermute x1, starting transfers between devices, shards(): peer = lax.ppermute(own, 'gz', [(i, i ^ 1) for i in range(peers)])  1.9 us
    ppermute x1, starting transfers between devices, shards(): inner = lax.ppermute(inner, 'gz', [(i, i ^ 1) for i in range(peers)])  1.5 us
    ppermute x1, starting transfers between devices, shards(): lax.ppermute(outer, ('gy', 'gz'), chip_neighbours(lax.axis_size('gy'), pe...  1.36 us
    ppermute x1, waiting for transfers between devices, shards(): peer = lax.ppermute(own, 'gz', [(i, i ^ 1) for i in range(peers)])  0.87 us
  transfers between devices with their start and end apart: 12, of which 8 were waited for; matrix products, arithmetic and copies ran while one was open for 0% of the time, Pallas kernels for 4%

profile of v2, /device:TPU:1, one launch (start us, length us, event | category | flops | bytes accessed | tf_op | source)
XLA Modules:
  0.0 33.9 jit_solution(7975191263613328613)
XLA Ops:
  0.0 1.1 %shard_map.55 = (f32[128,512]{1,0:T(8,128)S(1)}, f32[128,512]{1,0:T(8,128)S(1)}, f32[128,512]{1,0:T(8,128)S(1)}, f32[2,4,512]{2,1,0:T(4,128)S(1)}, f32[2,4,512]{...) custom-call(f32[128,512]{1,0:T(8,128)} %bitcast.6, f32[128,512]{1,0:T(8,128)} %bitcast.7, ...), custom_call_target="tpu_custom_call" | custom-call | flops 100000 | bytes 25000 | tf_op jit(solution)/shard_map/pallas_call | solution.py:262
  1.1 1.5 %collective-permute-start = (f32[2,4,512]{2,1,0:T(4,128)S(1)}, f32[2,4,512]{2,1,0:T(4,128)S(1)}, u32[]{:S(2)}, u32[]{:S(2)}) collective-permute-start(f32[2,4,512]{2,1,0:T(4,128)S(1)} %get-tuple-element.33), channel_id=1, source_target_pairs={{0,1},{1,0},{2,3},{3,2},{4,5},{5,4},{6,7},{7,6},{8,9},{9,8},{10,11... | collective-permute-start | bytes 49160 | tf_op jit(solution)/shard_map/ppermute | solution.py:394
  2.6 1.4 %collective-permute-start.1 = (f32[2,4,512]{2,1,0:T(4,128)S(1)}, f32[2,4,512]{2,1,0:T(4,128)S(1)}, u32[]{:S(2)}, u32[]{:S(2)}) collective-permute-start(f32[2,4,512]{2,1,0:T(4,128)S(1)} %get-tuple-element.34), channel_id=1, source_target_pairs={{0,32},{1,2},{2,1},{3,4},{4,3},{5,6},{6,5},{7,8},{8,7},{9,10},{10,... | collective-permute-start | bytes 49160 | tf_op jit(solution)/shard_map/ppermute | solution.py:395
  4.0 0.0 copy-start
  4.0 0.0 copy-start.1
  4.0 0.7 %copy-done = f32[2,2]{1,0:T(2,128)S(1)} copy-done((f32[2,2]{1,0:T(2,128)S(1)}, f32[2,2]{1,0:T(2,128)}, u32[]{:S(2)}) %copy-start) | copy-done | bytes 40
  4.7 0.0 copy-done.1
  4.7 1.0 %shard_map.56 = (f32[64,8,128]{2,1,0:T(8,128)S(1)}, f32[64,8,128]{2,1,0:T(8,128)S(1)}, f32[8,128]{1,0:T(8,128)S(1)}, f32[128,512]{1,0:T(8,128)S(1)}, f32[128,512...) custom-call(f32[2,2]{1,0:T(2,128)S(1)} %copy-done, f32[1,2]{1,0:T(1,128)S(1)} %bitcast.5, ...), custom_call_target="tpu_custom_call" | custom-call | flops 4000000 | bytes 1000000 | tf_op jit(solution)/shard_map/pallas_call | solution.py:262
  5.6 0.0 collective-permute-done.inner
  5.7 0.4 %collective-permute-done.1.outer = f32[2,4,512]{2,1,0:T(4,128)S(1)} collective-permute-done((f32[2,4,512]{2,1,0:T(4,128)S(1)}, f32[2,4,512]{2,1,0:T(4,128)S(1)}, u32[]{:S(2)}, u32[]{:S(2)}) %collective-permute-start.1) | collective-permute-done | bytes 16416 | tf_op jit(solution)/shard_map/ppermute | solution.py:395
  6.1 0.4 %shard_map.57 = (f32[8,128]{1,0:T(8,128)S(1)}, f32[512,128]{1,0:T(8,128)S(1)}, f32[64,8,128]{2,1,0:T(8,128)S(1)}, f32[64,8,128]{2,1,0:T(8,128)S(1)}) custom-call(f32[128,512]{1,0:T(8,128)S(1)} %get-tuple-element.30.r0, f32[2,4,512]{2,1,0:T(4,128)S(1)} %get-tuple-element.31.low, f32[2,4,512]{2,1,0:T(4,128)S(1)} %get-tuple-element.32.high, ...), custom_call_target="tpu_custom_call" | custom-call | flops 1000000 | bytes 250000 | tf_op jit(solution)/shard_map/pallas_call | solution.py:262
  6.5 3.9 %collective-permute-start.4 = (f32[8,128]{1,0:T(8,128)S(1)}, f32[8,128]{1,0:T(8,128)S(1)}, u32[]{:S(2)}, u32[]{:S(2)}) collective-permute-start(f32[8,128]{1,0:T(8,128)S(1)} %get-tuple-element.38.m0), channel_id=1, source_target_pairs={{0,96},{32,64},{64,32},{96,0},{1,97},{33,65},{65,33},{97,1},{2,98}... | collective-permute-start | bytes 12296 | tf_op jit(solution)/shard_map/ppermute | solution.py:368
  10.4 0.0 collective-permute-start.3
  10.4 0.7 %collective-permute-start.2 = (f32[8,128]{1,0:T(8,128)S(1)}, f32[8,128]{1,0:T(8,128)S(1)}, u32[]{:S(2)}, u32[]{:S(2)}) collective-permute-start(f32[8,128]{1,0:T(8,128)S(1)} %get-tuple-element.38.m0), channel_id=1, source_target_pairs={{0,32},{32,0},{64,96},{96,64},{1,33},{33,1},{65,97},{97,65},{2,34}... | collective-permute-start | bytes 12296 | tf_op jit(solution)/shard_map/ppermute | solution.py:368
  11.1 0.1 shard_map.58
  11.2 0.2 collective-permute-done.4.m3
  11.4 3.0 %collective-permute-done.3.m2 = f32[8,128]{1,0:T(8,128)S(1)} collective-permute-done((f32[8,128]{1,0:T(8,128)S(1)}, f32[8,128]{1,0:T(8,128)S(1)}, u32[]{:S(2)}, u32[]{:S(2)}) %collective-permute-start.3) | collective-permute-done | bytes 4128 | tf_op jit(solution)/shard_map/ppermute | solution.py:368
  14.3 0.0 collective-permute-done.2.m1
  14.3 0.4 %shard_map.59 = (f32[128,512]{1,0:T(8,128)S(1)}, f32[5,4,512]{2,1,0:T(4,128)S(1)}) custom-call(f32[8,128]{1,0:T(8,128)S(1)} %get-tuple-element.38.m0, f32[8,128]{1,0:T(8,128)S(1)} %collective-permute-done.2.m1, f32[8,128]{1,0:T(8,128)S(1)} %collective-permute-done.3.m2, f32[8,128]{1,0:T(8,128)S(1)} %collective-permute-done.4.m3, ...), custom_call_target="tpu_custom_call" | custom-call | flops 1000000 | bytes 250000 | tf_op jit(solution)/shard_map/pallas_call | solution.py:262
  14.7 1.9 %collective-permute-start.5 = (f32[5,4,512]{2,1,0:T(4,128)S(1)}, f32[5,4,512]{2,1,0:T(4,128)S(1)}, u32[]{:S(2)}, u32[]{:S(2)}) collective-permute-start(f32[5,4,512]{2,1,0:T(4,128)S(1)} %get-tuple-element.47.own), channel_id=1, source_target_pairs={{0,1},{1,0},{2,3},{3,2},{4,5},{5,4},{6,7},{7,6},{8,9},{9,8},{10,11... | collective-permute-start | bytes 122888 | tf_op jit(solution)/shard_map/ppermute | solution.py:417
  16.7 0.9 %collective-permute-done.5.peer = f32[5,4,512]{2,1,0:T(4,128)S(1)} collective-permute-done((f32[5,4,512]{2,1,0:T(4,128)S(1)}, f32[5,4,512]{2,1,0:T(4,128)S(1)}, u32[]{:S(2)}, u32[]{:S(2)}) %collective-permute-start.5) | collective-permute-done | bytes 40992 | tf_op jit(solution)/shard_map/ppermute | solution.py:417
  17.5 3.2 %collective-permute-start.8 = (f32[5,4,512]{2,1,0:T(4,128)S(1)}, f32[5,4,512]{2,1,0:T(4,128)S(1)}, u32[]{:S(2)}, u32[]{:S(2)}) collective-permute-start(f32[5,4,512]{2,1,0:T(4,128)S(1)} %shard_map.60.m0.c0), channel_id=1, source_target_pairs={{0,7},{1,6},{2,5},{3,4},{4,3},{5,2},{6,1},{7,0},{8,15},{9,14},{10,... | collective-permute-start | bytes 122888 | tf_op jit(solution)/shard_map/ppermute | solution.py:368
  20.8 0.0 collective-permute-start.7
  20.8 0.9 %collective-permute-start.6 = (f32[5,4,512]{2,1,0:T(4,128)S(1)}, f32[5,4,512]{2,1,0:T(4,128)S(1)}, u32[]{:S(2)}, u32[]{:S(2)}) collective-permute-start(f32[5,4,512]{2,1,0:T(4,128)S(1)} %shard_map.60.m0.c0), channel_id=1, source_target_pairs={{0,3},{1,2},{2,1},{3,0},{4,7},{5,6},{6,5},{7,4},{8,11},{9,10},{10,... | collective-permute-start | bytes 122888 | tf_op jit(solution)/shard_map/ppermute | solution.py:368
  21.7 0.9 %collective-permute-done.8.m3.c3 = f32[5,4,512]{2,1,0:T(4,128)S(1)} collective-permute-done((f32[5,4,512]{2,1,0:T(4,128)S(1)}, f32[5,4,512]{2,1,0:T(4,128)S(1)}, u32[]{:S(2)}, u32[]{:S(2)}) %collective-permute-start.8) | collective-permute-done | bytes 40992 | tf_op jit(solution)/shard_map/ppermute | solution.py:368
  22.5 3.6 %collective-permute-done.7.m2.c2 = f32[5,4,512]{2,1,0:T(4,128)S(1)} collective-permute-done((f32[5,4,512]{2,1,0:T(4,128)S(1)}, f32[5,4,512]{2,1,0:T(4,128)S(1)}, u32[]{:S(2)}, u32[]{:S(2)}) %collective-permute-start.7) | collective-permute-done | bytes 40992 | tf_op jit(solution)/shard_map/ppermute | solution.py:368
  26.1 0.0 collective-permute-done.6.m1.c1
  26.2 1.9 %collective-permute-start.11 = (f32[5,4,512]{2,1,0:T(4,128)S(1)}, f32[5,4,512]{2,1,0:T(4,128)S(1)}, u32[]{:S(2)}, u32[]{:S(2)}) collective-permute-start(f32[5,4,512]{2,1,0:T(4,128)S(1)} %shard_map.61.p0), channel_id=1, source_target_pairs={{0,25},{1,24},{2,27},{3,26},{4,29},{5,28},{6,31},{7,30},{8,17},{9,... | collective-permute-start | bytes 122888 | tf_op jit(solution)/shard_map/ppermute | solution.py:368
  28.1 1.4 %collective-permute-start.10 = (f32[5,4,512]{2,1,0:T(4,128)S(1)}, f32[5,4,512]{2,1,0:T(4,128)S(1)}, u32[]{:S(2)}, u32[]{:S(2)}) collective-permute-start(f32[5,4,512]{2,1,0:T(4,128)S(1)} %shard_map.61.p0), channel_id=1, source_target_pairs={{0,17},{1,16},{2,19},{3,18},{4,21},{5,20},{6,23},{7,22},{8,25},{9,... | collective-permute-start | bytes 122888 | tf_op jit(solution)/shard_map/ppermute | solution.py:368
  29.6 0.1 collective-permute-start.9
  29.7 0.2 shard_map.62.local
  29.9 1.0 %collective-permute-done.11.p3 = f32[5,4,512]{2,1,0:T(4,128)S(1)} collective-permute-done((f32[5,4,512]{2,1,0:T(4,128)S(1)}, f32[5,4,512]{2,1,0:T(4,128)S(1)}, u32[]{:S(2)}, u32[]{:S(2)}) %collective-permute-start.11) | collective-permute-done | bytes 40992 | tf_op jit(solution)/shard_map/ppermute | solution.py:368
  30.9 2.2 %collective-permute-done.10.p2 = f32[5,4,512]{2,1,0:T(4,128)S(1)} collective-permute-done((f32[5,4,512]{2,1,0:T(4,128)S(1)}, f32[5,4,512]{2,1,0:T(4,128)S(1)}, u32[]{:S(2)}, u32[]{:S(2)}) %collective-permute-start.10) | collective-permute-done | bytes 40992 | tf_op jit(solution)/shard_map/ppermute | solution.py:368
  33.1 0.0 collective-permute-done.9.p1
  33.1 0.9 %shard_map.63 = f32[128,512]{1,0:T(8,128)} custom-call(f32[5,4,512]{2,1,0:T(4,128)S(1)} %get-tuple-element.47.own, f32[5,4,512]{2,1,0:T(4,128)S(1)} %collective-permute-done.5.peer, f32[5,4,512]{2,1,0:T(4,128)S(1)} %shard_map.60.m0.c0, f32[5,4,512]{2,1,0:T(4,128)S(1)} %collective-permute-done.6.m1.c1, f32[5,4,512]{2,1,0:T(4,128)S(1)} %collective-permute-done.7.m2.c2, ...), custom_call_target="tpu_custom_call" | custom-call | flops 1000000 | bytes 250000 | tf_op jit(solution)/shard_map/pallas_call | solution.py:262
  (2 shorter events, 0.1 us)
Async XLA Ops:
  1.1 4.5 %collective-permute-start = (f32[2,4,512]{2,1,0:T(4,128)S(1)}, f32[2,4,512]{2,1,0:T(4,128)S(1)}, u32[]{:S(2)}, u32[]{:S(2)}) collective-permute-start(f32[2,4,512]{2,1,0:T(4,128)S(1)} %get-tuple-element.33), channel_id=1, source_target_pairs={{0,1},{1,0},{2,3},{3,2},{4,5},{5,4},{6,7},{7,6},{8,9},{9,8},{10,11... | collective-permute-start | bytes 49160 | tf_op jit(solution)/shard_map/ppermute | solution.py:394
  2.6 3.4 %collective-permute-start.1 = (f32[2,4,512]{2,1,0:T(4,128)S(1)}, f32[2,4,512]{2,1,0:T(4,128)S(1)}, u32[]{:S(2)}, u32[]{:S(2)}) collective-permute-start(f32[2,4,512]{2,1,0:T(4,128)S(1)} %get-tuple-element.34), channel_id=1, source_target_pairs={{0,32},{1,2},{2,1},{3,4},{4,3},{5,6},{6,5},{7,8},{8,7},{9,10},{10,... | collective-permute-start | bytes 49160 | tf_op jit(solution)/shard_map/ppermute | solution.py:395
  4.0 0.7 %copy-start = (f32[2,2]{1,0:T(2,128)S(1)}, f32[2,2]{1,0:T(2,128)}, u32[]{:S(2)}) copy-start(f32[2,2]{1,0:T(2,128)} %cx.1) | copy-start | bytes 52
  4.0 0.7 %copy-start.1 = (f32[2]{0:T(128)S(1)}, f32[2]{0:T(128)}, u32[]{:S(2)}) copy-start(f32[2]{0:T(128)} %param.9) | copy-start | bytes 28
  6.5 4.9 %collective-permute-start.4 = (f32[8,128]{1,0:T(8,128)S(1)}, f32[8,128]{1,0:T(8,128)S(1)}, u32[]{:S(2)}, u32[]{:S(2)}) collective-permute-start(f32[8,128]{1,0:T(8,128)S(1)} %get-tuple-element.38.m0), channel_id=1, source_target_pairs={{0,96},{32,64},{64,32},{96,0},{1,97},{33,65},{65,33},{97,1},{2,98}... | collective-permute-start | bytes 12296 | tf_op jit(solution)/shard_map/ppermute | solution.py:368
  10.4 4.0 %collective-permute-start.3 = (f32[8,128]{1,0:T(8,128)S(1)}, f32[8,128]{1,0:T(8,128)S(1)}, u32[]{:S(2)}, u32[]{:S(2)}) collective-permute-start(f32[8,128]{1,0:T(8,128)S(1)} %get-tuple-element.38.m0), channel_id=1, source_target_pairs={{0,64},{32,96},{64,0},{96,32},{1,65},{33,97},{65,1},{97,33},{2,66}... | collective-permute-start | bytes 12296 | tf_op jit(solution)/shard_map/ppermute | solution.py:368
  10.4 4.0 %collective-permute-start.2 = (f32[8,128]{1,0:T(8,128)S(1)}, f32[8,128]{1,0:T(8,128)S(1)}, u32[]{:S(2)}, u32[]{:S(2)}) collective-permute-start(f32[8,128]{1,0:T(8,128)S(1)} %get-tuple-element.38.m0), channel_id=1, source_target_pairs={{0,32},{32,0},{64,96},{96,64},{1,33},{33,1},{65,97},{97,65},{2,34}... | collective-permute-start | bytes 12296 | tf_op jit(solution)/shard_map/ppermute | solution.py:368
  14.7 2.8 %collective-permute-start.5 = (f32[5,4,512]{2,1,0:T(4,128)S(1)}, f32[5,4,512]{2,1,0:T(4,128)S(1)}, u32[]{:S(2)}, u32[]{:S(2)}) collective-permute-start(f32[5,4,512]{2,1,0:T(4,128)S(1)} %get-tuple-element.47.own), channel_id=1, source_target_pairs={{0,1},{1,0},{2,3},{3,2},{4,5},{5,4},{6,7},{7,6},{8,9},{9,8},{10,11... | collective-permute-start | bytes 122888 | tf_op jit(solution)/shard_map/ppermute | solution.py:417
  17.5 5.0 %collective-permute-start.8 = (f32[5,4,512]{2,1,0:T(4,128)S(1)}, f32[5,4,512]{2,1,0:T(4,128)S(1)}, u32[]{:S(2)}, u32[]{:S(2)}) collective-permute-start(f32[5,4,512]{2,1,0:T(4,128)S(1)} %shard_map.60.m0.c0), channel_id=1, source_target_pairs={{0,7},{1,6},{2,5},{3,4},{4,3},{5,2},{6,1},{7,0},{8,15},{9,14},{10,... | collective-permute-start | bytes 122888 | tf_op jit(solution)/shard_map/ppermute | solution.py:368
  20.8 5.4 %collective-permute-start.7 = (f32[5,4,512]{2,1,0:T(4,128)S(1)}, f32[5,4,512]{2,1,0:T(4,128)S(1)}, u32[]{:S(2)}, u32[]{:S(2)}) collective-permute-start(f32[5,4,512]{2,1,0:T(4,128)S(1)} %shard_map.60.m0.c0), channel_id=1, source_target_pairs={{0,5},{1,4},{2,7},{3,6},{4,1},{5,0},{6,3},{7,2},{8,13},{9,12},{10,... | collective-permute-start | bytes 122888 | tf_op jit(solution)/shard_map/ppermute | solution.py:368
  20.8 5.4 %collective-permute-start.6 = (f32[5,4,512]{2,1,0:T(4,128)S(1)}, f32[5,4,512]{2,1,0:T(4,128)S(1)}, u32[]{:S(2)}, u32[]{:S(2)}) collective-permute-start(f32[5,4,512]{2,1,0:T(4,128)S(1)} %shard_map.60.m0.c0), channel_id=1, source_target_pairs={{0,3},{1,2},{2,1},{3,0},{4,7},{5,6},{6,5},{7,4},{8,11},{9,10},{10,... | collective-permute-start | bytes 122888 | tf_op jit(solution)/shard_map/ppermute | solution.py:368
  26.2 4.7 %collective-permute-start.11 = (f32[5,4,512]{2,1,0:T(4,128)S(1)}, f32[5,4,512]{2,1,0:T(4,128)S(1)}, u32[]{:S(2)}, u32[]{:S(2)}) collective-permute-start(f32[5,4,512]{2,1,0:T(4,128)S(1)} %shard_map.61.p0), channel_id=1, source_target_pairs={{0,25},{1,24},{2,27},{3,26},{4,29},{5,28},{6,31},{7,30},{8,17},{9,... | collective-permute-start | bytes 122888 | tf_op jit(solution)/shard_map/ppermute | solution.py:368
  28.1 5.0 %collective-permute-start.10 = (f32[5,4,512]{2,1,0:T(4,128)S(1)}, f32[5,4,512]{2,1,0:T(4,128)S(1)}, u32[]{:S(2)}, u32[]{:S(2)}) collective-permute-start(f32[5,4,512]{2,1,0:T(4,128)S(1)} %shard_map.61.p0), channel_id=1, source_target_pairs={{0,17},{1,16},{2,19},{3,18},{4,21},{5,20},{6,23},{7,22},{8,25},{9,... | collective-permute-start | bytes 122888 | tf_op jit(solution)/shard_map/ppermute | solution.py:368
  29.6 3.5 %collective-permute-start.9 = (f32[5,4,512]{2,1,0:T(4,128)S(1)}, f32[5,4,512]{2,1,0:T(4,128)S(1)}, u32[]{:S(2)}, u32[]{:S(2)}) collective-permute-start(f32[5,4,512]{2,1,0:T(4,128)S(1)} %shard_map.61.p0), channel_id=1, source_target_pairs={{0,9},{1,8},{2,11},{3,10},{4,13},{5,12},{6,15},{7,14},{8,1},{9,0},... | collective-permute-start | bytes 122888 | tf_op jit(solution)/shard_map/ppermute | solution.py:368

commit v3 on v2

--- a/solution.py
+++ b/solution.py
@@ -240,7 +240,8 @@
         own[i + 2] = zends[i]
 
 
-def z_local_kernel(u, rz, gpz, gsz, zmat, out):
+def z_local_kernel(u, rz, gpz, gsz, zmat, out, ready):
+    ready[...] = jnp.zeros_like(ready)
     _, planes, length = zmat.shape
     depth = rz.shape[0] // planes
     for p in range(planes):
@@ -302,7 +303,7 @@
         ref[i] = value[i]
 
 
-def core_kernel(own, peer, chip):
+def core_kernel(own, peer, ready, chip):
     lower = lax.axis_index("gz") % 2 == 0
     mine, theirs = parts_of(own), parts_of(peer)
     put(chip, join(choose(lower, mine, theirs), choose(lower, theirs, mine)))
@@ -364,9 +365,16 @@
 
 
 def partners(value, axis, count, unit):
-    return [
-        lax.ppermute(value, axis, [(i, i ^ (k * unit) ^ (unit > 1)) for i in range(count)]) for k in (1, 2, 3)
-    ]
+    got = {
+        k: lax.ppermute(value, axis, [(i, i ^ (k * unit) ^ (unit > 1)) for i in range(count)])
+        for k in (1, 2, 3)
+    }
+    got[2] = got[2] * unity()
+    return [got[k] for k in (1, 2, 3)]
+
+
+def unity():
+    return jnp.where(lax.axis_index("gz") < lax.axis_size("gz"), 1.0, 0.0)
 
 
 def chip_neighbours(rows, peers):
@@ -401,6 +409,7 @@
         [VMEM] * 5,
         cond_x, coupling[None], u, ky, kz,
     )
+    outer = outer * unity()
     msg, rt, ss, qq = call(
         functools.partial(y_ends_kernel, peers), [(8, lines), (ny, lines), tall, tall], [], 1_000_000, [VMEM] * 8,
         r0, low, high, inner, outer, gpy, gsy, ymat,
@@ -415,8 +424,8 @@
         msg, *others, vloc, gpy, gsy, u, gpz, gsz, zends,
     )
     peer = lax.ppermute(own, "gz", [(i, i ^ 1) for i in range(peers)])
-    [local] = call(z_local_kernel, [flat], [], 1_000_000, [VMEM] * 5, u, rz, gpz, gsz, zmat)
-    [chip] = call(core_kernel, [ends], [], 50_000, [VMEM] * 2, own, peer)
+    local, ready = call(z_local_kernel, [flat, (8, 128)], [], 1_000_000, [VMEM] * 5, u, rz, gpz, gsz, zmat)
+    [chip] = call(core_kernel, [ends], [], 50_000, [VMEM] * 3, own, peer, ready)
     column = [chip] + partners(chip, "gz", peers, 2)
     [plane] = call(
         functools.partial(ring_kernel, position_y), [ends], [(4, *ends)], 50_000,

time: 34.1 us -> 33.4 us (0.979)
  waiting for transfers between devices: 12.1 us -> 11.3 us
    ppermute x1, starting transfers between devices: 1.36 us -> 2.77 us  [shards(): lax.ppermute(outer, ('gy', 'gz'), chip_neighbours(lax.axis_size('gy'), pe...]
    ppermute x1, starting transfers between devices: 1.5 us -> 0.74 us  [shards(): inner = lax.ppermute(inner, 'gz', [(i, i ^ 1) for i in range(peers)])]
    ppermute x9, starting transfers between devices: 12.2 us -> 11.6 us  [partners(): lax.ppermute(value, axis, [(i, i ^ k * unit ^ (unit > 1)) for i in range(...]
    ppermute x1, waiting for transfers between devices: 0.42 us -> 0.01 us  [shards(): lax.ppermute(outer, ('gy', 'gz'), chip_neighbours(lax.axis_size('gy'), pe...]
  transfers between devices with their start and end apart: 12 -> 12, of which waited for: 8 -> 7; matrix products, arithmetic and copies ran while one was open for 0% -> 0% of each run, Pallas kernels for 4% -> 4%
where the time goes in v3:
time: 33.4 us; the launch traced here: 33.3 us
  starting transfers between devices  17.1 us (51%)
  waiting for transfers between devices  11.3 us (34%)
  Pallas kernels  4.14 us (12%)
  local copies, waits for them, and re-layouts  0.68 us (2%)
    ppermute x9, starting transfers between devices, partners(): lax.ppermute(value, axis, [(i, i ^ k * unit ^ (unit > 1)) for i in range(...  11.6 us
    ppermute x9, waiting for transfers between devices, partners(): lax.ppermute(value, axis, [(i, i ^ k * unit ^ (unit > 1)) for i in range(...  10.6 us
    pallas_call x9, Pallas kernels, call(): pl.pallas_call(kernel, out_shape=[jax.ShapeDtypeStruct(s, F32) for s in o...  4.14 us
    ppermute x1, starting transfers between devices, shards(): lax.ppermute(outer, ('gy', 'gz'), chip_neighbours(lax.axis_size('gy'), pe...  2.77 us
    ppermute x1, starting transfers between devices, shards(): peer = lax.ppermute(own, 'gz', [(i, i ^ 1) for i in range(peers)])  1.94 us
    ppermute x1, starting transfers between devices, shards(): inner = lax.ppermute(inner, 'gz', [(i, i ^ 1) for i in range(peers)])  0.74 us
    unnamed x4, local copies, waits for them, and re-layouts  0.68 us
  transfers between devices with their start and end apart: 12, of which 7 were waited for; matrix products, arithmetic and copies ran while one was open for 0% of the time, Pallas kernels for 4%

profile of v3, /device:TPU:1, one launch (start us, length us, event | category | flops | bytes accessed | tf_op | source)
XLA Modules:
  0.0 33.3 jit_solution(3727553346339217377)
XLA Ops:
  0.0 1.1 %shard_map.55 = (f32[128,512]{1,0:T(8,128)S(1)}, f32[128,512]{1,0:T(8,128)S(1)}, f32[128,512]{1,0:T(8,128)S(1)}, f32[2,4,512]{2,1,0:T(4,128)S(1)}, f32[2,4,512]{...) custom-call(f32[128,512]{1,0:T(8,128)} %bitcast.10, f32[128,512]{1,0:T(8,128)} %bitcast.11, ...), custom_call_target="tpu_custom_call" | custom-call | flops 100000 | bytes 25000 | tf_op jit(solution)/shard_map/pallas_call | solution.py:263
  1.1 2.8 %collective-permute-start.1 = (f32[2,4,512]{2,1,0:T(4,128)S(1)}, f32[2,4,512]{2,1,0:T(4,128)S(1)}, u32[]{:S(2)}, u32[]{:S(2)}) collective-permute-start(f32[2,4,512]{2,1,0:T(4,128)S(1)} %get-tuple-element.36), channel_id=1, source_target_pairs={{0,32},{1,2},{2,1},{3,4},{4,3},{5,6},{6,5},{7,8},{8,7},{9,10},{10,... | collective-permute-start | bytes 49160 | tf_op jit(solution)/shard_map/ppermute | solution.py:403
  3.9 0.7 %collective-permute-start = (f32[2,4,512]{2,1,0:T(4,128)S(1)}, f32[2,4,512]{2,1,0:T(4,128)S(1)}, u32[]{:S(2)}, u32[]{:S(2)}) collective-permute-start(f32[2,4,512]{2,1,0:T(4,128)S(1)} %get-tuple-element.35), channel_id=1, source_target_pairs={{0,1},{1,0},{2,3},{3,2},{4,5},{5,4},{6,7},{7,6},{8,9},{9,8},{10,11... | collective-permute-start | bytes 49160 | tf_op jit(solution)/shard_map/ppermute | solution.py:402
  4.6 0.0 copy-start
  4.6 0.0 copy-start.1
  4.6 0.7 %copy-done = f32[2,2]{1,0:T(2,128)S(1)} copy-done((f32[2,2]{1,0:T(2,128)S(1)}, f32[2,2]{1,0:T(2,128)}, u32[]{:S(2)}) %copy-start) | copy-done | bytes 40
  5.3 0.0 copy-done.1
  5.3 1.0 %shard_map.56 = (f32[64,8,128]{2,1,0:T(8,128)S(1)}, f32[64,8,128]{2,1,0:T(8,128)S(1)}, f32[8,128]{1,0:T(8,128)S(1)}, f32[128,512]{1,0:T(8,128)S(1)}, f32[128,512...) custom-call(f32[2,2]{1,0:T(2,128)S(1)} %copy-done, f32[1,2]{1,0:T(1,128)S(1)} %bitcast.9, ...), custom_call_target="tpu_custom_call" | custom-call | flops 4000000 | bytes 1000000 | tf_op jit(solution)/shard_map/pallas_call | solution.py:263
  6.3 0.0 collective-permute-done.1
  6.3 0.0 collective-permute-done.inner
  6.3 0.4 %shard_map.57 = (f32[8,128]{1,0:T(8,128)S(1)}, f32[512,128]{1,0:T(8,128)S(1)}, f32[64,8,128]{2,1,0:T(8,128)S(1)}, f32[64,8,128]{2,1,0:T(8,128)S(1)}) custom-call(f32[128,512]{1,0:T(8,128)S(1)} %get-tuple-element.32.r0, f32[2,4,512]{2,1,0:T(4,128)S(1)} %get-tuple-element.33.low, f32[2,4,512]{2,1,0:T(4,128)S(1)} %get-tuple-element.34.high, ...), custom_call_target="tpu_custom_call" | custom-call | flops 1000000 | bytes 250000 | tf_op jit(solution)/shard_map/pallas_call | solution.py:263
  6.7 3.4 %collective-permute-start.3 = (f32[8,128]{1,0:T(8,128)S(1)}, f32[8,128]{1,0:T(8,128)S(1)}, u32[]{:S(2)}, u32[]{:S(2)}) collective-permute-start(f32[8,128]{1,0:T(8,128)S(1)} %get-tuple-element.40.m0), channel_id=1, source_target_pairs={{0,64},{32,96},{64,0},{96,32},{1,65},{33,97},{65,1},{97,33},{2,66}... | collective-permute-start | bytes 12296 | tf_op jit(solution)/shard_map/ppermute | solution.py:369
  10.1 0.0 collective-permute-start.4
  10.1 0.3 collective-permute-start.2
  10.4 0.1 shard_map.58
  10.5 0.6 %collective-permute-done.3 = f32[8,128]{1,0:T(8,128)S(1)} collective-permute-done((f32[8,128]{1,0:T(8,128)S(1)}, f32[8,128]{1,0:T(8,128)S(1)}, u32[]{:S(2)}, u32[]{:S(2)}) %collective-permute-start.3) | collective-permute-done | bytes 4128 | tf_op jit(solution)/shard_map/ppermute | solution.py:369
  11.1 2.7 %collective-permute-done.4.m3 = f32[8,128]{1,0:T(8,128)S(1)} collective-permute-done((f32[8,128]{1,0:T(8,128)S(1)}, f32[8,128]{1,0:T(8,128)S(1)}, u32[]{:S(2)}, u32[]{:S(2)}) %collective-permute-start.4) | collective-permute-done | bytes 4128 | tf_op jit(solution)/shard_map/ppermute | solution.py:369
  13.8 0.0 collective-permute-done.2.m1
  13.8 0.4 %shard_map.59 = (f32[128,512]{1,0:T(8,128)S(1)}, f32[5,4,512]{2,1,0:T(4,128)S(1)}) custom-call(f32[8,128]{1,0:T(8,128)S(1)} %get-tuple-element.40.m0, f32[8,128]{1,0:T(8,128)S(1)} %collective-permute-done.2.m1, f32[8,128]{1,0:T(8,128)S(1)} %broadcast_multiply_fusion.3.m2, f32[8,128]{1,0:T(8,128)S(1)} %collective-permute-done.4.m3, ...), custom_call_target="tpu_custom_call" | custom-call | flops 1000000 | bytes 250000 | tf_op jit(solution)/shard_map/pallas_call | solution.py:263
  14.2 1.9 %collective-permute-start.5 = (f32[5,4,512]{2,1,0:T(4,128)S(1)}, f32[5,4,512]{2,1,0:T(4,128)S(1)}, u32[]{:S(2)}, u32[]{:S(2)}) collective-permute-start(f32[5,4,512]{2,1,0:T(4,128)S(1)} %get-tuple-element.49.own), channel_id=1, source_target_pairs={{0,1},{1,0},{2,3},{3,2},{4,5},{5,4},{6,7},{7,6},{8,9},{9,8},{10,11... | collective-permute-start | bytes 122888 | tf_op jit(solution)/shard_map/ppermute | solution.py:426
  16.1 0.2 shard_map.60
  16.4 0.6 %collective-permute-done.5.peer = f32[5,4,512]{2,1,0:T(4,128)S(1)} collective-permute-done((f32[5,4,512]{2,1,0:T(4,128)S(1)}, f32[5,4,512]{2,1,0:T(4,128)S(1)}, u32[]{:S(2)}, u32[]{:S(2)}) %collective-permute-start.5) | collective-permute-done | bytes 40992 | tf_op jit(solution)/shard_map/ppermute | solution.py:426
  17.0 2.7 %collective-permute-start.7 = (f32[5,4,512]{2,1,0:T(4,128)S(1)}, f32[5,4,512]{2,1,0:T(4,128)S(1)}, u32[]{:S(2)}, u32[]{:S(2)}) collective-permute-start(f32[5,4,512]{2,1,0:T(4,128)S(1)} %shard_map.61.m0.c0), channel_id=1, source_target_pairs={{0,5},{1,4},{2,7},{3,6},{4,1},{5,0},{6,3},{7,2},{8,13},{9,12},{10,... | collective-permute-start | bytes 122888 | tf_op jit(solution)/shard_map/ppermute | solution.py:369
  19.7 1.0 %collective-permute-start.8 = (f32[5,4,512]{2,1,0:T(4,128)S(1)}, f32[5,4,512]{2,1,0:T(4,128)S(1)}, u32[]{:S(2)}, u32[]{:S(2)}) collective-permute-start(f32[5,4,512]{2,1,0:T(4,128)S(1)} %shard_map.61.m0.c0), channel_id=1, source_target_pairs={{0,7},{1,6},{2,5},{3,4},{4,3},{5,2},{6,1},{7,0},{8,15},{9,14},{10,... | collective-permute-start | bytes 122888 | tf_op jit(solution)/shard_map/ppermute | solution.py:369
  20.7 0.0 collective-permute-start.6
  20.7 1.4 %collective-permute-done.7 = f32[5,4,512]{2,1,0:T(4,128)S(1)} collective-permute-done((f32[5,4,512]{2,1,0:T(4,128)S(1)}, f32[5,4,512]{2,1,0:T(4,128)S(1)}, u32[]{:S(2)}, u32[]{:S(2)}) %collective-permute-start.7) | collective-permute-done | bytes 40992 | tf_op jit(solution)/shard_map/ppermute | solution.py:369
  22.1 2.2 %collective-permute-done.8.m3.c3 = f32[5,4,512]{2,1,0:T(4,128)S(1)} collective-permute-done((f32[5,4,512]{2,1,0:T(4,128)S(1)}, f32[5,4,512]{2,1,0:T(4,128)S(1)}, u32[]{:S(2)}, u32[]{:S(2)}) %collective-permute-start.8) | collective-permute-done | bytes 40992 | tf_op jit(solution)/shard_map/ppermute | solution.py:369
  24.3 0.0 collective-permute-done.6.m1.c1
  24.4 3.4 %collective-permute-start.10 = (f32[5,4,512]{2,1,0:T(4,128)S(1)}, f32[5,4,512]{2,1,0:T(4,128)S(1)}, u32[]{:S(2)}, u32[]{:S(2)}) collective-permute-start(f32[5,4,512]{2,1,0:T(4,128)S(1)} %shard_map.62.p0), channel_id=1, source_target_pairs={{0,17},{1,16},{2,19},{3,18},{4,21},{5,20},{6,23},{7,22},{8,25},{9,... | collective-permute-start | bytes 122888 | tf_op jit(solution)/shard_map/ppermute | solution.py:369
  27.8 0.9 %collective-permute-start.11 = (f32[5,4,512]{2,1,0:T(4,128)S(1)}, f32[5,4,512]{2,1,0:T(4,128)S(1)}, u32[]{:S(2)}, u32[]{:S(2)}) collective-permute-start(f32[5,4,512]{2,1,0:T(4,128)S(1)} %shard_map.62.p0), channel_id=1, source_target_pairs={{0,25},{1,24},{2,27},{3,26},{4,29},{5,28},{6,31},{7,30},{8,17},{9,... | collective-permute-start | bytes 122888 | tf_op jit(solution)/shard_map/ppermute | solution.py:369
  28.6 0.0 collective-permute-start.9
  28.6 0.8 %collective-permute-done.10 = f32[5,4,512]{2,1,0:T(4,128)S(1)} collective-permute-done((f32[5,4,512]{2,1,0:T(4,128)S(1)}, f32[5,4,512]{2,1,0:T(4,128)S(1)}, u32[]{:S(2)}, u32[]{:S(2)}) %collective-permute-start.10) | collective-permute-done | bytes 40992 | tf_op jit(solution)/shard_map/ppermute | solution.py:369
  29.5 3.0 %collective-permute-done.11.p3 = f32[5,4,512]{2,1,0:T(4,128)S(1)} collective-permute-done((f32[5,4,512]{2,1,0:T(4,128)S(1)}, f32[5,4,512]{2,1,0:T(4,128)S(1)}, u32[]{:S(2)}, u32[]{:S(2)}) %collective-permute-start.11) | collective-permute-done | bytes 40992 | tf_op jit(solution)/shard_map/ppermute | solution.py:369
  32.4 0.0 collective-permute-done.9.p1
  32.4 0.8 %shard_map.63 = f32[128,512]{1,0:T(8,128)} custom-call(f32[5,4,512]{2,1,0:T(4,128)S(1)} %get-tuple-element.49.own, f32[5,4,512]{2,1,0:T(4,128)S(1)} %collective-permute-done.5.peer, f32[5,4,512]{2,1,0:T(4,128)S(1)} %shard_map.61.m0.c0, f32[5,4,512]{2,1,0:T(4,128)S(1)} %collective-permute-done.6.m1.c1, f32[5,4,512]{2,1,0:T(4,128)S(1)} %broadcast_multiply_fusion.1.m2.c2, ...), custom_call_target="tpu_custom_call" | custom-call | flops 1000000 | bytes 250000 | tf_op jit(solution)/shard_map/pallas_call | solution.py:263
  (6 shorter events, 0.1 us)
Async XLA Ops:
  1.1 5.2 %collective-permute-start.1 = (f32[2,4,512]{2,1,0:T(4,128)S(1)}, f32[2,4,512]{2,1,0:T(4,128)S(1)}, u32[]{:S(2)}, u32[]{:S(2)}) collective-permute-start(f32[2,4,512]{2,1,0:T(4,128)S(1)} %get-tuple-element.36), channel_id=1, source_target_pairs={{0,32},{1,2},{2,1},{3,4},{4,3},{5,6},{6,5},{7,8},{8,7},{9,10},{10,... | collective-permute-start | bytes 49160 | tf_op jit(solution)/shard_map/ppermute | solution.py:403
  3.9 2.4 %collective-permute-start = (f32[2,4,512]{2,1,0:T(4,128)S(1)}, f32[2,4,512]{2,1,0:T(4,128)S(1)}, u32[]{:S(2)}, u32[]{:S(2)}) collective-permute-start(f32[2,4,512]{2,1,0:T(4,128)S(1)} %get-tuple-element.35), channel_id=1, source_target_pairs={{0,1},{1,0},{2,3},{3,2},{4,5},{5,4},{6,7},{7,6},{8,9},{9,8},{10,11... | collective-permute-start | bytes 49160 | tf_op jit(solution)/shard_map/ppermute | solution.py:402
  4.6 0.7 %copy-start = (f32[2,2]{1,0:T(2,128)S(1)}, f32[2,2]{1,0:T(2,128)}, u32[]{:S(2)}) copy-start(f32[2,2]{1,0:T(2,128)} %cx.1) | copy-start | bytes 52
  4.6 0.7 %copy-start.1 = (f32[2]{0:T(128)S(1)}, f32[2]{0:T(128)}, u32[]{:S(2)}) copy-start(f32[2]{0:T(128)} %param.9) | copy-start | bytes 28
  6.7 4.4 %collective-permute-start.3 = (f32[8,128]{1,0:T(8,128)S(1)}, f32[8,128]{1,0:T(8,128)S(1)}, u32[]{:S(2)}, u32[]{:S(2)}) collective-permute-start(f32[8,128]{1,0:T(8,128)S(1)} %get-tuple-element.40.m0), channel_id=1, source_target_pairs={{0,64},{32,96},{64,0},{96,32},{1,65},{33,97},{65,1},{97,33},{2,66}... | collective-permute-start | bytes 12296 | tf_op jit(solution)/shard_map/ppermute | solution.py:369
  10.1 3.7 %collective-permute-start.4 = (f32[8,128]{1,0:T(8,128)S(1)}, f32[8,128]{1,0:T(8,128)S(1)}, u32[]{:S(2)}, u32[]{:S(2)}) collective-permute-start(f32[8,128]{1,0:T(8,128)S(1)} %get-tuple-element.40.m0), channel_id=1, source_target_pairs={{0,96},{32,64},{64,32},{96,0},{1,97},{33,65},{65,33},{97,1},{2,98}... | collective-permute-start | bytes 12296 | tf_op jit(solution)/shard_map/ppermute | solution.py:369
  10.1 3.7 %collective-permute-start.2 = (f32[8,128]{1,0:T(8,128)S(1)}, f32[8,128]{1,0:T(8,128)S(1)}, u32[]{:S(2)}, u32[]{:S(2)}) collective-permute-start(f32[8,128]{1,0:T(8,128)S(1)} %get-tuple-element.40.m0), channel_id=1, source_target_pairs={{0,32},{32,0},{64,96},{96,64},{1,33},{33,1},{65,97},{97,65},{2,34}... | collective-permute-start | bytes 12296 | tf_op jit(solution)/shard_map/ppermute | solution.py:369
  14.2 2.8 %collective-permute-start.5 = (f32[5,4,512]{2,1,0:T(4,128)S(1)}, f32[5,4,512]{2,1,0:T(4,128)S(1)}, u32[]{:S(2)}, u32[]{:S(2)}) collective-permute-start(f32[5,4,512]{2,1,0:T(4,128)S(1)} %get-tuple-element.49.own), channel_id=1, source_target_pairs={{0,1},{1,0},{2,3},{3,2},{4,5},{5,4},{6,7},{7,6},{8,9},{9,8},{10,11... | collective-permute-start | bytes 122888 | tf_op jit(solution)/shard_map/ppermute | solution.py:426
  17.0 5.1 %collective-permute-start.7 = (f32[5,4,512]{2,1,0:T(4,128)S(1)}, f32[5,4,512]{2,1,0:T(4,128)S(1)}, u32[]{:S(2)}, u32[]{:S(2)}) collective-permute-start(f32[5,4,512]{2,1,0:T(4,128)S(1)} %shard_map.61.m0.c0), channel_id=1, source_target_pairs={{0,5},{1,4},{2,7},{3,6},{4,1},{5,0},{6,3},{7,2},{8,13},{9,12},{10,... | collective-permute-start | bytes 122888 | tf_op jit(solution)/shard_map/ppermute | solution.py:369
  19.7 4.6 %collective-permute-start.8 = (f32[5,4,512]{2,1,0:T(4,128)S(1)}, f32[5,4,512]{2,1,0:T(4,128)S(1)}, u32[]{:S(2)}, u32[]{:S(2)}) collective-permute-start(f32[5,4,512]{2,1,0:T(4,128)S(1)} %shard_map.61.m0.c0), channel_id=1, source_target_pairs={{0,7},{1,6},{2,5},{3,4},{4,3},{5,2},{6,1},{7,0},{8,15},{9,14},{10,... | collective-permute-start | bytes 122888 | tf_op jit(solution)/shard_map/ppermute | solution.py:369
  20.7 3.6 %collective-permute-start.6 = (f32[5,4,512]{2,1,0:T(4,128)S(1)}, f32[5,4,512]{2,1,0:T(4,128)S(1)}, u32[]{:S(2)}, u32[]{:S(2)}) collective-permute-start(f32[5,4,512]{2,1,0:T(4,128)S(1)} %shard_map.61.m0.c0), channel_id=1, source_target_pairs={{0,3},{1,2},{2,1},{3,0},{4,7},{5,6},{6,5},{7,4},{8,11},{9,10},{10,... | collective-permute-start | bytes 122888 | tf_op jit(solution)/shard_map/ppermute | solution.py:369
  24.4 5.1 %collective-permute-start.10 = (f32[5,4,512]{2,1,0:T(4,128)S(1)}, f32[5,4,512]{2,1,0:T(4,128)S(1)}, u32[]{:S(2)}, u32[]{:S(2)}) collective-permute-start(f32[5,4,512]{2,1,0:T(4,128)S(1)} %shard_map.62.p0), channel_id=1, source_target_pairs={{0,17},{1,16},{2,19},{3,18},{4,21},{5,20},{6,23},{7,22},{8,25},{9,... | collective-permute-start | bytes 122888 | tf_op jit(solution)/shard_map/ppermute | solution.py:369
  27.8 4.7 %collective-permute-start.11 = (f32[5,4,512]{2,1,0:T(4,128)S(1)}, f32[5,4,512]{2,1,0:T(4,128)S(1)}, u32[]{:S(2)}, u32[]{:S(2)}) collective-permute-start(f32[5,4,512]{2,1,0:T(4,128)S(1)} %shard_map.62.p0), channel_id=1, source_target_pairs={{0,25},{1,24},{2,27},{3,26},{4,29},{5,28},{6,31},{7,30},{8,17},{9,... | collective-permute-start | bytes 122888 | tf_op jit(solution)/shard_map/ppermute | solution.py:369
  28.6 3.8 %collective-permute-start.9 = (f32[5,4,512]{2,1,0:T(4,128)S(1)}, f32[5,4,512]{2,1,0:T(4,128)S(1)}, u32[]{:S(2)}, u32[]{:S(2)}) collective-permute-start(f32[5,4,512]{2,1,0:T(4,128)S(1)} %shard_map.62.p0), channel_id=1, source_target_pairs={{0,9},{1,8},{2,11},{3,10},{4,13},{5,12},{6,15},{7,14},{8,1},{9,0},... | collective-permute-start | bytes 122888 | tf_op jit(solution)/shard_map/ppermute | solution.py:369

commit v4 on v3

--- a/solution.py
+++ b/solution.py
@@ -311,7 +311,7 @@
 
 def ring_kernel(position, m0, m1, m2, m3, plane, buf):
     mine = position(lax.axis_index("gz"))
-    for k, got in enumerate((m0, m1, m2, m3)):
+    for k, got in zip(distances(lax.axis_index("gz")), (m0, m1, m2, m3)):
         buf[mine ^ k] = got[...]
     s = [parts_of(buf.at[j]) for j in range(4)]
     put(plane, join(join(s[0], s[1]), join(s[2], s[3])))
@@ -331,7 +331,7 @@
     own, peer, c0, c1, c2, c3, p0, p1, p2, p3, local, gpz, gsz, out, cbuf, pbuf
 ):
     iy, ix = position_y(lax.axis_index("gz")), position_x(lax.axis_index("gz"))
-    for k, (c, p) in enumerate(((c0, p0), (c1, p1), (c2, p2), (c3, p3))):
+    for k, (c, p) in zip(distances(lax.axis_index("gz")), ((c0, p0), (c1, p1), (c2, p2), (c3, p3))):
         cbuf[iy ^ k] = c[...]
         pbuf[ix ^ k] = p[...]
     column = [parts_of(cbuf.at[j]) for j in range(4)]
@@ -356,6 +356,18 @@
         )
 
 
+def distances(z):
+    core = z % 2
+    return 0, 1, 3 - core, 2 + core
+
+
+def chain_of(value, count, unit):
+    far = lax.ppermute(value, "gz", [(i, i ^ ((3 - i % 2) * unit)) for i in range(count)])
+    near = lax.ppermute(value, "gz", [(i, i ^ unit ^ 1) for i in range(count)])
+    rest = lax.ppermute(far, "gz", [(i, i ^ 1) for i in range(count)])
+    return [value, near, far, rest]
+
+
 def position_y(z):
     return z // 2 % 4
 
@@ -426,12 +438,12 @@
     peer = lax.ppermute(own, "gz", [(i, i ^ 1) for i in range(peers)])
     local, ready = call(z_local_kernel, [flat, (8, 128)], [], 1_000_000, [VMEM] * 5, u, rz, gpz, gsz, zmat)
     [chip] = call(core_kernel, [ends], [], 50_000, [VMEM] * 3, own, peer, ready)
-    column = [chip] + partners(chip, "gz", peers, 2)
+    column = chain_of(chip, peers, 2)
     [plane] = call(
         functools.partial(ring_kernel, position_y), [ends], [(4, *ends)], 50_000,
         [VMEM] * 4, *column,
     )
-    whole = [plane] + partners(plane, "gz", peers, 8)
+    whole = chain_of(plane, peers, 8)
     [out] = call(
         finish_kernel, [flat], [(4, *ends), (4, *ends)], 1_000_000, [VMEM] * 13,
         own, peer, *column, *whole, local, gpz, gsz,

time: 33.4 us -> 32.5 us (0.973)
  waiting for transfers between devices: 11.3 us -> 8.81 us
  starting transfers between devices: 17.1 us -> 18.6 us
    ppermute x0 -> x6, starting transfers between devices: none -> 9.49 us  [the longest x2 6.78 us: chain_of(): lax.ppermute(value, 'gz', [(i, i ^ (3 - i % 2) * unit) for i in range(cou...]
    ppermute x9 -> x3, starting transfers between devices: 11.6 us -> 3.68 us  [partners(): lax.ppermute(value, axis, [(i, i ^ k * unit ^ (unit > 1)) for i in range(...]
    ppermute x9 -> x3, waiting for transfers between devices: 10.6 us -> 3.26 us  [partners(): lax.ppermute(value, axis, [(i, i ^ k * unit ^ (unit > 1)) for i in range(...]
    ppermute x0 -> x6, waiting for transfers between devices: none -> 4.93 us  [the longest x2 3.03 us: chain_of(): lax.ppermute(value, 'gz', [(i, i ^ (3 - i % 2) * unit) for i in range(cou...]
  transfers between devices with their start and end apart: 12 -> 12, of which waited for: 7 -> 8; matrix products, arithmetic and copies ran while one was open for 0% -> 0% of each run, Pallas kernels for 4% -> 4%
where the time goes in v4:
time: 32.5 us; the launch traced here: 32.3 us
  starting transfers between devices  18.6 us (57%)
  waiting for transfers between devices  8.81 us (27%)
  Pallas kernels  4.14 us (13%)
  local copies, waits for them, and re-layouts  0.68 us (2%)
    ppermute x2, starting transfers between devices, chain_of(): lax.ppermute(value, 'gz', [(i, i ^ (3 - i % 2) * unit) for i in range(cou...  6.78 us
    pallas_call x9, Pallas kernels, call(): pl.pallas_call(kernel, out_shape=[jax.ShapeDtypeStruct(s, F32) for s in o...  4.14 us
    ppermute x3, starting transfers between devices, partners(): lax.ppermute(value, axis, [(i, i ^ k * unit ^ (unit > 1)) for i in range(...  3.68 us
    ppermute x3, waiting for transfers between devices, partners(): lax.ppermute(value, axis, [(i, i ^ k * unit ^ (unit > 1)) for i in range(...  3.26 us
    ppermute x2, waiting for transfers between devices, chain_of(): lax.ppermute(value, 'gz', [(i, i ^ (3 - i % 2) * unit) for i in range(cou...  3.03 us
    ppermute x1, starting transfers between devices, shards(): lax.ppermute(outer, ('gy', 'gz'), chip_neighbours(lax.axis_size('gy'), pe...  2.77 us
    ppermute x2, starting transfers between devices, chain_of(): rest = lax.ppermute(far, 'gz', [(i, i ^ 1) for i in range(count)])  2.32 us
    ppermute x1, starting transfers between devices, shards(): peer = lax.ppermute(own, 'gz', [(i, i ^ 1) for i in range(peers)])  1.94 us
  transfers between devices with their start and end apart: 12, of which 8 were waited for; matrix products, arithmetic and copies ran while one was open for 0% of the time, Pallas kernels for 4%

profile of v4, /device:TPU:1, one launch (start us, length us, event | category | flops | bytes accessed | tf_op | source)
XLA Modules:
  0.0 32.3 jit_solution(1305132078083623212)
XLA Ops:
  0.0 1.1 %shard_map.55 = (f32[128,512]{1,0:T(8,128)S(1)}, f32[128,512]{1,0:T(8,128)S(1)}, f32[128,512]{1,0:T(8,128)S(1)}, f32[2,4,512]{2,1,0:T(4,128)S(1)}, f32[2,4,512]{...) custom-call(f32[128,512]{1,0:T(8,128)} %bitcast.10, f32[128,512]{1,0:T(8,128)} %bitcast.11, ...), custom_call_target="tpu_custom_call" | custom-call | flops 100000 | bytes 25000 | tf_op jit(solution)/shard_map/pallas_call | solution.py:263
  1.1 2.8 %collective-permute-start.1 = (f32[2,4,512]{2,1,0:T(4,128)S(1)}, f32[2,4,512]{2,1,0:T(4,128)S(1)}, u32[]{:S(2)}, u32[]{:S(2)}) collective-permute-start(f32[2,4,512]{2,1,0:T(4,128)S(1)} %get-tuple-element.36), channel_id=1, source_target_pairs={{0,32},{1,2},{2,1},{3,4},{4,3},{5,6},{6,5},{7,8},{8,7},{9,10},{10,... | collective-permute-start | bytes 49160 | tf_op jit(solution)/shard_map/ppermute | solution.py:415
  3.9 0.7 %collective-permute-start = (f32[2,4,512]{2,1,0:T(4,128)S(1)}, f32[2,4,512]{2,1,0:T(4,128)S(1)}, u32[]{:S(2)}, u32[]{:S(2)}) collective-permute-start(f32[2,4,512]{2,1,0:T(4,128)S(1)} %get-tuple-element.35), channel_id=1, source_target_pairs={{0,1},{1,0},{2,3},{3,2},{4,5},{5,4},{6,7},{7,6},{8,9},{9,8},{10,11... | collective-permute-start | bytes 49160 | tf_op jit(solution)/shard_map/ppermute | solution.py:414
  4.6 0.0 copy-start
  4.6 0.0 copy-start.1
  4.6 0.7 %copy-done = f32[2,2]{1,0:T(2,128)S(1)} copy-done((f32[2,2]{1,0:T(2,128)S(1)}, f32[2,2]{1,0:T(2,128)}, u32[]{:S(2)}) %copy-start) | copy-done | bytes 40
  5.3 0.0 copy-done.1
  5.3 1.0 %shard_map.56 = (f32[64,8,128]{2,1,0:T(8,128)S(1)}, f32[64,8,128]{2,1,0:T(8,128)S(1)}, f32[8,128]{1,0:T(8,128)S(1)}, f32[128,512]{1,0:T(8,128)S(1)}, f32[128,512...) custom-call(f32[2,2]{1,0:T(2,128)S(1)} %copy-done, f32[1,2]{1,0:T(1,128)S(1)} %bitcast.9, ...), custom_call_target="tpu_custom_call" | custom-call | flops 4000000 | bytes 1000000 | tf_op jit(solution)/shard_map/pallas_call | solution.py:263
  6.3 0.0 collective-permute-done.1
  6.3 0.0 collective-permute-done.inner
  6.3 0.4 %shard_map.57 = (f32[8,128]{1,0:T(8,128)S(1)}, f32[512,128]{1,0:T(8,128)S(1)}, f32[64,8,128]{2,1,0:T(8,128)S(1)}, f32[64,8,128]{2,1,0:T(8,128)S(1)}) custom-call(f32[128,512]{1,0:T(8,128)S(1)} %get-tuple-element.32.r0, f32[2,4,512]{2,1,0:T(4,128)S(1)} %get-tuple-element.33.low, f32[2,4,512]{2,1,0:T(4,128)S(1)} %get-tuple-element.34.high, ...), custom_call_target="tpu_custom_call" | custom-call | flops 1000000 | bytes 250000 | tf_op jit(solution)/shard_map/pallas_call | solution.py:263
  6.7 3.4 %collective-permute-start.3 = (f32[8,128]{1,0:T(8,128)S(1)}, f32[8,128]{1,0:T(8,128)S(1)}, u32[]{:S(2)}, u32[]{:S(2)}) collective-permute-start(f32[8,128]{1,0:T(8,128)S(1)} %get-tuple-element.40.m0), channel_id=1, source_target_pairs={{0,64},{32,96},{64,0},{96,32},{1,65},{33,97},{65,1},{97,33},{2,66}... | collective-permute-start | bytes 12296 | tf_op jit(solution)/shard_map/ppermute | solution.py:381
  10.1 0.0 collective-permute-start.4
  10.1 0.3 collective-permute-start.2
  10.4 0.1 shard_map.58
  10.5 0.6 %collective-permute-done.3 = f32[8,128]{1,0:T(8,128)S(1)} collective-permute-done((f32[8,128]{1,0:T(8,128)S(1)}, f32[8,128]{1,0:T(8,128)S(1)}, u32[]{:S(2)}, u32[]{:S(2)}) %collective-permute-start.3) | collective-permute-done | bytes 4128 | tf_op jit(solution)/shard_map/ppermute | solution.py:381
  11.1 2.7 %collective-permute-done.4.m3 = f32[8,128]{1,0:T(8,128)S(1)} collective-permute-done((f32[8,128]{1,0:T(8,128)S(1)}, f32[8,128]{1,0:T(8,128)S(1)}, u32[]{:S(2)}, u32[]{:S(2)}) %collective-permute-start.4) | collective-permute-done | bytes 4128 | tf_op jit(solution)/shard_map/ppermute | solution.py:381
  13.8 0.0 collective-permute-done.2.m1
  13.8 0.4 %shard_map.59 = (f32[128,512]{1,0:T(8,128)S(1)}, f32[5,4,512]{2,1,0:T(4,128)S(1)}) custom-call(f32[8,128]{1,0:T(8,128)S(1)} %get-tuple-element.40.m0, f32[8,128]{1,0:T(8,128)S(1)} %collective-permute-done.2.m1, f32[8,128]{1,0:T(8,128)S(1)} %broadcast_multiply_fusion.1.m2, f32[8,128]{1,0:T(8,128)S(1)} %collective-permute-done.4.m3, ...), custom_call_target="tpu_custom_call" | custom-call | flops 1000000 | bytes 250000 | tf_op jit(solution)/shard_map/pallas_call | solution.py:263
  14.2 1.9 %collective-permute-start.5 = (f32[5,4,512]{2,1,0:T(4,128)S(1)}, f32[5,4,512]{2,1,0:T(4,128)S(1)}, u32[]{:S(2)}, u32[]{:S(2)}) collective-permute-start(f32[5,4,512]{2,1,0:T(4,128)S(1)} %get-tuple-element.49.own), channel_id=1, source_target_pairs={{0,1},{1,0},{2,3},{3,2},{4,5},{5,4},{6,7},{7,6},{8,9},{9,8},{10,11... | collective-permute-start | bytes 122888 | tf_op jit(solution)/shard_map/ppermute | solution.py:438
  16.1 0.2 shard_map.60
  16.4 0.6 %collective-permute-done.5.peer = f32[5,4,512]{2,1,0:T(4,128)S(1)} collective-permute-done((f32[5,4,512]{2,1,0:T(4,128)S(1)}, f32[5,4,512]{2,1,0:T(4,128)S(1)}, u32[]{:S(2)}, u32[]{:S(2)}) %collective-permute-start.5) | collective-permute-done | bytes 40992 | tf_op jit(solution)/shard_map/ppermute | solution.py:438
  17.0 2.4 %collective-permute-start.7 = (f32[5,4,512]{2,1,0:T(4,128)S(1)}, f32[5,4,512]{2,1,0:T(4,128)S(1)}, u32[]{:S(2)}, u32[]{:S(2)}) collective-permute-start(f32[5,4,512]{2,1,0:T(4,128)S(1)} %shard_map.61.m0.c0), channel_id=1, source_target_pairs={{0,6},{1,5},{2,4},{3,7},{4,2},{5,1},{6,0},{7,3},{8,14},{9,13},{10,... | collective-permute-start | bytes 122888 | tf_op jit(solution)/shard_map/ppermute | solution.py:365
  19.4 0.2 collective-permute-start.6
  19.6 1.8 %collective-permute-done.7.m2.c2 = f32[5,4,512]{2,1,0:T(4,128)S(1)} collective-permute-done((f32[5,4,512]{2,1,0:T(4,128)S(1)}, f32[5,4,512]{2,1,0:T(4,128)S(1)}, u32[]{:S(2)}, u32[]{:S(2)}) %collective-permute-start.7) | collective-permute-done | bytes 40992 | tf_op jit(solution)/shard_map/ppermute | solution.py:365
  21.4 1.2 %collective-permute-start.8 = (f32[5,4,512]{2,1,0:T(4,128)S(1)}, f32[5,4,512]{2,1,0:T(4,128)S(1)}, u32[]{:S(2)}, u32[]{:S(2)}) collective-permute-start(f32[5,4,512]{2,1,0:T(4,128)S(1)} %collective-permute-done.7.m2.c2), channel_id=1, source_target_pairs={{0,1},{1,0},{2,3},{3,2},{4,5},{5,4},{6,7},{7,6},{8,9},{9,8},{10,11... | collective-permute-start | bytes 122888 | tf_op jit(solution)/shard_map/ppermute | solution.py:367
  22.6 0.8 %collective-permute-done.6.m1.c1 = f32[5,4,512]{2,1,0:T(4,128)S(1)} collective-permute-done((f32[5,4,512]{2,1,0:T(4,128)S(1)}, f32[5,4,512]{2,1,0:T(4,128)S(1)}, u32[]{:S(2)}, u32[]{:S(2)}) %collective-permute-start.6) | collective-permute-done | bytes 40992 | tf_op jit(solution)/shard_map/ppermute | solution.py:366
  23.4 0.1 collective-permute-done.8.m3.c3
  23.6 4.4 %collective-permute-start.10 = (f32[5,4,512]{2,1,0:T(4,128)S(1)}, f32[5,4,512]{2,1,0:T(4,128)S(1)}, u32[]{:S(2)}, u32[]{:S(2)}) collective-permute-start(f32[5,4,512]{2,1,0:T(4,128)S(1)} %shard_map.62.p0), channel_id=1, source_target_pairs={{0,24},{1,17},{2,26},{3,19},{4,28},{5,21},{6,30},{7,23},{8,16},{9,... | collective-permute-start | bytes 122888 | tf_op jit(solution)/shard_map/ppermute | solution.py:365
  27.9 0.2 collective-permute-start.9
  28.1 1.2 %collective-permute-done.10.p2 = f32[5,4,512]{2,1,0:T(4,128)S(1)} collective-permute-done((f32[5,4,512]{2,1,0:T(4,128)S(1)}, f32[5,4,512]{2,1,0:T(4,128)S(1)}, u32[]{:S(2)}, u32[]{:S(2)}) %collective-permute-start.10) | collective-permute-done | bytes 40992 | tf_op jit(solution)/shard_map/ppermute | solution.py:365
  29.3 1.1 %collective-permute-start.11 = (f32[5,4,512]{2,1,0:T(4,128)S(1)}, f32[5,4,512]{2,1,0:T(4,128)S(1)}, u32[]{:S(2)}, u32[]{:S(2)}) collective-permute-start(f32[5,4,512]{2,1,0:T(4,128)S(1)} %collective-permute-done.10.p2), channel_id=1, source_target_pairs={{0,1},{1,0},{2,3},{3,2},{4,5},{5,4},{6,7},{7,6},{8,9},{9,8},{10,11... | collective-permute-start | bytes 122888 | tf_op jit(solution)/shard_map/ppermute | solution.py:367
  30.4 1.0 %collective-permute-done.9.p1 = f32[5,4,512]{2,1,0:T(4,128)S(1)} collective-permute-done((f32[5,4,512]{2,1,0:T(4,128)S(1)}, f32[5,4,512]{2,1,0:T(4,128)S(1)}, u32[]{:S(2)}, u32[]{:S(2)}) %collective-permute-start.9) | collective-permute-done | bytes 40992 | tf_op jit(solution)/shard_map/ppermute | solution.py:366
  31.5 0.0 collective-permute-done.11.p3
  31.5 0.9 %shard_map.63 = f32[128,512]{1,0:T(8,128)} custom-call(f32[5,4,512]{2,1,0:T(4,128)S(1)} %get-tuple-element.49.own, f32[5,4,512]{2,1,0:T(4,128)S(1)} %collective-permute-done.5.peer, f32[5,4,512]{2,1,0:T(4,128)S(1)} %shard_map.61.m0.c0, f32[5,4,512]{2,1,0:T(4,128)S(1)} %collective-permute-done.6.m1.c1, f32[5,4,512]{2,1,0:T(4,128)S(1)} %collective-permute-done.7.m2.c2, ...), custom_call_target="tpu_custom_call" | custom-call | flops 1000000 | bytes 250000 | tf_op jit(solution)/shard_map/pallas_call | solution.py:263
  (4 shorter events, 0.1 us)
Async XLA Ops:
  1.1 5.2 %collective-permute-start.1 = (f32[2,4,512]{2,1,0:T(4,128)S(1)}, f32[2,4,512]{2,1,0:T(4,128)S(1)}, u32[]{:S(2)}, u32[]{:S(2)}) collective-permute-start(f32[2,4,512]{2,1,0:T(4,128)S(1)} %get-tuple-element.36), channel_id=1, source_target_pairs={{0,32},{1,2},{2,1},{3,4},{4,3},{5,6},{6,5},{7,8},{8,7},{9,10},{10,... | collective-permute-start | bytes 49160 | tf_op jit(solution)/shard_map/ppermute | solution.py:415
  3.9 2.4 %collective-permute-start = (f32[2,4,512]{2,1,0:T(4,128)S(1)}, f32[2,4,512]{2,1,0:T(4,128)S(1)}, u32[]{:S(2)}, u32[]{:S(2)}) collective-permute-start(f32[2,4,512]{2,1,0:T(4,128)S(1)} %get-tuple-element.35), channel_id=1, source_target_pairs={{0,1},{1,0},{2,3},{3,2},{4,5},{5,4},{6,7},{7,6},{8,9},{9,8},{10,11... | collective-permute-start | bytes 49160 | tf_op jit(solution)/shard_map/ppermute | solution.py:414
  4.6 0.7 %copy-start = (f32[2,2]{1,0:T(2,128)S(1)}, f32[2,2]{1,0:T(2,128)}, u32[]{:S(2)}) copy-start(f32[2,2]{1,0:T(2,128)} %cx.1) | copy-start | bytes 52
  4.6 0.7 %copy-start.1 = (f32[2]{0:T(128)S(1)}, f32[2]{0:T(128)}, u32[]{:S(2)}) copy-start(f32[2]{0:T(128)} %param.9) | copy-start | bytes 28
  6.7 4.4 %collective-permute-start.3 = (f32[8,128]{1,0:T(8,128)S(1)}, f32[8,128]{1,0:T(8,128)S(1)}, u32[]{:S(2)}, u32[]{:S(2)}) collective-permute-start(f32[8,128]{1,0:T(8,128)S(1)} %get-tuple-element.40.m0), channel_id=1, source_target_pairs={{0,64},{32,96},{64,0},{96,32},{1,65},{33,97},{65,1},{97,33},{2,66}... | collective-permute-start | bytes 12296 | tf_op jit(solution)/shard_map/ppermute | solution.py:381
  10.1 3.7 %collective-permute-start.4 = (f32[8,128]{1,0:T(8,128)S(1)}, f32[8,128]{1,0:T(8,128)S(1)}, u32[]{:S(2)}, u32[]{:S(2)}) collective-permute-start(f32[8,128]{1,0:T(8,128)S(1)} %get-tuple-element.40.m0), channel_id=1, source_target_pairs={{0,96},{32,64},{64,32},{96,0},{1,97},{33,65},{65,33},{97,1},{2,98}... | collective-permute-start | bytes 12296 | tf_op jit(solution)/shard_map/ppermute | solution.py:381
  10.1 3.7 %collective-permute-start.2 = (f32[8,128]{1,0:T(8,128)S(1)}, f32[8,128]{1,0:T(8,128)S(1)}, u32[]{:S(2)}, u32[]{:S(2)}) collective-permute-start(f32[8,128]{1,0:T(8,128)S(1)} %get-tuple-element.40.m0), channel_id=1, source_target_pairs={{0,32},{32,0},{64,96},{96,64},{1,33},{33,1},{65,97},{97,65},{2,34}... | collective-permute-start | bytes 12296 | tf_op jit(solution)/shard_map/ppermute | solution.py:381
  14.2 2.8 %collective-permute-start.5 = (f32[5,4,512]{2,1,0:T(4,128)S(1)}, f32[5,4,512]{2,1,0:T(4,128)S(1)}, u32[]{:S(2)}, u32[]{:S(2)}) collective-permute-start(f32[5,4,512]{2,1,0:T(4,128)S(1)} %get-tuple-element.49.own), channel_id=1, source_target_pairs={{0,1},{1,0},{2,3},{3,2},{4,5},{5,4},{6,7},{7,6},{8,9},{9,8},{10,11... | collective-permute-start | bytes 122888 | tf_op jit(solution)/shard_map/ppermute | solution.py:438
  17.0 4.4 %collective-permute-start.7 = (f32[5,4,512]{2,1,0:T(4,128)S(1)}, f32[5,4,512]{2,1,0:T(4,128)S(1)}, u32[]{:S(2)}, u32[]{:S(2)}) collective-permute-start(f32[5,4,512]{2,1,0:T(4,128)S(1)} %shard_map.61.m0.c0), channel_id=1, source_target_pairs={{0,6},{1,5},{2,4},{3,7},{4,2},{5,1},{6,0},{7,3},{8,14},{9,13},{10,... | collective-permute-start | bytes 122888 | tf_op jit(solution)/shard_map/ppermute | solution.py:365
  19.4 4.0 %collective-permute-start.6 = (f32[5,4,512]{2,1,0:T(4,128)S(1)}, f32[5,4,512]{2,1,0:T(4,128)S(1)}, u32[]{:S(2)}, u32[]{:S(2)}) collective-permute-start(f32[5,4,512]{2,1,0:T(4,128)S(1)} %shard_map.61.m0.c0), channel_id=1, source_target_pairs={{0,3},{1,2},{2,1},{3,0},{4,7},{5,6},{6,5},{7,4},{8,11},{9,10},{10,... | collective-permute-start | bytes 122888 | tf_op jit(solution)/shard_map/ppermute | solution.py:366
  21.4 2.1 %collective-permute-start.8 = (f32[5,4,512]{2,1,0:T(4,128)S(1)}, f32[5,4,512]{2,1,0:T(4,128)S(1)}, u32[]{:S(2)}, u32[]{:S(2)}) collective-permute-start(f32[5,4,512]{2,1,0:T(4,128)S(1)} %collective-permute-done.7.m2.c2), channel_id=1, source_target_pairs={{0,1},{1,0},{2,3},{3,2},{4,5},{5,4},{6,7},{7,6},{8,9},{9,8},{10,11... | collective-permute-start | bytes 122888 | tf_op jit(solution)/shard_map/ppermute | solution.py:367
  23.6 5.8 %collective-permute-start.10 = (f32[5,4,512]{2,1,0:T(4,128)S(1)}, f32[5,4,512]{2,1,0:T(4,128)S(1)}, u32[]{:S(2)}, u32[]{:S(2)}) collective-permute-start(f32[5,4,512]{2,1,0:T(4,128)S(1)} %shard_map.62.p0), channel_id=1, source_target_pairs={{0,24},{1,17},{2,26},{3,19},{4,28},{5,21},{6,30},{7,23},{8,16},{9,... | collective-permute-start | bytes 122888 | tf_op jit(solution)/shard_map/ppermute | solution.py:365
  27.9 3.5 %collective-permute-start.9 = (f32[5,4,512]{2,1,0:T(4,128)S(1)}, f32[5,4,512]{2,1,0:T(4,128)S(1)}, u32[]{:S(2)}, u32[]{:S(2)}) collective-permute-start(f32[5,4,512]{2,1,0:T(4,128)S(1)} %shard_map.62.p0), channel_id=1, source_target_pairs={{0,9},{1,8},{2,11},{3,10},{4,13},{5,12},{6,15},{7,14},{8,1},{9,0},... | collective-permute-start | bytes 122888 | tf_op jit(solution)/shard_map/ppermute | solution.py:366
  29.3 2.1 %collective-permute-start.11 = (f32[5,4,512]{2,1,0:T(4,128)S(1)}, f32[5,4,512]{2,1,0:T(4,128)S(1)}, u32[]{:S(2)}, u32[]{:S(2)}) collective-permute-start(f32[5,4,512]{2,1,0:T(4,128)S(1)} %collective-permute-done.10.p2), channel_id=1, source_target_pairs={{0,1},{1,0},{2,3},{3,2},{4,5},{5,4},{6,7},{7,6},{8,9},{9,8},{10,11... | collective-permute-start | bytes 122888 | tf_op jit(solution)/shard_map/ppermute | solution.py:367

commit v5 on v4

--- a/solution.py
+++ b/solution.py
@@ -138,10 +138,30 @@
             )
 
 
-def y_ends_kernel(peers, r0, low, high, inner, outer, gpy, gsy, ymat, msg, rt, ss, qq):
+def y_base_kernel(r0, gpy, gsy, ymat, base, gp_edge, gs_edge, gp_rows, gs_rows, rt):
     steps, _, lines = gpy.shape
-    length = steps * SUB
-    planes = low.shape[1]
+    planes = gp_edge.shape[0] // 2
+    depth = lines // planes
+    rt[...] = r0[...].T
+    s = jnp.zeros((SUB, lines), F32)
+    q = jnp.zeros((SUB, lines), F32)
+    for t in range(steps):
+        r = strided(rt, t, SUB, steps)
+        s, q = s + gpy[t] * r, q + gsy[t] * r
+    base[...] = ymat[...]
+    base[0:1, :] = jnp.sum(q, axis=0, keepdims=True)
+    base[1:2, :] = jnp.sum(s, axis=0, keepdims=True)
+    for g, edge, rows in ((gpy, gp_edge, gp_rows), (gsy, gs_edge, gs_rows)):
+        for t in range(steps):
+            rt[pl.ds(t, SUB, stride=steps), :] = g[t]
+        rows[...] = rt[...].T
+        for p in range(planes):
+            edge[p : p + 1, :] = rows[p * depth : p * depth + 1]
+            edge[planes + p : planes + p + 1, :] = rows[(p + 1) * depth - 1 : (p + 1) * depth]
+
+
+def y_ends_kernel(peers, low, high, inner, outer, base, gp_edge, gs_edge, msg, change):
+    planes, lines = low.shape[1], base.shape[1]
     depth = lines // planes
     under = jnp.where(lax.axis_index("gz") > 0, 1.0, 0.0)
     over = jnp.where(lax.axis_index("gz") < peers - 1, 1.0, 0.0)
@@ -150,15 +170,33 @@
     above = [jnp.where(even, inner[i], outer[i]) * over for i in range(2)]
     lo = 0.5 * (below[1] + low[1]) * (below[0] - low[0])
     hi = 0.5 * (above[1] + high[1]) * (above[0] - high[0])
+    both = jnp.concatenate([lo, hi], 0)
+    change[...] = both
+    row = lax.broadcasted_iota(jnp.int32, (2 * planes, lines), 0)
+    line = lax.broadcasted_iota(jnp.int32, (2 * planes, lines), 1)
+    here = line == jnp.where(row < planes, row * depth, (row - planes + 1) * depth - 1)
+    msg[...] = base[...]
+    for i, edge in enumerate((gs_edge, gp_edge)):
+        ends = jnp.sum(edge[...] * both, axis=1, keepdims=True)
+        added = jnp.sum(jnp.where(here, ends, 0.0), axis=0, keepdims=True)
+        msg[i : i + 1, :] = base[i : i + 1, :] + added
+
+
+def y_local_kernel(
+    peers, u, r0, change, low, high, inner, outer, zmat, gpy, gsy, ymat, rz0, zends, rt, ss, qq
+):
+    steps, _, lines = gpy.shape
+    planes, length = low.shape[1:]
+    depth = lines // planes
     row = lax.broadcasted_iota(jnp.int32, (SUB, length), 0)
     parts = []
     for p in range(planes):
         i = p * depth
         top, mid, end = r0[i : i + SUB], r0[i + SUB : i + depth - SUB], r0[i + depth - SUB : i + depth]
         parts += [
-            jnp.where(row == 0, top + lo[p : p + 1, :], top),
+            jnp.where(row == 0, top + change[p : p + 1, :], top),
             mid,
-            jnp.where(row == SUB - 1, end + hi[p : p + 1, :], end),
+            jnp.where(row == SUB - 1, end + change[planes + p : planes + p + 1, :], end),
         ]
     rt[...] = jnp.concatenate(parts, 0).T
     s = jnp.zeros((SUB, lines), F32)
@@ -169,15 +207,6 @@
         ss[t] = s
         qq[back] = q
         q = q + gsy[back] * strided(rt, back, SUB, steps)
-    msg[...] = ymat[...]
-    msg[0:1, :] = jnp.sum(q, axis=0, keepdims=True)
-    msg[1:2, :] = jnp.sum(s, axis=0, keepdims=True)
-
-
-def y_local_kernel(peers, low, high, inner, outer, zmat, rt, ss, qq, gpy, gsy, ymat, vloc, zends):
-    steps, _, lines = gpy.shape
-    s = ss[steps - 1]
-    q = qq[0] + gsy[0] * strided(rt, 0, SUB, steps)
     row = lax.broadcasted_iota(jnp.int32, (SUB, lines), 0)
     so, qo = jnp.zeros_like(s), jnp.zeros_like(q)
     for j in range(1, SUB):
@@ -185,7 +214,8 @@
         qo = qo + jnp.where(row < SUB - j, pltpu.roll(q, SUB - j, 0), 0.0)
     w = 1.0 / ymat[3:4, :]
     for t in range(steps):
-        vloc[t] = gsy[t] * w * (ss[t] + so) + gpy[t] * w * (qq[t] + qo)
+        rt[pl.ds(t, SUB, stride=steps), :] = gsy[t] * w * (ss[t] + so) + gpy[t] * w * (qq[t] + qo)
+    rz0[...] = rt[...].T - 2.0 * u[...]
     under = jnp.where(lax.axis_index("gz") > 0, 0.0, 1.0)
     over = jnp.where(lax.axis_index("gz") < peers - 1, 1.0, 0.0)
     zends[0] = zmat[0] + under * 4.0 / low[1]
@@ -194,8 +224,8 @@
     zends[2] = zmat[2] + 4.0 / (above * over + high[1])
 
 
-def y_finish_kernel(m0, m1, m2, m3, vloc, gpy, gsy, u, gpz, gsz, zends, rz, own, buf, vt):
-    steps, _, lines = gpy.shape
+def y_finish_kernel(m0, m1, m2, m3, rz0, gp_rows, gs_rows, gpz, gsz, zends, rz, own, buf):
+    lines = m0.shape[1]
     planes = own.shape[1]
     depth = lines // planes
     got = (m0, m1, m2, m3)
@@ -227,15 +257,13 @@
     inv = 1.0 / (left * right - c * c)
     ql = ((el - a) * right - c * (er - d)) * inv
     qr = ((er - d) * left - c * (el - a)) * inv
-    for t in range(steps):
-        vt[pl.ds(t, SUB, stride=steps), :] = vloc[t] + gsy[t] * ql + gpy[t] * qr
-    v = vt[...].T
+    flux = jnp.concatenate([ql, qr, jnp.zeros((6, lines), F32)], 0).T
     for p in range(planes):
-        i = p * depth
-        r = v[i : i + depth, :] - 2.0 * u[i : i + depth, :]
-        rz[i : i + depth, :] = r
-        own[0, p : p + 1, :] = jnp.sum(gsz[i : i + depth, :] * r, axis=0, keepdims=True)
-        own[1, p : p + 1, :] = jnp.sum(gpz[i : i + depth, :] * r, axis=0, keepdims=True)
+        rows = slice(p * depth, (p + 1) * depth)
+        r = rz0[rows, :] + gs_rows[rows, :] * flux[rows, 0:1] + gp_rows[rows, :] * flux[rows, 1:2]
+        rz[rows, :] = r
+        own[0, p : p + 1, :] = jnp.sum(gsz[rows, :] * r, axis=0, keepdims=True)
+        own[1, p : p + 1, :] = jnp.sum(gpz[rows, :] * r, axis=0, keepdims=True)
     for i in range(3):
         own[i + 2] = zends[i]
 
@@ -381,7 +409,8 @@
         k: lax.ppermute(value, axis, [(i, i ^ (k * unit) ^ (unit > 1)) for i in range(count)])
         for k in (1, 2, 3)
     }
-    got[2] = got[2] * unity()
+    got[2], got[3] = got[2] * unity(), got[3] * unity()
+    got[2] = lax.optimization_barrier(got[2]) * unity()
     return [got[k] for k in (1, 2, 3)]
 
 
@@ -421,19 +450,25 @@
         [VMEM] * 5,
         cond_x, coupling[None], u, ky, kz,
     )
+    base, gp_edge, gs_edge, gp_rows, gs_rows = call(
+        y_base_kernel, [(8, lines)] + [(2 * planes, ny)] * 2 + [flat] * 2, [(ny, lines)], 1_000_000, [VMEM] * 4,
+        r0, gpy, gsy, ymat,
+    )
     outer = outer * unity()
-    msg, rt, ss, qq = call(
-        functools.partial(y_ends_kernel, peers), [(8, lines), (ny, lines), tall, tall], [], 1_000_000, [VMEM] * 8,
-        r0, low, high, inner, outer, gpy, gsy, ymat,
+    msg, change = call(
+        functools.partial(y_ends_kernel, peers), [(8, lines), (2 * planes, ny)], [], 100_000,
+        [VMEM] * 7,
+        low, high, inner, outer, base, gp_edge, gs_edge,
     )
     others = partners(msg, "gy", 4, 1)
-    vloc, zends = call(
-        functools.partial(y_local_kernel, peers), [tall, (3, *face)], [], 1_000_000, [VMEM] * 11,
-        low, high, inner, outer, zmat, rt, ss, qq, gpy, gsy, ymat,
+    rz0, zends = call(
+        functools.partial(y_local_kernel, peers), [flat, (3, *face)], [(ny, lines), tall, tall],
+        1_000_000, [VMEM] * 11,
+        u, r0, change, low, high, inner, outer, zmat, gpy, gsy, ymat,
     )
     rz, own = call(
-        y_finish_kernel, [flat, ends], [(4, 8, lines), (ny, lines)], 1_000_000, [VMEM] * 11,
-        msg, *others, vloc, gpy, gsy, u, gpz, gsz, zends,
+        y_finish_kernel, [flat, ends], [(4, 8, lines)], 1_000_000, [VMEM] * 10,
+        msg, *others, rz0, gp_rows, gs_rows, gpz, gsz, zends,
     )
     peer = lax.ppermute(own, "gz", [(i, i ^ 1) for i in range(peers)])
     local, ready = call(z_local_kernel, [flat, (8, 128)], [], 1_000_000, [VMEM] * 5, u, rz, gpz, gsz, zmat)

time: 32.5 us -> 32 us (0.985)
  Pallas kernels: 4.14 us -> 5.18 us
  waiting for transfers between devices: 8.81 us -> 7.96 us
  starting transfers between devices: 18.6 us -> 18 us
    pallas_call x9 -> x10, Pallas kernels: 4.14 us -> 5.18 us  [call(): pl.pallas_call(kernel, out_shape=[jax.ShapeDtypeStruct(s, F32) for s in o...]
    ppermute x3, waiting for transfers between devices: 3.26 us -> 2.69 us  [partners(): lax.ppermute(value, axis, [(i, i ^ k * unit ^ (unit > 1)) for i in range(...]
    ppermute x1, starting transfers between devices: 1.94 us -> 1.58 us  [shards(): peer = lax.ppermute(own, 'gz', [(i, i ^ 1) for i in range(peers)])]
  transfers between devices with their start and end apart: 12 -> 12, of which waited for: 8 -> 7; matrix products, arithmetic and copies ran while one was open for 0% -> 0% of each run, Pallas kernels for 4% -> 8%
where the time goes in v5:
time: 32 us; the launch traced here: 31.9 us
  starting transfers between devices  18 us (56%)
  waiting for transfers between devices  7.96 us (25%)
  Pallas kernels  5.18 us (16%)
  local copies, waits for them, and re-layouts  0.68 us (2%)
    ppermute x2, starting transfers between devices, chain_of(): lax.ppermute(value, 'gz', [(i, i ^ (3 - i % 2) * unit) for i in range(cou...  6.58 us
    pallas_call x10, Pallas kernels, call(): pl.pallas_call(kernel, out_shape=[jax.ShapeDtypeStruct(s, F32) for s in o...  5.18 us
    ppermute x3, starting transfers between devices, partners(): lax.ppermute(value, axis, [(i, i ^ k * unit ^ (unit > 1)) for i in range(...  3.62 us
    ppermute x1, starting transfers between devices, shards(): lax.ppermute(outer, ('gy', 'gz'), chip_neighbours(lax.axis_size('gy'), pe...  2.77 us
    ppermute x2, waiting for transfers between devices, chain_of(): lax.ppermute(value, 'gz', [(i, i ^ (3 - i % 2) * unit) for i in range(cou...  2.75 us
    ppermute x3, waiting for transfers between devices, partners(): lax.ppermute(value, axis, [(i, i ^ k * unit ^ (unit > 1)) for i in range(...  2.69 us
    ppermute x2, starting transfers between devices, chain_of(): rest = lax.ppermute(far, 'gz', [(i, i ^ 1) for i in range(count)])  2.32 us
    ppermute x2, waiting for transfers between devices, chain_of(): near = lax.ppermute(value, 'gz', [(i, i ^ unit ^ 1) for i in range(count)])  1.58 us
  transfers between devices with their start and end apart: 12, of which 7 were waited for; matrix products, arithmetic and copies ran while one was open for 0% of the time, Pallas kernels for 8%

profile of v5, /device:TPU:1, one launch (start us, length us, event | category | flops | bytes accessed | tf_op | source)
XLA Modules:
  0.0 31.9 jit_solution(15287082027599535424)
XLA Ops:
  0.0 1.1 %shard_map.55 = (f32[128,512]{1,0:T(8,128)S(1)}, f32[128,512]{1,0:T(8,128)S(1)}, f32[128,512]{1,0:T(8,128)S(1)}, f32[2,4,512]{2,1,0:T(4,128)S(1)}, f32[2,4,512]{...) custom-call(f32[128,512]{1,0:T(8,128)} %bitcast.10, f32[128,512]{1,0:T(8,128)} %bitcast.11, ...), custom_call_target="tpu_custom_call" | custom-call | flops 100000 | bytes 25000 | tf_op jit(solution)/shard_map/pallas_call | solution.py:291
  1.1 2.8 %collective-permute-start.1 = (f32[2,4,512]{2,1,0:T(4,128)S(1)}, f32[2,4,512]{2,1,0:T(4,128)S(1)}, u32[]{:S(2)}, u32[]{:S(2)}) collective-permute-start(f32[2,4,512]{2,1,0:T(4,128)S(1)} %get-tuple-element.35), channel_id=1, source_target_pairs={{0,32},{1,2},{2,1},{3,4},{4,3},{5,6},{6,5},{7,8},{8,7},{9,10},{10,... | collective-permute-start | bytes 49160 | tf_op jit(solution)/shard_map/ppermute | solution.py:444
  3.9 0.7 %collective-permute-start = (f32[2,4,512]{2,1,0:T(4,128)S(1)}, f32[2,4,512]{2,1,0:T(4,128)S(1)}, u32[]{:S(2)}, u32[]{:S(2)}) collective-permute-start(f32[2,4,512]{2,1,0:T(4,128)S(1)} %get-tuple-element.34), channel_id=1, source_target_pairs={{0,1},{1,0},{2,3},{3,2},{4,5},{5,4},{6,7},{7,6},{8,9},{9,8},{10,11... | collective-permute-start | bytes 49160 | tf_op jit(solution)/shard_map/ppermute | solution.py:443
  4.6 0.0 copy-start
  4.6 0.0 copy-start.1
  4.6 0.7 %copy-done = f32[2,2]{1,0:T(2,128)S(1)} copy-done((f32[2,2]{1,0:T(2,128)S(1)}, f32[2,2]{1,0:T(2,128)}, u32[]{:S(2)}) %copy-start) | copy-done | bytes 40
  5.3 0.0 copy-done.1
  5.3 1.0 %shard_map.56 = (f32[64,8,128]{2,1,0:T(8,128)S(1)}, f32[64,8,128]{2,1,0:T(8,128)S(1)}, f32[8,128]{1,0:T(8,128)S(1)}, f32[128,512]{1,0:T(8,128)S(1)}, f32[128,512...) custom-call(f32[2,2]{1,0:T(2,128)S(1)} %copy-done, f32[1,2]{1,0:T(1,128)S(1)} %bitcast.9, ...), custom_call_target="tpu_custom_call" | custom-call | flops 4000000 | bytes 1000000 | tf_op jit(solution)/shard_map/pallas_call | solution.py:291
  6.3 0.8 %shard_map.57 = (f32[8,128]{1,0:T(8,128)S(1)}, f32[8,512]{1,0:T(8,128)S(1)}, f32[8,512]{1,0:T(8,128)S(1)}, f32[128,512]{1,0:T(8,128)S(1)}, f32[128,512]{1,0:T(8,128)S(1)}) custom-call(f32[128,512]{1,0:T(8,128)S(1)} %get-tuple-element.39.r0, f32[64,8,128]{2,1,0:T(8,128)S(1)} %get-tuple-element.40.gpy, f32[64,8,128]{2,1,0:T(8,128)S(1)} %get-tuple-element.41.gsy, ...), custom_call_target="tpu_custom_call" | custom-call | flops 1000000 | bytes 250000 | tf_op jit(solution)/shard_map/pallas_call | solution.py:291
  7.1 0.0 collective-permute-done.1
  7.2 0.0 collective-permute-done.inner
  7.2 0.1 shard_map.58
  7.3 3.3 %collective-permute-start.3 = (f32[8,128]{1,0:T(8,128)S(1)}, f32[8,128]{1,0:T(8,128)S(1)}, u32[]{:S(2)}, u32[]{:S(2)}) collective-permute-start(f32[8,128]{1,0:T(8,128)S(1)} %get-tuple-element.46.m0), channel_id=1, source_target_pairs={{0,64},{32,96},{64,0},{96,32},{1,65},{33,97},{65,1},{97,33},{2,66}... | collective-permute-start | bytes 12296 | tf_op jit(solution)/shard_map/ppermute | solution.py:409
  10.6 0.0 collective-permute-start.4
  10.6 0.3 collective-permute-start.2
  10.9 0.7 %shard_map.59 = (f32[128,512]{1,0:T(8,128)S(1)}, f32[3,4,512]{2,1,0:T(4,128)S(1)}) custom-call(f32[128,512]{1,0:T(8,128)S(1)} %get-tuple-element.36.u, f32[128,512]{1,0:T(8,128)S(1)} %get-tuple-element.39.r0, f32[8,512]{1,0:T(8,128)S(1)} %get-tuple-element.47.change, f32[2,4,512]{2,1,0:T(4,128)S(1)} %get-tuple-element.32.low, ...), custom_call_target="tpu_custom_call" | custom-call | flops 1000000 | bytes 250000 | tf_op jit(solution)/shard_map/pallas_call | solution.py:291
  11.6 0.0 collective-permute-done.3
  11.6 2.7 %collective-permute-done.4 = f32[8,128]{1,0:T(8,128)S(1)} collective-permute-done((f32[8,128]{1,0:T(8,128)S(1)}, f32[8,128]{1,0:T(8,128)S(1)}, u32[]{:S(2)}, u32[]{:S(2)}) %collective-permute-start.4) | collective-permute-done | bytes 4128 | tf_op jit(solution)/shard_map/ppermute | solution.py:409
  14.3 0.0 collective-permute-done.2.m1
  14.3 0.3 shard_map.60
  14.6 1.6 %collective-permute-start.5 = (f32[5,4,512]{2,1,0:T(4,128)S(1)}, f32[5,4,512]{2,1,0:T(4,128)S(1)}, u32[]{:S(2)}, u32[]{:S(2)}) collective-permute-start(f32[5,4,512]{2,1,0:T(4,128)S(1)} %get-tuple-element.55.own), channel_id=1, source_target_pairs={{0,1},{1,0},{2,3},{3,2},{4,5},{5,4},{6,7},{7,6},{8,9},{9,8},{10,11... | collective-permute-start | bytes 122888 | tf_op jit(solution)/shard_map/ppermute | solution.py:473
  16.2 0.2 shard_map.61
  16.4 0.6 %collective-permute-done.5.peer = f32[5,4,512]{2,1,0:T(4,128)S(1)} collective-permute-done((f32[5,4,512]{2,1,0:T(4,128)S(1)}, f32[5,4,512]{2,1,0:T(4,128)S(1)}, u32[]{:S(2)}, u32[]{:S(2)}) %collective-permute-start.5) | collective-permute-done | bytes 40992 | tf_op jit(solution)/shard_map/ppermute | solution.py:473
  17.1 2.7 %collective-permute-start.7 = (f32[5,4,512]{2,1,0:T(4,128)S(1)}, f32[5,4,512]{2,1,0:T(4,128)S(1)}, u32[]{:S(2)}, u32[]{:S(2)}) collective-permute-start(f32[5,4,512]{2,1,0:T(4,128)S(1)} %shard_map.62.m0.c0), channel_id=1, source_target_pairs={{0,6},{1,5},{2,4},{3,7},{4,2},{5,1},{6,0},{7,3},{8,14},{9,13},{10,... | collective-permute-start | bytes 122888 | tf_op jit(solution)/shard_map/ppermute | solution.py:393
  19.8 0.2 collective-permute-start.6
  20.0 1.5 %collective-permute-done.7.m2.c2 = f32[5,4,512]{2,1,0:T(4,128)S(1)} collective-permute-done((f32[5,4,512]{2,1,0:T(4,128)S(1)}, f32[5,4,512]{2,1,0:T(4,128)S(1)}, u32[]{:S(2)}, u32[]{:S(2)}) %collective-permute-start.7) | collective-permute-done | bytes 40992 | tf_op jit(solution)/shard_map/ppermute | solution.py:393
  21.5 1.2 %collective-permute-start.8 = (f32[5,4,512]{2,1,0:T(4,128)S(1)}, f32[5,4,512]{2,1,0:T(4,128)S(1)}, u32[]{:S(2)}, u32[]{:S(2)}) collective-permute-start(f32[5,4,512]{2,1,0:T(4,128)S(1)} %collective-permute-done.7.m2.c2), channel_id=1, source_target_pairs={{0,1},{1,0},{2,3},{3,2},{4,5},{5,4},{6,7},{7,6},{8,9},{9,8},{10,11... | collective-permute-start | bytes 122888 | tf_op jit(solution)/shard_map/ppermute | solution.py:395
  22.7 0.6 %collective-permute-done.6.m1.c1 = f32[5,4,512]{2,1,0:T(4,128)S(1)} collective-permute-done((f32[5,4,512]{2,1,0:T(4,128)S(1)}, f32[5,4,512]{2,1,0:T(4,128)S(1)}, u32[]{:S(2)}, u32[]{:S(2)}) %collective-permute-start.6) | collective-permute-done | bytes 40992 | tf_op jit(solution)/shard_map/ppermute | solution.py:394
  23.3 0.3 collective-permute-done.8.m3.c3
  23.6 3.9 %collective-permute-start.10 = (f32[5,4,512]{2,1,0:T(4,128)S(1)}, f32[5,4,512]{2,1,0:T(4,128)S(1)}, u32[]{:S(2)}, u32[]{:S(2)}) collective-permute-start(f32[5,4,512]{2,1,0:T(4,128)S(1)} %shard_map.63.p0), channel_id=1, source_target_pairs={{0,24},{1,17},{2,26},{3,19},{4,28},{5,21},{6,30},{7,23},{8,16},{9,... | collective-permute-start | bytes 122888 | tf_op jit(solution)/shard_map/ppermute | solution.py:393
  27.5 0.2 collective-permute-start.9
  27.7 1.2 %collective-permute-done.10.p2 = f32[5,4,512]{2,1,0:T(4,128)S(1)} collective-permute-done((f32[5,4,512]{2,1,0:T(4,128)S(1)}, f32[5,4,512]{2,1,0:T(4,128)S(1)}, u32[]{:S(2)}, u32[]{:S(2)}) %collective-permute-start.10) | collective-permute-done | bytes 40992 | tf_op jit(solution)/shard_map/ppermute | solution.py:393
  28.9 1.1 %collective-permute-start.11 = (f32[5,4,512]{2,1,0:T(4,128)S(1)}, f32[5,4,512]{2,1,0:T(4,128)S(1)}, u32[]{:S(2)}, u32[]{:S(2)}) collective-permute-start(f32[5,4,512]{2,1,0:T(4,128)S(1)} %collective-permute-done.10.p2), channel_id=1, source_target_pairs={{0,1},{1,0},{2,3},{3,2},{4,5},{5,4},{6,7},{7,6},{8,9},{9,8},{10,11... | collective-permute-start | bytes 122888 | tf_op jit(solution)/shard_map/ppermute | solution.py:395
  30.0 1.0 %collective-permute-done.9.p1 = f32[5,4,512]{2,1,0:T(4,128)S(1)} collective-permute-done((f32[5,4,512]{2,1,0:T(4,128)S(1)}, f32[5,4,512]{2,1,0:T(4,128)S(1)}, u32[]{:S(2)}, u32[]{:S(2)}) %collective-permute-start.9) | collective-permute-done | bytes 40992 | tf_op jit(solution)/shard_map/ppermute | solution.py:394
  31.0 0.0 collective-permute-done.11.p3
  31.1 0.9 %shard_map.64 = f32[128,512]{1,0:T(8,128)} custom-call(f32[5,4,512]{2,1,0:T(4,128)S(1)} %get-tuple-element.55.own, f32[5,4,512]{2,1,0:T(4,128)S(1)} %collective-permute-done.5.peer, f32[5,4,512]{2,1,0:T(4,128)S(1)} %shard_map.62.m0.c0, f32[5,4,512]{2,1,0:T(4,128)S(1)} %collective-permute-done.6.m1.c1, f32[5,4,512]{2,1,0:T(4,128)S(1)} %collective-permute-done.7.m2.c2, ...), custom_call_target="tpu_custom_call" | custom-call | flops 1000000 | bytes 250000 | tf_op jit(solution)/shard_map/pallas_call | solution.py:291
  (6 shorter events, 0.1 us)
Async XLA Ops:
  1.1 6.0 %collective-permute-start.1 = (f32[2,4,512]{2,1,0:T(4,128)S(1)}, f32[2,4,512]{2,1,0:T(4,128)S(1)}, u32[]{:S(2)}, u32[]{:S(2)}) collective-permute-start(f32[2,4,512]{2,1,0:T(4,128)S(1)} %get-tuple-element.35), channel_id=1, source_target_pairs={{0,32},{1,2},{2,1},{3,4},{4,3},{5,6},{6,5},{7,8},{8,7},{9,10},{10,... | collective-permute-start | bytes 49160 | tf_op jit(solution)/shard_map/ppermute | solution.py:444
  3.9 3.3 %collective-permute-start = (f32[2,4,512]{2,1,0:T(4,128)S(1)}, f32[2,4,512]{2,1,0:T(4,128)S(1)}, u32[]{:S(2)}, u32[]{:S(2)}) collective-permute-start(f32[2,4,512]{2,1,0:T(4,128)S(1)} %get-tuple-element.34), channel_id=1, source_target_pairs={{0,1},{1,0},{2,3},{3,2},{4,5},{5,4},{6,7},{7,6},{8,9},{9,8},{10,11... | collective-permute-start | bytes 49160 | tf_op jit(solution)/shard_map/ppermute | solution.py:443
  4.6 0.7 %copy-start = (f32[2,2]{1,0:T(2,128)S(1)}, f32[2,2]{1,0:T(2,128)}, u32[]{:S(2)}) copy-start(f32[2,2]{1,0:T(2,128)} %cx.1) | copy-start | bytes 52
  4.6 0.7 %copy-start.1 = (f32[2]{0:T(128)S(1)}, f32[2]{0:T(128)}, u32[]{:S(2)}) copy-start(f32[2]{0:T(128)} %param.9) | copy-start | bytes 28
  7.3 4.3 %collective-permute-start.3 = (f32[8,128]{1,0:T(8,128)S(1)}, f32[8,128]{1,0:T(8,128)S(1)}, u32[]{:S(2)}, u32[]{:S(2)}) collective-permute-start(f32[8,128]{1,0:T(8,128)S(1)} %get-tuple-element.46.m0), channel_id=1, source_target_pairs={{0,64},{32,96},{64,0},{96,32},{1,65},{33,97},{65,1},{97,33},{2,66}... | collective-permute-start | bytes 12296 | tf_op jit(solution)/shard_map/ppermute | solution.py:409
  10.6 3.7 %collective-permute-start.4 = (f32[8,128]{1,0:T(8,128)S(1)}, f32[8,128]{1,0:T(8,128)S(1)}, u32[]{:S(2)}, u32[]{:S(2)}) collective-permute-start(f32[8,128]{1,0:T(8,128)S(1)} %get-tuple-element.46.m0), channel_id=1, source_target_pairs={{0,96},{32,64},{64,32},{96,0},{1,97},{33,65},{65,33},{97,1},{2,98}... | collective-permute-start | bytes 12296 | tf_op jit(solution)/shard_map/ppermute | solution.py:409
  10.6 3.7 %collective-permute-start.2 = (f32[8,128]{1,0:T(8,128)S(1)}, f32[8,128]{1,0:T(8,128)S(1)}, u32[]{:S(2)}, u32[]{:S(2)}) collective-permute-start(f32[8,128]{1,0:T(8,128)S(1)} %get-tuple-element.46.m0), channel_id=1, source_target_pairs={{0,32},{32,0},{64,96},{96,64},{1,33},{33,1},{65,97},{97,65},{2,34}... | collective-permute-start | bytes 12296 | tf_op jit(solution)/shard_map/ppermute | solution.py:409
  14.6 2.4 %collective-permute-start.5 = (f32[5,4,512]{2,1,0:T(4,128)S(1)}, f32[5,4,512]{2,1,0:T(4,128)S(1)}, u32[]{:S(2)}, u32[]{:S(2)}) collective-permute-start(f32[5,4,512]{2,1,0:T(4,128)S(1)} %get-tuple-element.55.own), channel_id=1, source_target_pairs={{0,1},{1,0},{2,3},{3,2},{4,5},{5,4},{6,7},{7,6},{8,9},{9,8},{10,11... | collective-permute-start | bytes 122888 | tf_op jit(solution)/shard_map/ppermute | solution.py:473
  17.1 4.4 %collective-permute-start.7 = (f32[5,4,512]{2,1,0:T(4,128)S(1)}, f32[5,4,512]{2,1,0:T(4,128)S(1)}, u32[]{:S(2)}, u32[]{:S(2)}) collective-permute-start(f32[5,4,512]{2,1,0:T(4,128)S(1)} %shard_map.62.m0.c0), channel_id=1, source_target_pairs={{0,6},{1,5},{2,4},{3,7},{4,2},{5,1},{6,0},{7,3},{8,14},{9,13},{10,... | collective-permute-start | bytes 122888 | tf_op jit(solution)/shard_map/ppermute | solution.py:393
  19.8 3.5 %collective-permute-start.6 = (f32[5,4,512]{2,1,0:T(4,128)S(1)}, f32[5,4,512]{2,1,0:T(4,128)S(1)}, u32[]{:S(2)}, u32[]{:S(2)}) collective-permute-start(f32[5,4,512]{2,1,0:T(4,128)S(1)} %shard_map.62.m0.c0), channel_id=1, source_target_pairs={{0,3},{1,2},{2,1},{3,0},{4,7},{5,6},{6,5},{7,4},{8,11},{9,10},{10,... | collective-permute-start | bytes 122888 | tf_op jit(solution)/shard_map/ppermute | solution.py:394
  21.5 2.1 %collective-permute-start.8 = (f32[5,4,512]{2,1,0:T(4,128)S(1)}, f32[5,4,512]{2,1,0:T(4,128)S(1)}, u32[]{:S(2)}, u32[]{:S(2)}) collective-permute-start(f32[5,4,512]{2,1,0:T(4,128)S(1)} %collective-permute-done.7.m2.c2), channel_id=1, source_target_pairs={{0,1},{1,0},{2,3},{3,2},{4,5},{5,4},{6,7},{7,6},{8,9},{9,8},{10,11... | collective-permute-start | bytes 122888 | tf_op jit(solution)/shard_map/ppermute | solution.py:395
  23.6 5.3 %collective-permute-start.10 = (f32[5,4,512]{2,1,0:T(4,128)S(1)}, f32[5,4,512]{2,1,0:T(4,128)S(1)}, u32[]{:S(2)}, u32[]{:S(2)}) collective-permute-start(f32[5,4,512]{2,1,0:T(4,128)S(1)} %shard_map.63.p0), channel_id=1, source_target_pairs={{0,24},{1,17},{2,26},{3,19},{4,28},{5,21},{6,30},{7,23},{8,16},{9,... | collective-permute-start | bytes 122888 | tf_op jit(solution)/shard_map/ppermute | solution.py:393
  27.5 3.5 %collective-permute-start.9 = (f32[5,4,512]{2,1,0:T(4,128)S(1)}, f32[5,4,512]{2,1,0:T(4,128)S(1)}, u32[]{:S(2)}, u32[]{:S(2)}) collective-permute-start(f32[5,4,512]{2,1,0:T(4,128)S(1)} %shard_map.63.p0), channel_id=1, source_target_pairs={{0,9},{1,8},{2,11},{3,10},{4,13},{5,12},{6,15},{7,14},{8,1},{9,0},... | collective-permute-start | bytes 122888 | tf_op jit(solution)/shard_map/ppermute | solution.py:394
  28.9 2.1 %collective-permute-start.11 = (f32[5,4,512]{2,1,0:T(4,128)S(1)}, f32[5,4,512]{2,1,0:T(4,128)S(1)}, u32[]{:S(2)}, u32[]{:S(2)}) collective-permute-start(f32[5,4,512]{2,1,0:T(4,128)S(1)} %collective-permute-done.10.p2), channel_id=1, source_target_pairs={{0,1},{1,0},{2,3},{3,2},{4,5},{5,4},{6,7},{7,6},{8,9},{9,8},{10,11... | collective-permute-start | bytes 122888 | tf_op jit(solution)/shard_map/ppermute | solution.py:395

commit v6 on v5

--- a/solution.py
+++ b/solution.py
@@ -391,7 +391,7 @@
 
 def chain_of(value, count, unit):
     far = lax.ppermute(value, "gz", [(i, i ^ ((3 - i % 2) * unit)) for i in range(count)])
-    near = lax.ppermute(value, "gz", [(i, i ^ unit ^ 1) for i in range(count)])
+    near = lax.ppermute(value, "gz", [(i, i ^ unit) for i in range(count)])
     rest = lax.ppermute(far, "gz", [(i, i ^ 1) for i in range(count)])
     return [value, near, far, rest]
 

time: 32 us -> 31.9 us (level)
  waiting for transfers between devices: 7.96 us -> 7.62 us
    ppermute x2, waiting for transfers between devices: 1.58 us -> 0.33 us  [chain_of(): near = lax.ppermute(value, 'gz', [(i, i ^ unit) for i in range(count)])]
    ppermute x2, waiting for transfers between devices: 0.32 us -> 1.41 us  [chain_of(): rest = lax.ppermute(far, 'gz', [(i, i ^ 1) for i in range(count)])]
  transfers between devices with their start and end apart: 12 -> 12, of which waited for: 7 -> 7; matrix products, arithmetic and copies ran while one was open for 0% -> 0% of each run, Pallas kernels for 8% -> 9%
where the time goes in v6:
time: 31.9 us; the launch traced here: 31.7 us
  starting transfers between devices  18.2 us (57%)
  waiting for transfers between devices  7.62 us (24%)
  Pallas kernels  5.18 us (16%)
  local copies, waits for them, and re-layouts  0.68 us (2%)
    ppermute x2, starting transfers between devices, chain_of(): lax.ppermute(value, 'gz', [(i, i ^ (3 - i % 2) * unit) for i in range(cou...  6.58 us
    pallas_call x10, Pallas kernels, call(): pl.pallas_call(kernel, out_shape=[jax.ShapeDtypeStruct(s, F32) for s in o...  5.18 us
    ppermute x3, starting transfers between devices, partners(): lax.ppermute(value, axis, [(i, i ^ k * unit ^ (unit > 1)) for i in range(...  3.62 us
    ppermute x1, starting transfers between devices, shards(): lax.ppermute(outer, ('gy', 'gz'), chip_neighbours(lax.axis_size('gy'), pe...  2.77 us
    ppermute x3, waiting for transfers between devices, partners(): lax.ppermute(value, axis, [(i, i ^ k * unit ^ (unit > 1)) for i in range(...  2.69 us
    ppermute x2, waiting for transfers between devices, chain_of(): lax.ppermute(value, 'gz', [(i, i ^ (3 - i % 2) * unit) for i in range(cou...  2.57 us
    ppermute x2, starting transfers between devices, chain_of(): rest = lax.ppermute(far, 'gz', [(i, i ^ 1) for i in range(count)])  2.32 us
    ppermute x1, starting transfers between devices, shards(): peer = lax.ppermute(own, 'gz', [(i, i ^ 1) for i in range(peers)])  1.58 us
  transfers between devices with their start and end apart: 12, of which 7 were waited for; matrix products, arithmetic and copies ran while one was open for 0% of the time, Pallas kernels for 9%

profile of v6, /device:TPU:1, one launch (start us, length us, event | category | flops | bytes accessed | tf_op | source)
XLA Modules:
  0.0 31.7 jit_solution(12400043926268362618)
XLA Ops:
  0.0 1.1 %shard_map.55 = (f32[128,512]{1,0:T(8,128)S(1)}, f32[128,512]{1,0:T(8,128)S(1)}, f32[128,512]{1,0:T(8,128)S(1)}, f32[2,4,512]{2,1,0:T(4,128)S(1)}, f32[2,4,512]{...) custom-call(f32[128,512]{1,0:T(8,128)} %bitcast.10, f32[128,512]{1,0:T(8,128)} %bitcast.11, ...), custom_call_target="tpu_custom_call" | custom-call | flops 100000 | bytes 25000 | tf_op jit(solution)/shard_map/pallas_call | solution.py:291
  1.1 2.8 %collective-permute-start.1 = (f32[2,4,512]{2,1,0:T(4,128)S(1)}, f32[2,4,512]{2,1,0:T(4,128)S(1)}, u32[]{:S(2)}, u32[]{:S(2)}) collective-permute-start(f32[2,4,512]{2,1,0:T(4,128)S(1)} %get-tuple-element.35), channel_id=1, source_target_pairs={{0,32},{1,2},{2,1},{3,4},{4,3},{5,6},{6,5},{7,8},{8,7},{9,10},{10,... | collective-permute-start | bytes 49160 | tf_op jit(solution)/shard_map/ppermute | solution.py:444
  3.9 0.7 %collective-permute-start = (f32[2,4,512]{2,1,0:T(4,128)S(1)}, f32[2,4,512]{2,1,0:T(4,128)S(1)}, u32[]{:S(2)}, u32[]{:S(2)}) collective-permute-start(f32[2,4,512]{2,1,0:T(4,128)S(1)} %get-tuple-element.34), channel_id=1, source_target_pairs={{0,1},{1,0},{2,3},{3,2},{4,5},{5,4},{6,7},{7,6},{8,9},{9,8},{10,11... | collective-permute-start | bytes 49160 | tf_op jit(solution)/shard_map/ppermute | solution.py:443
  4.6 0.0 copy-start
  4.6 0.0 copy-start.1
  4.6 0.7 %copy-done = f32[2,2]{1,0:T(2,128)S(1)} copy-done((f32[2,2]{1,0:T(2,128)S(1)}, f32[2,2]{1,0:T(2,128)}, u32[]{:S(2)}) %copy-start) | copy-done | bytes 40
  5.3 0.0 copy-done.1
  5.3 1.0 %shard_map.56 = (f32[64,8,128]{2,1,0:T(8,128)S(1)}, f32[64,8,128]{2,1,0:T(8,128)S(1)}, f32[8,128]{1,0:T(8,128)S(1)}, f32[128,512]{1,0:T(8,128)S(1)}, f32[128,512...) custom-call(f32[2,2]{1,0:T(2,128)S(1)} %copy-done, f32[1,2]{1,0:T(1,128)S(1)} %bitcast.9, ...), custom_call_target="tpu_custom_call" | custom-call | flops 4000000 | bytes 1000000 | tf_op jit(solution)/shard_map/pallas_call | solution.py:291
  6.3 0.8 %shard_map.57 = (f32[8,128]{1,0:T(8,128)S(1)}, f32[8,512]{1,0:T(8,128)S(1)}, f32[8,512]{1,0:T(8,128)S(1)}, f32[128,512]{1,0:T(8,128)S(1)}, f32[128,512]{1,0:T(8,128)S(1)}) custom-call(f32[128,512]{1,0:T(8,128)S(1)} %get-tuple-element.39.r0, f32[64,8,128]{2,1,0:T(8,128)S(1)} %get-tuple-element.40.gpy, f32[64,8,128]{2,1,0:T(8,128)S(1)} %get-tuple-element.41.gsy, ...), custom_call_target="tpu_custom_call" | custom-call | flops 1000000 | bytes 250000 | tf_op jit(solution)/shard_map/pallas_call | solution.py:291
  7.1 0.0 collective-permute-done.1
  7.2 0.0 collective-permute-done.inner
  7.2 0.1 shard_map.58
  7.3 3.3 %collective-permute-start.3 = (f32[8,128]{1,0:T(8,128)S(1)}, f32[8,128]{1,0:T(8,128)S(1)}, u32[]{:S(2)}, u32[]{:S(2)}) collective-permute-start(f32[8,128]{1,0:T(8,128)S(1)} %get-tuple-element.46.m0), channel_id=1, source_target_pairs={{0,64},{32,96},{64,0},{96,32},{1,65},{33,97},{65,1},{97,33},{2,66}... | collective-permute-start | bytes 12296 | tf_op jit(solution)/shard_map/ppermute | solution.py:409
  10.6 0.0 collective-permute-start.4
  10.6 0.3 collective-permute-start.2
  10.9 0.7 %shard_map.59 = (f32[128,512]{1,0:T(8,128)S(1)}, f32[3,4,512]{2,1,0:T(4,128)S(1)}) custom-call(f32[128,512]{1,0:T(8,128)S(1)} %get-tuple-element.36.u, f32[128,512]{1,0:T(8,128)S(1)} %get-tuple-element.39.r0, f32[8,512]{1,0:T(8,128)S(1)} %get-tuple-element.47.change, f32[2,4,512]{2,1,0:T(4,128)S(1)} %get-tuple-element.32.low, ...), custom_call_target="tpu_custom_call" | custom-call | flops 1000000 | bytes 250000 | tf_op jit(solution)/shard_map/pallas_call | solution.py:291
  11.6 0.0 collective-permute-done.3
  11.6 2.7 %collective-permute-done.4 = f32[8,128]{1,0:T(8,128)S(1)} collective-permute-done((f32[8,128]{1,0:T(8,128)S(1)}, f32[8,128]{1,0:T(8,128)S(1)}, u32[]{:S(2)}, u32[]{:S(2)}) %collective-permute-start.4) | collective-permute-done | bytes 4128 | tf_op jit(solution)/shard_map/ppermute | solution.py:409
  14.3 0.0 collective-permute-done.2.m1
  14.3 0.3 shard_map.60
  14.6 1.6 %collective-permute-start.5 = (f32[5,4,512]{2,1,0:T(4,128)S(1)}, f32[5,4,512]{2,1,0:T(4,128)S(1)}, u32[]{:S(2)}, u32[]{:S(2)}) collective-permute-start(f32[5,4,512]{2,1,0:T(4,128)S(1)} %get-tuple-element.55.own), channel_id=1, source_target_pairs={{0,1},{1,0},{2,3},{3,2},{4,5},{5,4},{6,7},{7,6},{8,9},{9,8},{10,11... | collective-permute-start | bytes 122888 | tf_op jit(solution)/shard_map/ppermute | solution.py:473
  16.2 0.2 shard_map.61
  16.4 0.6 %collective-permute-done.5.peer = f32[5,4,512]{2,1,0:T(4,128)S(1)} collective-permute-done((f32[5,4,512]{2,1,0:T(4,128)S(1)}, f32[5,4,512]{2,1,0:T(4,128)S(1)}, u32[]{:S(2)}, u32[]{:S(2)}) %collective-permute-start.5) | collective-permute-done | bytes 40992 | tf_op jit(solution)/shard_map/ppermute | solution.py:473
  17.1 2.7 %collective-permute-start.7 = (f32[5,4,512]{2,1,0:T(4,128)S(1)}, f32[5,4,512]{2,1,0:T(4,128)S(1)}, u32[]{:S(2)}, u32[]{:S(2)}) collective-permute-start(f32[5,4,512]{2,1,0:T(4,128)S(1)} %shard_map.62.m0.c0), channel_id=1, source_target_pairs={{0,6},{1,5},{2,4},{3,7},{4,2},{5,1},{6,0},{7,3},{8,14},{9,13},{10,... | collective-permute-start | bytes 122888 | tf_op jit(solution)/shard_map/ppermute | solution.py:393
  19.8 0.3 collective-permute-start.6
  20.0 1.5 %collective-permute-done.7.m2.c2 = f32[5,4,512]{2,1,0:T(4,128)S(1)} collective-permute-done((f32[5,4,512]{2,1,0:T(4,128)S(1)}, f32[5,4,512]{2,1,0:T(4,128)S(1)}, u32[]{:S(2)}, u32[]{:S(2)}) %collective-permute-start.7) | collective-permute-done | bytes 40992 | tf_op jit(solution)/shard_map/ppermute | solution.py:393
  21.5 1.2 %collective-permute-start.8 = (f32[5,4,512]{2,1,0:T(4,128)S(1)}, f32[5,4,512]{2,1,0:T(4,128)S(1)}, u32[]{:S(2)}, u32[]{:S(2)}) collective-permute-start(f32[5,4,512]{2,1,0:T(4,128)S(1)} %collective-permute-done.7.m2.c2), channel_id=1, source_target_pairs={{0,1},{1,0},{2,3},{3,2},{4,5},{5,4},{6,7},{7,6},{8,9},{9,8},{10,11... | collective-permute-start | bytes 122888 | tf_op jit(solution)/shard_map/ppermute | solution.py:395
  22.7 0.0 collective-permute-done.6.m1.c1
  22.7 0.9 %collective-permute-done.8.m3.c3 = f32[5,4,512]{2,1,0:T(4,128)S(1)} collective-permute-done((f32[5,4,512]{2,1,0:T(4,128)S(1)}, f32[5,4,512]{2,1,0:T(4,128)S(1)}, u32[]{:S(2)}, u32[]{:S(2)}) %collective-permute-start.8) | collective-permute-done | bytes 40992 | tf_op jit(solution)/shard_map/ppermute | solution.py:395
  23.6 3.9 %collective-permute-start.10 = (f32[5,4,512]{2,1,0:T(4,128)S(1)}, f32[5,4,512]{2,1,0:T(4,128)S(1)}, u32[]{:S(2)}, u32[]{:S(2)}) collective-permute-start(f32[5,4,512]{2,1,0:T(4,128)S(1)} %shard_map.63.p0), channel_id=1, source_target_pairs={{0,24},{1,17},{2,26},{3,19},{4,28},{5,21},{6,30},{7,23},{8,16},{9,... | collective-permute-start | bytes 122888 | tf_op jit(solution)/shard_map/ppermute | solution.py:393
  27.5 0.3 collective-permute-start.9
  27.8 1.1 %collective-permute-done.10.p2 = f32[5,4,512]{2,1,0:T(4,128)S(1)} collective-permute-done((f32[5,4,512]{2,1,0:T(4,128)S(1)}, f32[5,4,512]{2,1,0:T(4,128)S(1)}, u32[]{:S(2)}, u32[]{:S(2)}) %collective-permute-start.10) | collective-permute-done | bytes 40992 | tf_op jit(solution)/shard_map/ppermute | solution.py:393
  28.9 1.1 %collective-permute-start.11 = (f32[5,4,512]{2,1,0:T(4,128)S(1)}, f32[5,4,512]{2,1,0:T(4,128)S(1)}, u32[]{:S(2)}, u32[]{:S(2)}) collective-permute-start(f32[5,4,512]{2,1,0:T(4,128)S(1)} %collective-permute-done.10.p2), channel_id=1, source_target_pairs={{0,1},{1,0},{2,3},{3,2},{4,5},{5,4},{6,7},{7,6},{8,9},{9,8},{10,11... | collective-permute-start | bytes 122888 | tf_op jit(solution)/shard_map/ppermute | solution.py:395
  30.0 0.3 %collective-permute-done.9.p1 = f32[5,4,512]{2,1,0:T(4,128)S(1)} collective-permute-done((f32[5,4,512]{2,1,0:T(4,128)S(1)}, f32[5,4,512]{2,1,0:T(4,128)S(1)}, u32[]{:S(2)}, u32[]{:S(2)}) %collective-permute-start.9) | collective-permute-done | bytes 40992 | tf_op jit(solution)/shard_map/ppermute | solution.py:394
  30.4 0.5 %collective-permute-done.11.p3 = f32[5,4,512]{2,1,0:T(4,128)S(1)} collective-permute-done((f32[5,4,512]{2,1,0:T(4,128)S(1)}, f32[5,4,512]{2,1,0:T(4,128)S(1)}, u32[]{:S(2)}, u32[]{:S(2)}) %collective-permute-start.11) | collective-permute-done | bytes 40992 | tf_op jit(solution)/shard_map/ppermute | solution.py:395
  30.9 0.9 %shard_map.64 = f32[128,512]{1,0:T(8,128)} custom-call(f32[5,4,512]{2,1,0:T(4,128)S(1)} %get-tuple-element.55.own, f32[5,4,512]{2,1,0:T(4,128)S(1)} %collective-permute-done.5.peer, f32[5,4,512]{2,1,0:T(4,128)S(1)} %shard_map.62.m0.c0, f32[5,4,512]{2,1,0:T(4,128)S(1)} %collective-permute-done.6.m1.c1, f32[5,4,512]{2,1,0:T(4,128)S(1)} %collective-permute-done.7.m2.c2, ...), custom_call_target="tpu_custom_call" | custom-call | flops 1000000 | bytes 250000 | tf_op jit(solution)/shard_map/pallas_call | solution.py:291
  (6 shorter events, 0.1 us)
Async XLA Ops:
  1.1 6.0 %collective-permute-start.1 = (f32[2,4,512]{2,1,0:T(4,128)S(1)}, f32[2,4,512]{2,1,0:T(4,128)S(1)}, u32[]{:S(2)}, u32[]{:S(2)}) collective-permute-start(f32[2,4,512]{2,1,0:T(4,128)S(1)} %get-tuple-element.35), channel_id=1, source_target_pairs={{0,32},{1,2},{2,1},{3,4},{4,3},{5,6},{6,5},{7,8},{8,7},{9,10},{10,... | collective-permute-start | bytes 49160 | tf_op jit(solution)/shard_map/ppermute | solution.py:444
  3.9 3.3 %collective-permute-start = (f32[2,4,512]{2,1,0:T(4,128)S(1)}, f32[2,4,512]{2,1,0:T(4,128)S(1)}, u32[]{:S(2)}, u32[]{:S(2)}) collective-permute-start(f32[2,4,512]{2,1,0:T(4,128)S(1)} %get-tuple-element.34), channel_id=1, source_target_pairs={{0,1},{1,0},{2,3},{3,2},{4,5},{5,4},{6,7},{7,6},{8,9},{9,8},{10,11... | collective-permute-start | bytes 49160 | tf_op jit(solution)/shard_map/ppermute | solution.py:443
  4.6 0.7 %copy-start = (f32[2,2]{1,0:T(2,128)S(1)}, f32[2,2]{1,0:T(2,128)}, u32[]{:S(2)}) copy-start(f32[2,2]{1,0:T(2,128)} %cx.1) | copy-start | bytes 52
  4.6 0.7 %copy-start.1 = (f32[2]{0:T(128)S(1)}, f32[2]{0:T(128)}, u32[]{:S(2)}) copy-start(f32[2]{0:T(128)} %param.9) | copy-start | bytes 28
  7.3 4.3 %collective-permute-start.3 = (f32[8,128]{1,0:T(8,128)S(1)}, f32[8,128]{1,0:T(8,128)S(1)}, u32[]{:S(2)}, u32[]{:S(2)}) collective-permute-start(f32[8,128]{1,0:T(8,128)S(1)} %get-tuple-element.46.m0), channel_id=1, source_target_pairs={{0,64},{32,96},{64,0},{96,32},{1,65},{33,97},{65,1},{97,33},{2,66}... | collective-permute-start | bytes 12296 | tf_op jit(solution)/shard_map/ppermute | solution.py:409
  10.6 3.7 %collective-permute-start.4 = (f32[8,128]{1,0:T(8,128)S(1)}, f32[8,128]{1,0:T(8,128)S(1)}, u32[]{:S(2)}, u32[]{:S(2)}) collective-permute-start(f32[8,128]{1,0:T(8,128)S(1)} %get-tuple-element.46.m0), channel_id=1, source_target_pairs={{0,96},{32,64},{64,32},{96,0},{1,97},{33,65},{65,33},{97,1},{2,98}... | collective-permute-start | bytes 12296 | tf_op jit(solution)/shard_map/ppermute | solution.py:409
  10.6 3.7 %collective-permute-start.2 = (f32[8,128]{1,0:T(8,128)S(1)}, f32[8,128]{1,0:T(8,128)S(1)}, u32[]{:S(2)}, u32[]{:S(2)}) collective-permute-start(f32[8,128]{1,0:T(8,128)S(1)} %get-tuple-element.46.m0), channel_id=1, source_target_pairs={{0,32},{32,0},{64,96},{96,64},{1,33},{33,1},{65,97},{97,65},{2,34}... | collective-permute-start | bytes 12296 | tf_op jit(solution)/shard_map/ppermute | solution.py:409
  14.6 2.4 %collective-permute-start.5 = (f32[5,4,512]{2,1,0:T(4,128)S(1)}, f32[5,4,512]{2,1,0:T(4,128)S(1)}, u32[]{:S(2)}, u32[]{:S(2)}) collective-permute-start(f32[5,4,512]{2,1,0:T(4,128)S(1)} %get-tuple-element.55.own), channel_id=1, source_target_pairs={{0,1},{1,0},{2,3},{3,2},{4,5},{5,4},{6,7},{7,6},{8,9},{9,8},{10,11... | collective-permute-start | bytes 122888 | tf_op jit(solution)/shard_map/ppermute | solution.py:473
  17.1 4.4 %collective-permute-start.7 = (f32[5,4,512]{2,1,0:T(4,128)S(1)}, f32[5,4,512]{2,1,0:T(4,128)S(1)}, u32[]{:S(2)}, u32[]{:S(2)}) collective-permute-start(f32[5,4,512]{2,1,0:T(4,128)S(1)} %shard_map.62.m0.c0), channel_id=1, source_target_pairs={{0,6},{1,5},{2,4},{3,7},{4,2},{5,1},{6,0},{7,3},{8,14},{9,13},{10,... | collective-permute-start | bytes 122888 | tf_op jit(solution)/shard_map/ppermute | solution.py:393
  19.8 2.9 %collective-permute-start.6 = (f32[5,4,512]{2,1,0:T(4,128)S(1)}, f32[5,4,512]{2,1,0:T(4,128)S(1)}, u32[]{:S(2)}, u32[]{:S(2)}) collective-permute-start(f32[5,4,512]{2,1,0:T(4,128)S(1)} %shard_map.62.m0.c0), channel_id=1, source_target_pairs={{0,2},{1,3},{2,0},{3,1},{4,6},{5,7},{6,4},{7,5},{8,10},{9,11},{10,... | collective-permute-start | bytes 122888 | tf_op jit(solution)/shard_map/ppermute | solution.py:394
  21.5 2.1 %collective-permute-start.8 = (f32[5,4,512]{2,1,0:T(4,128)S(1)}, f32[5,4,512]{2,1,0:T(4,128)S(1)}, u32[]{:S(2)}, u32[]{:S(2)}) collective-permute-start(f32[5,4,512]{2,1,0:T(4,128)S(1)} %collective-permute-done.7.m2.c2), channel_id=1, source_target_pairs={{0,1},{1,0},{2,3},{3,2},{4,5},{5,4},{6,7},{7,6},{8,9},{9,8},{10,11... | collective-permute-start | bytes 122888 | tf_op jit(solution)/shard_map/ppermute | solution.py:395
  23.6 5.3 %collective-permute-start.10 = (f32[5,4,512]{2,1,0:T(4,128)S(1)}, f32[5,4,512]{2,1,0:T(4,128)S(1)}, u32[]{:S(2)}, u32[]{:S(2)}) collective-permute-start(f32[5,4,512]{2,1,0:T(4,128)S(1)} %shard_map.63.p0), channel_id=1, source_target_pairs={{0,24},{1,17},{2,26},{3,19},{4,28},{5,21},{6,30},{7,23},{8,16},{9,... | collective-permute-start | bytes 122888 | tf_op jit(solution)/shard_map/ppermute | solution.py:393
  27.5 2.9 %collective-permute-start.9 = (f32[5,4,512]{2,1,0:T(4,128)S(1)}, f32[5,4,512]{2,1,0:T(4,128)S(1)}, u32[]{:S(2)}, u32[]{:S(2)}) collective-permute-start(f32[5,4,512]{2,1,0:T(4,128)S(1)} %shard_map.63.p0), channel_id=1, source_target_pairs={{0,8},{1,9},{2,10},{3,11},{4,12},{5,13},{6,14},{7,15},{8,0},{9,1},... | collective-permute-start | bytes 122888 | tf_op jit(solution)/shard_map/ppermute | solution.py:394
  28.9 2.0 %collective-permute-start.11 = (f32[5,4,512]{2,1,0:T(4,128)S(1)}, f32[5,4,512]{2,1,0:T(4,128)S(1)}, u32[]{:S(2)}, u32[]{:S(2)}) collective-permute-start(f32[5,4,512]{2,1,0:T(4,128)S(1)} %collective-permute-done.10.p2), channel_id=1, source_target_pairs={{0,1},{1,0},{2,3},{3,2},{4,5},{5,4},{6,7},{7,6},{8,9},{9,8},{10,11... | collective-permute-start | bytes 122888 | tf_op jit(solution)/shard_map/ppermute | solution.py:395

commit v7 on v6

--- a/solution.py
+++ b/solution.py
@@ -287,12 +287,12 @@
             q = q + gsz[at, :] * rz[at, :]
 
 
-def call(kernel, outs, scratch, cost, in_specs, *args, vmem=32):
+def call(kernel, outs, scratch, cost, in_specs, *args, vmem=32, out_spec=VMEM):
     return pl.pallas_call(
         kernel,
         out_shape=[jax.ShapeDtypeStruct(s, F32) for s in outs],
         in_specs=in_specs,
-        out_specs=[VMEM] * len(outs),
+        out_specs=[out_spec] * len(outs),
         scratch_shapes=[pltpu.VMEM(s, F32) if isinstance(s, tuple) else s for s in scratch],
         compiler_params=pltpu.CompilerParams(vmem_limit_bytes=int(vmem * 2**20)),
         cost_estimate=pl.CostEstimate(flops=cost, bytes_accessed=cost // 4, transcendentals=0),
@@ -356,7 +356,7 @@
 
 
 def finish_kernel(
-    own, peer, c0, c1, c2, c3, p0, p1, p2, p3, local, gpz, gsz, out, cbuf, pbuf
+    own, peer, c0, c1, c2, c3, p0, p1, p2, p3, local, gpz, gsz, out, cbuf, pbuf, stage, sem
 ):
     iy, ix = position_y(lax.axis_index("gz")), position_x(lax.axis_index("gz"))
     for k, (c, p) in zip(distances(lax.axis_index("gz")), ((c0, p0), (c1, p1), (c2, p2), (c3, p3))):
@@ -375,13 +375,16 @@
     ql, qr = jnp.where(lower, ql, -q), jnp.where(lower, q, qr)
     planes = ql.shape[0]
     depth = out.shape[0] // planes
+    copies = []
     for p in range(planes):
-        i = p * depth
-        out[i : i + depth, :] = (
-            local[i : i + depth, :]
-            + gsz[i : i + depth, :] * ql[p : p + 1, :]
-            + gpz[i : i + depth, :] * qr[p : p + 1, :]
+        rows = slice(p * depth, (p + 1) * depth)
+        stage[rows, :] = (
+            local[rows, :] + gsz[rows, :] * ql[p : p + 1, :] + gpz[rows, :] * qr[p : p + 1, :]
         )
+        copies.append(pltpu.make_async_copy(stage.at[rows, :], out.at[rows, :], sem.at[p]))
+        copies[-1].start()
+    for copy in copies:
+        copy.wait()
 
 
 def distances(z):
@@ -480,8 +483,8 @@
     )
     whole = chain_of(plane, peers, 8)
     [out] = call(
-        finish_kernel, [flat], [(4, *ends), (4, *ends)], 1_000_000, [VMEM] * 13,
-        own, peer, *column, *whole, local, gpz, gsz,
+        finish_kernel, [flat], [(4, *ends), (4, *ends), flat, dma((planes,))], 1_000_000, [VMEM] * 13,
+        own, peer, *column, *whole, local, gpz, gsz, out_spec=hbm,
     )
     return out.reshape(fields.shape)
 

time: 31.9 us -> 31.9 us (level)
  no operation moved by 1% of the time
where the time goes in v7:
time: 31.9 us; the launch traced here: 31.7 us
  starting transfers between devices  18.2 us (57%)
  waiting for transfers between devices  7.62 us (24%)
  Pallas kernels  5.16 us (16%)
  local copies, waits for them, and re-layouts  0.68 us (2%)
    ppermute x2, starting transfers between devices, chain_of(): lax.ppermute(value, 'gz', [(i, i ^ (3 - i % 2) * unit) for i in range(cou...  6.58 us
    pallas_call x10, Pallas kernels, call(): pl.pallas_call(kernel, out_shape=[jax.ShapeDtypeStruct(s, F32) for s in o...  5.16 us
    ppermute x3, starting transfers between devices, partners(): lax.ppermute(value, axis, [(i, i ^ k * unit ^ (unit > 1)) for i in range(...  3.62 us
    ppermute x1, starting transfers between devices, shards(): lax.ppermute(outer, ('gy', 'gz'), chip_neighbours(lax.axis_size('gy'), pe...  2.77 us
    ppermute x3, waiting for transfers between devices, partners(): lax.ppermute(value, axis, [(i, i ^ k * unit ^ (unit > 1)) for i in range(...  2.69 us
    ppermute x2, waiting for transfers between devices, chain_of(): lax.ppermute(value, 'gz', [(i, i ^ (3 - i % 2) * unit) for i in range(cou...  2.57 us
    ppermute x2, starting transfers between devices, chain_of(): rest = lax.ppermute(far, 'gz', [(i, i ^ 1) for i in range(count)])  2.32 us
    ppermute x1, starting transfers between devices, shards(): peer = lax.ppermute(own, 'gz', [(i, i ^ 1) for i in range(peers)])  1.58 us
  transfers between devices with their start and end apart: 12, of which 7 were waited for; matrix products, arithmetic and copies ran while one was open for 0% of the time, Pallas kernels for 9%

profile of v7, /device:TPU:1, one launch (start us, length us, event | category | flops | bytes accessed | tf_op | source)
XLA Modules:
  0.0 31.7 jit_solution(12349124495369943261)
XLA Ops:
  0.0 1.1 %shard_map.55 = (f32[128,512]{1,0:T(8,128)S(1)}, f32[128,512]{1,0:T(8,128)S(1)}, f32[128,512]{1,0:T(8,128)S(1)}, f32[2,4,512]{2,1,0:T(4,128)S(1)}, f32[2,4,512]{...) custom-call(f32[128,512]{1,0:T(8,128)} %bitcast.10, f32[128,512]{1,0:T(8,128)} %bitcast.11, ...), custom_call_target="tpu_custom_call" | custom-call | flops 100000 | bytes 25000 | tf_op jit(solution)/shard_map/pallas_call | solution.py:291
  1.1 2.8 %collective-permute-start.1 = (f32[2,4,512]{2,1,0:T(4,128)S(1)}, f32[2,4,512]{2,1,0:T(4,128)S(1)}, u32[]{:S(2)}, u32[]{:S(2)}) collective-permute-start(f32[2,4,512]{2,1,0:T(4,128)S(1)} %get-tuple-element.35), channel_id=1, source_target_pairs={{0,32},{1,2},{2,1},{3,4},{4,3},{5,6},{6,5},{7,8},{8,7},{9,10},{10,... | collective-permute-start | bytes 49160 | tf_op jit(solution)/shard_map/ppermute | solution.py:447
  3.9 0.7 %collective-permute-start = (f32[2,4,512]{2,1,0:T(4,128)S(1)}, f32[2,4,512]{2,1,0:T(4,128)S(1)}, u32[]{:S(2)}, u32[]{:S(2)}) collective-permute-start(f32[2,4,512]{2,1,0:T(4,128)S(1)} %get-tuple-element.34), channel_id=1, source_target_pairs={{0,1},{1,0},{2,3},{3,2},{4,5},{5,4},{6,7},{7,6},{8,9},{9,8},{10,11... | collective-permute-start | bytes 49160 | tf_op jit(solution)/shard_map/ppermute | solution.py:446
  4.6 0.0 copy-start
  4.6 0.0 copy-start.1
  4.6 0.7 %copy-done = f32[2,2]{1,0:T(2,128)S(1)} copy-done((f32[2,2]{1,0:T(2,128)S(1)}, f32[2,2]{1,0:T(2,128)}, u32[]{:S(2)}) %copy-start) | copy-done | bytes 40
  5.3 0.0 copy-done.1
  5.3 1.0 %shard_map.56 = (f32[64,8,128]{2,1,0:T(8,128)S(1)}, f32[64,8,128]{2,1,0:T(8,128)S(1)}, f32[8,128]{1,0:T(8,128)S(1)}, f32[128,512]{1,0:T(8,128)S(1)}, f32[128,512...) custom-call(f32[2,2]{1,0:T(2,128)S(1)} %copy-done, f32[1,2]{1,0:T(1,128)S(1)} %bitcast.9, ...), custom_call_target="tpu_custom_call" | custom-call | flops 4000000 | bytes 1000000 | tf_op jit(solution)/shard_map/pallas_call | solution.py:291
  6.3 0.8 %shard_map.57 = (f32[8,128]{1,0:T(8,128)S(1)}, f32[8,512]{1,0:T(8,128)S(1)}, f32[8,512]{1,0:T(8,128)S(1)}, f32[128,512]{1,0:T(8,128)S(1)}, f32[128,512]{1,0:T(8,128)S(1)}) custom-call(f32[128,512]{1,0:T(8,128)S(1)} %get-tuple-element.39.r0, f32[64,8,128]{2,1,0:T(8,128)S(1)} %get-tuple-element.40.gpy, f32[64,8,128]{2,1,0:T(8,128)S(1)} %get-tuple-element.41.gsy, ...), custom_call_target="tpu_custom_call" | custom-call | flops 1000000 | bytes 250000 | tf_op jit(solution)/shard_map/pallas_call | solution.py:291
  7.1 0.0 collective-permute-done.1
  7.2 0.0 collective-permute-done.inner
  7.2 0.1 shard_map.58
  7.3 3.3 %collective-permute-start.3 = (f32[8,128]{1,0:T(8,128)S(1)}, f32[8,128]{1,0:T(8,128)S(1)}, u32[]{:S(2)}, u32[]{:S(2)}) collective-permute-start(f32[8,128]{1,0:T(8,128)S(1)} %get-tuple-element.46.m0), channel_id=1, source_target_pairs={{0,64},{32,96},{64,0},{96,32},{1,65},{33,97},{65,1},{97,33},{2,66}... | collective-permute-start | bytes 12296 | tf_op jit(solution)/shard_map/ppermute | solution.py:412
  10.6 0.0 collective-permute-start.4
  10.6 0.3 collective-permute-start.2
  10.9 0.7 %shard_map.59 = (f32[128,512]{1,0:T(8,128)S(1)}, f32[3,4,512]{2,1,0:T(4,128)S(1)}) custom-call(f32[128,512]{1,0:T(8,128)S(1)} %get-tuple-element.36.u, f32[128,512]{1,0:T(8,128)S(1)} %get-tuple-element.39.r0, f32[8,512]{1,0:T(8,128)S(1)} %get-tuple-element.47.change, f32[2,4,512]{2,1,0:T(4,128)S(1)} %get-tuple-element.32.low, ...), custom_call_target="tpu_custom_call" | custom-call | flops 1000000 | bytes 250000 | tf_op jit(solution)/shard_map/pallas_call | solution.py:291
  11.6 0.0 collective-permute-done.3
  11.6 2.7 %collective-permute-done.4 = f32[8,128]{1,0:T(8,128)S(1)} collective-permute-done((f32[8,128]{1,0:T(8,128)S(1)}, f32[8,128]{1,0:T(8,128)S(1)}, u32[]{:S(2)}, u32[]{:S(2)}) %collective-permute-start.4) | collective-permute-done | bytes 4128 | tf_op jit(solution)/shard_map/ppermute | solution.py:412
  14.3 0.0 collective-permute-done.2.m1
  14.3 0.3 shard_map.60
  14.6 1.6 %collective-permute-start.5 = (f32[5,4,512]{2,1,0:T(4,128)S(1)}, f32[5,4,512]{2,1,0:T(4,128)S(1)}, u32[]{:S(2)}, u32[]{:S(2)}) collective-permute-start(f32[5,4,512]{2,1,0:T(4,128)S(1)} %get-tuple-element.55.own), channel_id=1, source_target_pairs={{0,1},{1,0},{2,3},{3,2},{4,5},{5,4},{6,7},{7,6},{8,9},{9,8},{10,11... | collective-permute-start | bytes 122888 | tf_op jit(solution)/shard_map/ppermute | solution.py:476
  16.2 0.2 shard_map.61
  16.4 0.6 %collective-permute-done.5.peer = f32[5,4,512]{2,1,0:T(4,128)S(1)} collective-permute-done((f32[5,4,512]{2,1,0:T(4,128)S(1)}, f32[5,4,512]{2,1,0:T(4,128)S(1)}, u32[]{:S(2)}, u32[]{:S(2)}) %collective-permute-start.5) | collective-permute-done | bytes 40992 | tf_op jit(solution)/shard_map/ppermute | solution.py:476
  17.1 2.7 %collective-permute-start.7 = (f32[5,4,512]{2,1,0:T(4,128)S(1)}, f32[5,4,512]{2,1,0:T(4,128)S(1)}, u32[]{:S(2)}, u32[]{:S(2)}) collective-permute-start(f32[5,4,512]{2,1,0:T(4,128)S(1)} %shard_map.62.m0.c0), channel_id=1, source_target_pairs={{0,6},{1,5},{2,4},{3,7},{4,2},{5,1},{6,0},{7,3},{8,14},{9,13},{10,... | collective-permute-start | bytes 122888 | tf_op jit(solution)/shard_map/ppermute | solution.py:396
  19.8 0.3 collective-permute-start.6
  20.0 1.5 %collective-permute-done.7.m2.c2 = f32[5,4,512]{2,1,0:T(4,128)S(1)} collective-permute-done((f32[5,4,512]{2,1,0:T(4,128)S(1)}, f32[5,4,512]{2,1,0:T(4,128)S(1)}, u32[]{:S(2)}, u32[]{:S(2)}) %collective-permute-start.7) | collective-permute-done | bytes 40992 | tf_op jit(solution)/shard_map/ppermute | solution.py:396
  21.5 1.2 %collective-permute-start.8 = (f32[5,4,512]{2,1,0:T(4,128)S(1)}, f32[5,4,512]{2,1,0:T(4,128)S(1)}, u32[]{:S(2)}, u32[]{:S(2)}) collective-permute-start(f32[5,4,512]{2,1,0:T(4,128)S(1)} %collective-permute-done.7.m2.c2), channel_id=1, source_target_pairs={{0,1},{1,0},{2,3},{3,2},{4,5},{5,4},{6,7},{7,6},{8,9},{9,8},{10,11... | collective-permute-start | bytes 122888 | tf_op jit(solution)/shard_map/ppermute | solution.py:398
  22.7 0.0 collective-permute-done.6.m1.c1
  22.7 0.9 %collective-permute-done.8.m3.c3 = f32[5,4,512]{2,1,0:T(4,128)S(1)} collective-permute-done((f32[5,4,512]{2,1,0:T(4,128)S(1)}, f32[5,4,512]{2,1,0:T(4,128)S(1)}, u32[]{:S(2)}, u32[]{:S(2)}) %collective-permute-start.8) | collective-permute-done | bytes 40992 | tf_op jit(solution)/shard_map/ppermute | solution.py:398
  23.6 3.9 %collective-permute-start.10 = (f32[5,4,512]{2,1,0:T(4,128)S(1)}, f32[5,4,512]{2,1,0:T(4,128)S(1)}, u32[]{:S(2)}, u32[]{:S(2)}) collective-permute-start(f32[5,4,512]{2,1,0:T(4,128)S(1)} %shard_map.63.p0), channel_id=1, source_target_pairs={{0,24},{1,17},{2,26},{3,19},{4,28},{5,21},{6,30},{7,23},{8,16},{9,... | collective-permute-start | bytes 122888 | tf_op jit(solution)/shard_map/ppermute | solution.py:396
  27.5 0.3 collective-permute-start.9
  27.8 1.1 %collective-permute-done.10.p2 = f32[5,4,512]{2,1,0:T(4,128)S(1)} collective-permute-done((f32[5,4,512]{2,1,0:T(4,128)S(1)}, f32[5,4,512]{2,1,0:T(4,128)S(1)}, u32[]{:S(2)}, u32[]{:S(2)}) %collective-permute-start.10) | collective-permute-done | bytes 40992 | tf_op jit(solution)/shard_map/ppermute | solution.py:396
  28.9 1.1 %collective-permute-start.11 = (f32[5,4,512]{2,1,0:T(4,128)S(1)}, f32[5,4,512]{2,1,0:T(4,128)S(1)}, u32[]{:S(2)}, u32[]{:S(2)}) collective-permute-start(f32[5,4,512]{2,1,0:T(4,128)S(1)} %collective-permute-done.10.p2), channel_id=1, source_target_pairs={{0,1},{1,0},{2,3},{3,2},{4,5},{5,4},{6,7},{7,6},{8,9},{9,8},{10,11... | collective-permute-start | bytes 122888 | tf_op jit(solution)/shard_map/ppermute | solution.py:398
  30.0 0.3 %collective-permute-done.9.p1 = f32[5,4,512]{2,1,0:T(4,128)S(1)} collective-permute-done((f32[5,4,512]{2,1,0:T(4,128)S(1)}, f32[5,4,512]{2,1,0:T(4,128)S(1)}, u32[]{:S(2)}, u32[]{:S(2)}) %collective-permute-start.9) | collective-permute-done | bytes 40992 | tf_op jit(solution)/shard_map/ppermute | solution.py:397
  30.4 0.5 %collective-permute-done.11.p3 = f32[5,4,512]{2,1,0:T(4,128)S(1)} collective-permute-done((f32[5,4,512]{2,1,0:T(4,128)S(1)}, f32[5,4,512]{2,1,0:T(4,128)S(1)}, u32[]{:S(2)}, u32[]{:S(2)}) %collective-permute-start.11) | collective-permute-done | bytes 40992 | tf_op jit(solution)/shard_map/ppermute | solution.py:398
  30.9 0.8 %shard_map.64 = f32[128,512]{1,0:T(8,128)} custom-call(f32[5,4,512]{2,1,0:T(4,128)S(1)} %get-tuple-element.55.own, f32[5,4,512]{2,1,0:T(4,128)S(1)} %collective-permute-done.5.peer, f32[5,4,512]{2,1,0:T(4,128)S(1)} %shard_map.62.m0.c0, f32[5,4,512]{2,1,0:T(4,128)S(1)} %collective-permute-done.6.m1.c1, f32[5,4,512]{2,1,0:T(4,128)S(1)} %collective-permute-done.7.m2.c2, ...), custom_call_target="tpu_custom_call" | custom-call | flops 1000000 | bytes 250000 | tf_op jit(solution)/shard_map/pallas_call | solution.py:291
  (6 shorter events, 0.1 us)
Async XLA Ops:
  1.1 6.0 %collective-permute-start.1 = (f32[2,4,512]{2,1,0:T(4,128)S(1)}, f32[2,4,512]{2,1,0:T(4,128)S(1)}, u32[]{:S(2)}, u32[]{:S(2)}) collective-permute-start(f32[2,4,512]{2,1,0:T(4,128)S(1)} %get-tuple-element.35), channel_id=1, source_target_pairs={{0,32},{1,2},{2,1},{3,4},{4,3},{5,6},{6,5},{7,8},{8,7},{9,10},{10,... | collective-permute-start | bytes 49160 | tf_op jit(solution)/shard_map/ppermute | solution.py:447
  3.9 3.3 %collective-permute-start = (f32[2,4,512]{2,1,0:T(4,128)S(1)}, f32[2,4,512]{2,1,0:T(4,128)S(1)}, u32[]{:S(2)}, u32[]{:S(2)}) collective-permute-start(f32[2,4,512]{2,1,0:T(4,128)S(1)} %get-tuple-element.34), channel_id=1, source_target_pairs={{0,1},{1,0},{2,3},{3,2},{4,5},{5,4},{6,7},{7,6},{8,9},{9,8},{10,11... | collective-permute-start | bytes 49160 | tf_op jit(solution)/shard_map/ppermute | solution.py:446
  4.6 0.7 %copy-start = (f32[2,2]{1,0:T(2,128)S(1)}, f32[2,2]{1,0:T(2,128)}, u32[]{:S(2)}) copy-start(f32[2,2]{1,0:T(2,128)} %cx.1) | copy-start | bytes 52
  4.6 0.7 %copy-start.1 = (f32[2]{0:T(128)S(1)}, f32[2]{0:T(128)}, u32[]{:S(2)}) copy-start(f32[2]{0:T(128)} %param.9) | copy-start | bytes 28
  7.3 4.3 %collective-permute-start.3 = (f32[8,128]{1,0:T(8,128)S(1)}, f32[8,128]{1,0:T(8,128)S(1)}, u32[]{:S(2)}, u32[]{:S(2)}) collective-permute-start(f32[8,128]{1,0:T(8,128)S(1)} %get-tuple-element.46.m0), channel_id=1, source_target_pairs={{0,64},{32,96},{64,0},{96,32},{1,65},{33,97},{65,1},{97,33},{2,66}... | collective-permute-start | bytes 12296 | tf_op jit(solution)/shard_map/ppermute | solution.py:412
  10.6 3.7 %collective-permute-start.4 = (f32[8,128]{1,0:T(8,128)S(1)}, f32[8,128]{1,0:T(8,128)S(1)}, u32[]{:S(2)}, u32[]{:S(2)}) collective-permute-start(f32[8,128]{1,0:T(8,128)S(1)} %get-tuple-element.46.m0), channel_id=1, source_target_pairs={{0,96},{32,64},{64,32},{96,0},{1,97},{33,65},{65,33},{97,1},{2,98}... | collective-permute-start | bytes 12296 | tf_op jit(solution)/shard_map/ppermute | solution.py:412
  10.6 3.7 %collective-permute-start.2 = (f32[8,128]{1,0:T(8,128)S(1)}, f32[8,128]{1,0:T(8,128)S(1)}, u32[]{:S(2)}, u32[]{:S(2)}) collective-permute-start(f32[8,128]{1,0:T(8,128)S(1)} %get-tuple-element.46.m0), channel_id=1, source_target_pairs={{0,32},{32,0},{64,96},{96,64},{1,33},{33,1},{65,97},{97,65},{2,34}... | collective-permute-start | bytes 12296 | tf_op jit(solution)/shard_map/ppermute | solution.py:412
  14.6 2.4 %collective-permute-start.5 = (f32[5,4,512]{2,1,0:T(4,128)S(1)}, f32[5,4,512]{2,1,0:T(4,128)S(1)}, u32[]{:S(2)}, u32[]{:S(2)}) collective-permute-start(f32[5,4,512]{2,1,0:T(4,128)S(1)} %get-tuple-element.55.own), channel_id=1, source_target_pairs={{0,1},{1,0},{2,3},{3,2},{4,5},{5,4},{6,7},{7,6},{8,9},{9,8},{10,11... | collective-permute-start | bytes 122888 | tf_op jit(solution)/shard_map/ppermute | solution.py:476
  17.1 4.4 %collective-permute-start.7 = (f32[5,4,512]{2,1,0:T(4,128)S(1)}, f32[5,4,512]{2,1,0:T(4,128)S(1)}, u32[]{:S(2)}, u32[]{:S(2)}) collective-permute-start(f32[5,4,512]{2,1,0:T(4,128)S(1)} %shard_map.62.m0.c0), channel_id=1, source_target_pairs={{0,6},{1,5},{2,4},{3,7},{4,2},{5,1},{6,0},{7,3},{8,14},{9,13},{10,... | collective-permute-start | bytes 122888 | tf_op jit(solution)/shard_map/ppermute | solution.py:396
  19.8 2.9 %collective-permute-start.6 = (f32[5,4,512]{2,1,0:T(4,128)S(1)}, f32[5,4,512]{2,1,0:T(4,128)S(1)}, u32[]{:S(2)}, u32[]{:S(2)}) collective-permute-start(f32[5,4,512]{2,1,0:T(4,128)S(1)} %shard_map.62.m0.c0), channel_id=1, source_target_pairs={{0,2},{1,3},{2,0},{3,1},{4,6},{5,7},{6,4},{7,5},{8,10},{9,11},{10,... | collective-permute-start | bytes 122888 | tf_op jit(solution)/shard_map/ppermute | solution.py:397
  21.5 2.1 %collective-permute-start.8 = (f32[5,4,512]{2,1,0:T(4,128)S(1)}, f32[5,4,512]{2,1,0:T(4,128)S(1)}, u32[]{:S(2)}, u32[]{:S(2)}) collective-permute-start(f32[5,4,512]{2,1,0:T(4,128)S(1)} %collective-permute-done.7.m2.c2), channel_id=1, source_target_pairs={{0,1},{1,0},{2,3},{3,2},{4,5},{5,4},{6,7},{7,6},{8,9},{9,8},{10,11... | collective-permute-start | bytes 122888 | tf_op jit(solution)/shard_map/ppermute | solution.py:398
  23.6 5.3 %collective-permute-start.10 = (f32[5,4,512]{2,1,0:T(4,128)S(1)}, f32[5,4,512]{2,1,0:T(4,128)S(1)}, u32[]{:S(2)}, u32[]{:S(2)}) collective-permute-start(f32[5,4,512]{2,1,0:T(4,128)S(1)} %shard_map.63.p0), channel_id=1, source_target_pairs={{0,24},{1,17},{2,26},{3,19},{4,28},{5,21},{6,30},{7,23},{8,16},{9,... | collective-permute-start | bytes 122888 | tf_op jit(solution)/shard_map/ppermute | solution.py:396
  27.5 2.9 %collective-permute-start.9 = (f32[5,4,512]{2,1,0:T(4,128)S(1)}, f32[5,4,512]{2,1,0:T(4,128)S(1)}, u32[]{:S(2)}, u32[]{:S(2)}) collective-permute-start(f32[5,4,512]{2,1,0:T(4,128)S(1)} %shard_map.63.p0), channel_id=1, source_target_pairs={{0,8},{1,9},{2,10},{3,11},{4,12},{5,13},{6,14},{7,15},{8,0},{9,1},... | collective-permute-start | bytes 122888 | tf_op jit(solution)/shard_map/ppermute | solution.py:397
  28.9 2.0 %collective-permute-start.11 = (f32[5,4,512]{2,1,0:T(4,128)S(1)}, f32[5,4,512]{2,1,0:T(4,128)S(1)}, u32[]{:S(2)}, u32[]{:S(2)}) collective-permute-start(f32[5,4,512]{2,1,0:T(4,128)S(1)} %collective-permute-done.10.p2), channel_id=1, source_target_pairs={{0,1},{1,0},{2,3},{3,2},{4,5},{5,4},{6,7},{7,6},{8,9},{9,8},{10,11... | collective-permute-start | bytes 122888 | tf_op jit(solution)/shard_map/ppermute | solution.py:398
